TPU v7x, 32 devices: a whole 2x2x4 slice. The times are simulated.
32 devices in a mesh: dp: 8 (over y, x, core), cont: 4 (over z).
Axes of the slice: x: 2, y: 2, z: 4, core: 2. Of those that a mesh axis runs over, the one named last changes fastest.
Arguments:
- prompt_x: bfloat16 [16, 1024, 512], P('dp', 'cont'), may hold values from -6 to 6
- cont_x: bfloat16 [16, 4, 128, 512], P('dp', 'cont'), may hold values from -6 to 6
- prompt_dy: bfloat16 [16, 1024, 512], P('dp', 'cont'), may hold values from -6 to 6
- cont_dy: bfloat16 [16, 4, 128, 512], P('dp', 'cont'), may hold values from -6 to 6
- teacher: bfloat16 [16, 4, 128, 512], P('dp', 'cont'), may hold values from -6 to 6
- cont_lengths: int32 [16, 4], P('dp', 'cont'), may hold values from 1 to 128, as said below
- loss_scale: float32 [], replicated, may hold values from 131072 to 524288
- norm1_gain: bfloat16 [512], P(('dp', 'cont')), may hold values from 0.5 to 1.5
- norm1_bias: bfloat16 [512], P(('dp', 'cont')), may hold values from -1.5 to 1.5
- w_query: bfloat16 [512, 512], P(('dp', 'cont')), may hold values from -0.375 to 0.375
- w_key: bfloat16 [512, 512], P(('dp', 'cont')), may hold values from -0.25 to 0.25
- w_value: bfloat16 [512, 512], P(('dp', 'cont')), may hold values from -0.25 to 0.25
- w_out: bfloat16 [512, 512], P(('dp', 'cont')), may hold values from -4 to 4
- norm2_gain: bfloat16 [512], P(('dp', 'cont')), may hold values from 0.5 to 1.5
- norm2_bias: bfloat16 [512], P(('dp', 'cont')), may hold values from -1.5 to 1.5
- w_up: bfloat16 [512, 2048], P(('dp', 'cont')), may hold values from -0.25 to 0.25
- up_bias: bfloat16 [2048], P(('dp', 'cont')), may hold values from -1.5 to 1.5
- w_down: bfloat16 [2048, 512], P(('dp', 'cont')), may hold values from -0.1875 to 0.1875
- down_bias: bfloat16 [512], P(('dp', 'cont')), may hold values from -1.5 to 1.5
Outputs:
- prompt_y: bfloat16 [16, 1024, 512], P('dp', 'cont')
- cont_y: bfloat16 [16, 4, 128, 512], P('dp', 'cont')
- loss: float32 [], replicated
- prompt_dx: float32 [16, 1024, 512], P('dp', 'cont')
- cont_dx: float32 [16, 4, 128, 512], P('dp', 'cont')
- grad_norm1_gain: float32 [512], P(('dp', 'cont'))
- grad_norm1_bias: float32 [512], P(('dp', 'cont'))
- grad_w_query: float32 [512, 512], P(('dp', 'cont'))
- grad_w_key: float32 [512, 512], P(('dp', 'cont'))
- grad_w_value: float32 [512, 512], P(('dp', 'cont'))
- grad_w_out: float32 [512, 512], P(('dp', 'cont'))
- grad_norm2_gain: float32 [512], P(('dp', 'cont'))
- grad_norm2_bias: float32 [512], P(('dp', 'cont'))
- grad_w_up: float32 [512, 2048], P(('dp', 'cont'))
- grad_up_bias: float32 [2048], P(('dp', 'cont'))
- grad_w_down: float32 [2048, 512], P(('dp', 'cont'))
- grad_down_bias: float32 [512], P(('dp', 'cont'))
Inputs may be any that keep to these rules, and one draw needn't show every extreme that they name: `cont_lengths`: some continuation has length 128.
All inputs are finite; a program needn't handle non-finite values.
Results may differ from a plain program's by a relative error of at most 0.0095.
Values may be sent and summed in bfloat16 or wider, within the bound.
A program may use at most 192 MiB of HBM per device.

v0:
```python
from functools import partial

import jax
import jax.numpy as jnp
from jax import lax
from jax.sharding import PartitionSpec as P

D = 512
HEADS = 8
HEAD_DIM = 64
BLOCK = 16
CONT_LEN = 128
MICRO = 2


epsilon = 1e-05
largest_score = lax.Precision.HIGHEST


def layer_norm(row_data, gain_vec, offset_vec):
    center = row_data - jnp.mean(row_data, -1, keepdims=True)
    variance = jnp.mean(center * center, -1, keepdims=True)
    return center * lax.rsqrt(variance + epsilon) * gain_vec + offset_vec


def divide_into_heads(row_data):
    return row_data.reshape(row_data.shape[:-1] + (HEADS, HEAD_DIM))


def pair_sum(row_data):
    old_shape = row_data.shape
    return row_data.reshape((old_shape[0], old_shape[1] // 2, 2) + old_shape[2:]).sum(2)


def coarse_sum(row_data):
    factor = CONT_LEN // BLOCK
    old_shape = row_data.shape
    return row_data.reshape(old_shape[:-2] + (old_shape[-2] // factor, factor, old_shape[-1])).sum(
        -2
    )


def diagonal_terms(query_tier_rows, key_level, value_level, count_level, logit_scale_factor):
    batch_blocks, positions = (query_tier_rows.shape[0], query_tier_rows.shape[1])
    blocks = positions // BLOCK
    query_block = query_tier_rows.reshape(batch_blocks, blocks, BLOCK, HEADS, HEAD_DIM)
    key_block = key_level.reshape(batch_blocks, blocks, BLOCK, HEADS, HEAD_DIM)
    value_block = value_level.reshape(batch_blocks, blocks, BLOCK, HEADS, HEAD_DIM)
    count_block = count_level.reshape(batch_blocks, blocks, BLOCK)
    causal = (jnp.arange(BLOCK)[:, None] >= jnp.arange(BLOCK)[None, :]).astype(jnp.float32)
    expo_scores = (
        jnp.exp(
            jnp.einsum("abqhd,abkhd->hqkab", query_block, key_block, precision=largest_score)
            * logit_scale_factor
        )
        * causal[None, :, :, None, None]
    )
    numerator = jnp.einsum("hqkab,abkhd->abqhd", expo_scores, value_block, precision=largest_score)
    denominator = jnp.einsum("hqkab,abk->abqh", expo_scores, count_block, precision=largest_score)
    return (
        numerator.reshape(batch_blocks, positions, HEADS, HEAD_DIM),
        denominator.reshape(batch_blocks, positions, HEADS),
    )


def sibling_terms(query_tier_rows, key_level, value_level, count_level, logit_scale_factor):
    batch_blocks, positions = (query_tier_rows.shape[0], query_tier_rows.shape[1])
    pair_count = positions // (2 * BLOCK)
    query_odd = query_tier_rows.reshape(batch_blocks, pair_count, 2, BLOCK, HEADS, HEAD_DIM)[
        :, :, 1
    ]
    key_even = key_level.reshape(batch_blocks, pair_count, 2, BLOCK, HEADS, HEAD_DIM)[:, :, 0]
    value_even = value_level.reshape(batch_blocks, pair_count, 2, BLOCK, HEADS, HEAD_DIM)[:, :, 0]
    count_even = count_level.reshape(batch_blocks, pair_count, 2, BLOCK)[:, :, 0]
    expo_scores = jnp.exp(
        jnp.einsum("abqhd,abkhd->hqkab", query_odd, key_even, precision=largest_score)
        * logit_scale_factor
    )
    numerator = jnp.einsum("hqkab,abkhd->abqhd", expo_scores, value_even, precision=largest_score)
    denominator = jnp.einsum("hqkab,abk->abqh", expo_scores, count_even, precision=largest_score)
    numerator = jnp.stack([jnp.zeros_like(numerator), numerator], 2).reshape(
        batch_blocks, positions, HEADS, HEAD_DIM
    )
    denominator = jnp.stack([jnp.zeros_like(denominator), denominator], 2).reshape(
        batch_blocks, positions, HEADS
    )
    return (numerator, denominator)


def hier_attention(
    query_rows,
    key_rows,
    value_rows,
    valid_rows,
    distant_key_rows,
    distant_value_rows,
    distant_allow_mask,
):
    logit_scale_factor = HEAD_DIM ** (-0.5)
    batch_blocks, top_len = (query_rows.shape[0], query_rows.shape[1])
    query_tier_rows = divide_into_heads(query_rows)
    key_level = divide_into_heads(key_rows * valid_rows[..., None])
    value_level = divide_into_heads(value_rows * valid_rows[..., None])
    count_level = valid_rows
    numerator, denominator = diagonal_terms(
        query_tier_rows, key_level, value_level, count_level, logit_scale_factor
    )
    factor = 1
    while top_len // factor >= 2 * BLOCK:
        level_numerator, level_denominator = sibling_terms(
            query_tier_rows, key_level, value_level, count_level, logit_scale_factor
        )
        numerator = numerator + jnp.repeat(level_numerator, factor, axis=1)
        denominator = denominator + jnp.repeat(level_denominator, factor, axis=1)
        query_tier_rows = 0.5 * pair_sum(query_tier_rows)
        key_level = 0.5 * pair_sum(key_level)
        value_level = pair_sum(value_level)
        count_level = pair_sum(count_level)
        factor = factor * 2
    distant_score_rows = (
        jnp.exp(
            jnp.einsum(
                "cfgi,ugi->cgfu",
                query_tier_rows,
                divide_into_heads(distant_key_rows),
                precision=largest_score,
            )
            * logit_scale_factor
        )
        * distant_allow_mask[:, None, None, :]
    )
    upper_tier_numerator = jnp.einsum(
        "ewcl,lwr->ecwr",
        distant_score_rows,
        divide_into_heads(distant_value_rows),
        precision=largest_score,
    )
    top_denominator = float(factor) * jnp.transpose(jnp.sum(distant_score_rows, axis=3), (0, 2, 1))
    numerator = numerator + jnp.repeat(upper_tier_numerator, factor, axis=1)
    denominator = denominator + jnp.repeat(top_denominator, factor, axis=1)
    return (numerator / denominator[..., None]).reshape(batch_blocks, top_len, HEADS * HEAD_DIM)


def outer_grad(left_rows, right_rows):
    return lax.dot_general(
        left_rows, right_rows, (((0,), (0,)), ((), ())), preferred_element_type=jnp.float32
    )


def back_dot(grad_rows, weight_mat):
    return lax.dot_general(
        grad_rows, weight_mat, (((1,), (1,)), ((), ())), preferred_element_type=jnp.float32
    )


def local(
    prompt_x,
    cont_x,
    prompt_dy,
    cont_dy,
    teacher,
    cont_lengths,
    loss_scale,
    norm1_gain,
    norm1_bias,
    w_query,
    w_key,
    w_value,
    w_out,
    norm2_gain,
    norm2_bias,
    w_up,
    up_bias,
    w_down,
    down_bias,
):
    shards = (
        norm1_gain,
        norm1_bias,
        w_query,
        w_key,
        w_value,
        w_out,
        norm2_gain,
        norm2_bias,
        w_up,
        up_bias,
        w_down,
        down_bias,
    )
    coarse = CONT_LEN // BLOCK
    groups_here = prompt_x.shape[0]
    local_prompt = prompt_x.shape[1]
    conts_here = cont_x.shape[1]
    per_batch = groups_here // MICRO
    prompt_blocks = local_prompt // CONT_LEN
    rows_group = local_prompt + conts_here * CONT_LEN
    far_len = local_prompt * lax.axis_size("cont") // coarse
    block_ids = lax.axis_index("cont") * prompt_blocks + jnp.arange(prompt_blocks, dtype=jnp.int32)
    prompt_allow = (
        jnp.arange(far_len, dtype=jnp.int32)[None, :] // BLOCK < block_ids[:, None]
    ).astype(jnp.float32)
    allow_all = jnp.concatenate([prompt_allow, jnp.ones((conts_here, far_len), jnp.float32)], 0)
    valid = (
        jnp.arange(CONT_LEN, dtype=jnp.int32)[None, None, :] < cont_lengths[:, :, None]
    ).astype(jnp.float32)
    token_total = lax.psum(jnp.sum(valid), ("dp", "cont"))
    scale_all = token_total * D
    loss_weight = loss_scale / scale_all

    def attend(valid_all, query_all, key_all, value_all, far_key_all, far_value_all):

        def one_group(query_rows, key_rows, value_rows, far_key_rows, far_value_rows, valid_rows):
            shaped = (-1, CONT_LEN, D)
            attended_rows = hier_attention(
                query_rows.reshape(shaped),
                key_rows.reshape(shaped),
                value_rows.reshape(shaped),
                valid_rows,
                far_key_rows,
                far_value_rows,
                allow_all,
            )
            return attended_rows.reshape(-1, D)

        return jax.vmap(one_group)(
            query_all, key_all, value_all, far_key_all, far_value_all, valid_all
        )

    prompt_outs, cont_outs, prompt_grads, cont_grads = ([], [], [], [])
    square_sum = jnp.zeros((), jnp.float32)
    accumulated = None
    for batch_index in range(MICRO):
        first_group = batch_index * per_batch
        end_group = first_group + per_batch
        forward_set = (
            lax.all_gather(shards[0], ("dp", "cont"), axis=0, tiled=True),
            lax.all_gather(shards[1], ("dp", "cont"), axis=0, tiled=True),
            lax.all_gather(shards[2], ("dp", "cont"), axis=0, tiled=True),
            lax.all_gather(shards[3], ("dp", "cont"), axis=0, tiled=True),
            lax.all_gather(shards[4], ("dp", "cont"), axis=0, tiled=True),
            lax.all_gather(shards[5], ("dp", "cont"), axis=0, tiled=True),
            lax.all_gather(shards[6], ("dp", "cont"), axis=0, tiled=True),
            lax.all_gather(shards[7], ("dp", "cont"), axis=0, tiled=True),
            lax.all_gather(shards[8], ("dp", "cont"), axis=0, tiled=True),
            lax.all_gather(shards[9], ("dp", "cont"), axis=0, tiled=True),
            lax.all_gather(shards[10], ("dp", "cont"), axis=0, tiled=True),
            lax.all_gather(shards[11], ("dp", "cont"), axis=0, tiled=True),
        )
        (
            gain_one,
            bias_one,
            query_mat,
            key_mat,
            value_mat,
            out_mat,
            gain_two,
            bias_two,
            up_mat,
            up_vec,
            down_mat,
            down_vec,
        ) = forward_set
        inputs = jnp.concatenate(
            [
                prompt_x[first_group:end_group],
                cont_x[first_group:end_group].reshape(per_batch, conts_here * CONT_LEN, D),
            ],
            1,
        ).astype(jnp.float32)
        flat_in = inputs.reshape(-1, D)
        normed_one, norm_one_pull = jax.vjp(
            layer_norm, flat_in, gain_one.astype(jnp.float32), bias_one.astype(jnp.float32)
        )
        normed_one_low = normed_one.astype(jnp.bfloat16)
        qkv_mat = jnp.concatenate([query_mat, key_mat, value_mat], 1)
        projected = jnp.dot(normed_one_low, qkv_mat, preferred_element_type=jnp.float32).astype(
            jnp.bfloat16
        )
        projected = projected.reshape(per_batch, rows_group, 3 * D)
        query_all = projected[..., :D]
        key_all = projected[..., D : 2 * D]
        value_all = projected[..., 2 * D :]
        far_key_own = (
            coarse_sum(key_all[:, :local_prompt].astype(jnp.float32)) * (1.0 / coarse)
        ).astype(jnp.bfloat16)
        far_value_own = coarse_sum(value_all[:, :local_prompt].astype(jnp.float32)).astype(
            jnp.bfloat16
        )
        distant_key_rows, distant_value_rows = (
            lax.all_gather(far_key_own, "cont", axis=1, tiled=True),
            lax.all_gather(far_value_own, "cont", axis=1, tiled=True),
        )
        valid_all = jnp.concatenate(
            [
                jnp.ones((per_batch, prompt_blocks, CONT_LEN), jnp.float32),
                valid[first_group:end_group],
            ],
            1,
        )
        attended, attend_pull = jax.vjp(
            partial(attend, valid_all),
            query_all.astype(jnp.float32),
            key_all.astype(jnp.float32),
            value_all.astype(jnp.float32),
            distant_key_rows.astype(jnp.float32),
            distant_value_rows.astype(jnp.float32),
        )
        attended_low = attended.reshape(-1, D).astype(jnp.bfloat16)
        mixed = flat_in + jnp.dot(attended_low, out_mat, preferred_element_type=jnp.float32)
        normed_two, norm_two_pull = jax.vjp(
            layer_norm, mixed, gain_two.astype(jnp.float32), bias_two.astype(jnp.float32)
        )
        normed_two_low = normed_two.astype(jnp.bfloat16)
        pre_act = jnp.dot(
            normed_two_low, up_mat, preferred_element_type=jnp.float32
        ) + up_vec.astype(jnp.float32)
        hidden_low = jax.nn.relu(pre_act).astype(jnp.bfloat16)
        result = (
            mixed
            + jnp.dot(hidden_low, down_mat, preferred_element_type=jnp.float32)
            + down_vec.astype(jnp.float32)
        )
        result = result.reshape(per_batch, rows_group, D)
        cont_result = result[:, local_prompt:].reshape(per_batch, conts_here, CONT_LEN, D)
        prompt_outs.append(result[:, :local_prompt].astype(jnp.bfloat16))
        cont_outs.append(cont_result.astype(jnp.bfloat16))
        valid_mask = valid[first_group:end_group][..., None]
        difference = cont_result - teacher[first_group:end_group].astype(jnp.float32)
        square_sum = square_sum + jnp.sum(valid_mask * difference * difference)
        backward_set = (
            lax.all_gather(shards[0], ("dp", "cont"), axis=0, tiled=True),
            lax.all_gather(shards[1], ("dp", "cont"), axis=0, tiled=True),
            lax.all_gather(shards[2], ("dp", "cont"), axis=0, tiled=True),
            lax.all_gather(shards[3], ("dp", "cont"), axis=0, tiled=True),
            lax.all_gather(shards[4], ("dp", "cont"), axis=0, tiled=True),
            lax.all_gather(shards[5], ("dp", "cont"), axis=0, tiled=True),
            lax.all_gather(shards[6], ("dp", "cont"), axis=0, tiled=True),
            lax.all_gather(shards[7], ("dp", "cont"), axis=0, tiled=True),
            lax.all_gather(shards[8], ("dp", "cont"), axis=0, tiled=True),
            lax.all_gather(shards[9], ("dp", "cont"), axis=0, tiled=True),
            lax.all_gather(shards[10], ("dp", "cont"), axis=0, tiled=True),
            lax.all_gather(shards[11], ("dp", "cont"), axis=0, tiled=True),
        )
        back_qkv = jnp.concatenate([backward_set[2], backward_set[3], backward_set[4]], 1)
        cont_extra = 2.0 * loss_weight * valid_mask * difference
        grad_rows = jnp.concatenate(
            [
                prompt_dy[first_group:end_group].astype(jnp.float32),
                (cont_dy[first_group:end_group].astype(jnp.float32) + cont_extra).reshape(
                    per_batch, conts_here * CONT_LEN, D
                ),
            ],
            1,
        )
        grad_rows = grad_rows.reshape(-1, D)
        grad_down_vec = jnp.sum(grad_rows, 0)
        grad_branch = grad_rows.astype(jnp.bfloat16)
        grad_down_mat = outer_grad(hidden_low, grad_branch)
        grad_hidden = back_dot(grad_branch, backward_set[10])
        grad_pre = jnp.where(pre_act > 0, grad_hidden, 0.0).astype(jnp.bfloat16)
        grad_up_vec = jnp.sum(grad_pre.astype(jnp.float32), 0)
        grad_up_mat = outer_grad(normed_two_low, grad_pre)
        grad_mixed, grad_gain_two, grad_bias_two = norm_two_pull(
            back_dot(grad_pre, backward_set[8])
        )
        grad_mixed = grad_mixed + grad_rows
        grad_mixed_low = grad_mixed.astype(jnp.bfloat16)
        grad_out_mat = outer_grad(attended_low, grad_mixed_low)
        grad_attended = back_dot(grad_mixed_low, backward_set[5]).reshape(per_batch, rows_group, D)
        grad_query, grad_key, grad_value, grad_far_key, grad_far_value = attend_pull(grad_attended)
        own_far_key, own_far_value = (
            lax.psum_scatter(
                grad_far_key.astype(jnp.bfloat16), "cont", scatter_dimension=1, tiled=True
            ).astype(jnp.float32),
            lax.psum_scatter(
                grad_far_value.astype(jnp.bfloat16), "cont", scatter_dimension=1, tiled=True
            ).astype(jnp.float32),
        )
        spread_key = jnp.repeat(own_far_key * (1.0 / coarse), coarse, axis=1)
        spread_value = jnp.repeat(own_far_value, coarse, axis=1)
        grad_key = jnp.concatenate(
            [grad_key[:, :local_prompt] + spread_key, grad_key[:, local_prompt:]], 1
        )
        grad_value = jnp.concatenate(
            [grad_value[:, :local_prompt] + spread_value, grad_value[:, local_prompt:]], 1
        )
        grad_qkv = (
            jnp.concatenate([grad_query, grad_key, grad_value], 2)
            .reshape(-1, 3 * D)
            .astype(jnp.bfloat16)
        )
        grad_qkv_mat = outer_grad(normed_one_low, grad_qkv)
        grad_input, grad_gain_one, grad_bias_one = norm_one_pull(back_dot(grad_qkv, back_qkv))
        grad_input = (grad_input + grad_mixed).reshape(per_batch, rows_group, D)
        prompt_grads.append(grad_input[:, :local_prompt])
        cont_grads.append(grad_input[:, local_prompt:].reshape(per_batch, conts_here, CONT_LEN, D))
        new_terms = (
            grad_gain_one,
            grad_bias_one,
            grad_qkv_mat[:, :D],
            grad_qkv_mat[:, D : 2 * D],
            grad_qkv_mat[:, 2 * D :],
            grad_out_mat,
            grad_gain_two,
            grad_bias_two,
            grad_up_mat,
            grad_up_vec,
            grad_down_mat,
            grad_down_vec,
        )
        if batch_index == 0:
            accumulated = new_terms
        else:
            accumulated = tuple(
                (held_term + new_term for held_term, new_term in zip(accumulated, new_terms))
            )
    reduced = lax.psum_scatter(accumulated, ("dp", "cont"), scatter_dimension=0, tiled=True)
    loss_value = lax.psum(square_sum, ("dp", "cont")) / scale_all
    return (
        jnp.concatenate(prompt_outs, 0),
        jnp.concatenate(cont_outs, 0),
        loss_value,
        jnp.concatenate(prompt_grads, 0),
        jnp.concatenate(cont_grads, 0),
    ) + tuple(reduced)


def solution(mesh):
    return jax.shard_map(
        local,
        mesh=mesh,
        in_specs=(
            P("dp", "cont", None),
            P("dp", "cont", None, None),
            P("dp", "cont", None),
            P("dp", "cont", None, None),
            P("dp", "cont", None, None),
            P("dp", "cont"),
            P(),
            P(("dp", "cont")),
            P(("dp", "cont")),
            P(("dp", "cont"), None),
            P(("dp", "cont"), None),
            P(("dp", "cont"), None),
            P(("dp", "cont"), None),
            P(("dp", "cont")),
            P(("dp", "cont")),
            P(("dp", "cont"), None),
            P(("dp", "cont")),
            P(("dp", "cont"), None),
            P(("dp", "cont")),
        ),
        out_specs=(
            P("dp", "cont", None),
            P("dp", "cont", None, None),
            P(),
            P("dp", "cont", None),
            P("dp", "cont", None, None),
            P(("dp", "cont")),
            P(("dp", "cont")),
            P(("dp", "cont"), None),
            P(("dp", "cont"), None),
            P(("dp", "cont"), None),
            P(("dp", "cont"), None),
            P(("dp", "cont")),
            P(("dp", "cont")),
            P(("dp", "cont"), None),
            P(("dp", "cont")),
            P(("dp", "cont"), None),
            P(("dp", "cont")),
        ),
        check_vma=False,
    )
```

profile of v0, /device:TPU:0, one launch (start us, length us, event | category | flops | bytes accessed | tf_op | source)
XLA Modules:
  0.0 1824.6 jit_solution(9853460461037718691)
XLA Ops:
  25.2 43.1 %all-reduce.50 = (bf16[512]{0:T(512)(128)(2,1)S(1)}, bf16[512]{0:T(512)(128)(2,1)S(1)}, bf16[2048]{0:T(1024)(128)(2,1)}, bf16[512]{0:T(512)(128)(2,1)}, bf16[512]{0:T(512)(128)(2,1)}, /*index=5*/bf16[512]{0:T(512)(128)(2,1)}) all-reduce(bf16[512]{0:T(512)(128)(2,1)S(1)} %dynamic-update-slice.1, ...), channel_id=1, replica_groups=mesh['dp'=8,'cont'=4] {'dp','cont'}, use_global_device_ids=true, to_apply=%add.34 | all-reduce | flops 4608 | bytes 18432
  69.4 71.2 %all_gather.34 = bf16[512,512]{1,0:T(8,128)(2,1)S(1)} all-gather(bf16[16,512]{1,0:T(8,128)(2,1)} %param.28), channel_id=1, replica_groups=mesh['dp'=8,'cont'=4] {'dp','cont'}, dimensions={0}, use_global_device_ids=true | all-gather | bytes 540672 | tf_op jit(solution)/shard_map/all_gather | solution.py:239
  140.6 67.8 %all_gather.35 = bf16[512,512]{1,0:T(8,128)(2,1)S(1)} all-gather(bf16[16,512]{1,0:T(8,128)(2,1)S(1)} %copy-done.312), channel_id=1, replica_groups=mesh['dp'=8,'cont'=4] {'dp','cont'}, dimensions={0}, use_global_device_ids=true | all-gather | bytes 540672 | tf_op jit(solution)/shard_map/all_gather | solution.py:240
  208.4 69.7 %all_gather.36 = bf16[512,512]{1,0:T(8,128)(2,1)S(1)} all-gather(bf16[16,512]{1,0:T(8,128)(2,1)S(1)} %copy-done.313), channel_id=1, replica_groups=mesh['dp'=8,'cont'=4] {'dp','cont'}, dimensions={0}, use_global_device_ids=true | all-gather | bytes 540672 | tf_op jit(solution)/shard_map/all_gather | solution.py:241
  304.8 2.7 fusion.276
  311.7 13.4 all-gather.3
  326.7 13.9 all-gather.1
  341.3 2.6 reshape.3149
  343.8 2.5 reduce_sum.729
  354.5 2.6 reshape.3153
  357.1 2.5 reduce_sum.745
  390.8 2.5 reshape.3009
  393.4 2.5 reshape.3022
  395.9 2.7 reshape.3014
  398.7 2.9 multiply_exponential_fusion.1
  401.6 2.4 multiply_exponential_fusion
  418.5 37.8 %psum.15 = f32[]{:T(128)} all-reduce(f32[]{:T(128)} %fusion.251), channel_id=1, replica_groups=mesh['dp'=8,'cont'=4] {'dp','cont'}, use_global_device_ids=true, to_apply=%region_36.37 | all-reduce | flops 1 | bytes 8 | tf_op jit(solution)/shard_map/psum | solution.py:207
  466.9 75.8 %all_gather.39 = bf16[512,512]{1,0:T(8,128)(2,1)} all-gather(bf16[16,512]{1,0:T(8,128)(2,1)} %param.31), channel_id=1, replica_groups=mesh['dp'=8,'cont'=4] {'dp','cont'}, dimensions={0}, use_global_device_ids=true | all-gather | bytes 540672 | tf_op jit(solution)/shard_map/all_gather | solution.py:242
  542.8 13.5 all-gather.2
  557.1 13.6 all-gather
  575.5 3.5 multiply_reduce_fusion.3
  616.8 3.5 multiply_reduce_fusion.1
  658.0 2.3 copy.747
  661.4 2.3 copy.781
  663.7 4.4 fusion.20
  671.4 3.0 divide_convert_fusion.1
  676.3 3.6 fusion.23
  683.2 2.9 divide_convert_fusion
  699.8 4.7 convolution_add_fusion.2
  704.5 2.8 convolution_add_fusion.3
  707.3 3.8 fusion.45
  734.1 2.8 copy.859
  736.8 3.0 multiply_reduce_fusion.6
  741.9 5.1 convolution_bitcast_fusion
  747.0 4.0 fusion.4
  751.0 4.8 convolution_bitcast_fusion.1
  762.8 2.7 convolution_bitcast_fusion.8
  796.6 2.8 copy.783
  799.4 3.0 multiply_reduce_fusion.8
  804.4 4.8 convolution_bitcast_fusion.2
  809.3 4.0 fusion.7
  813.3 4.9 convolution_bitcast_fusion.3
  825.1 2.5 convolution_bitcast_fusion.11
  864.2 2.5 copy.921
  867.9 2.3 copy.916
  871.5 2.6 copy.1054
  890.8 2.6 add_multiply_fusion.1
  903.0 2.5 copy.845
  906.8 2.3 copy.840
  910.4 2.6 copy.1046
  923.8 2.3 add_multiply_fusion.5
  934.2 44.3 %all-reduce.54.cloned.1.call-done = (bf16[1,128,512]{2,0,1:T(2,128)(2,1)}, bf16[1,128,512]{2,0,1:T(2,128)(2,1)}, bf16[1,128,512]{2,0,1:T(2,128)(2,1)}, bf16[1,128,512]{2,0,1:T(2,128)(2,1)}) async-done(((bf16[1,128,512]{2,0,1:T(2,128)(2,1)}, bf16[1,128,512]{2,0,1:T(2,128)(2,1)}, bf16[1,128,512]{2,0,1:T(2,128)(2,1)}, bf16[1,128,512]{2,0,1:T(2,128)(2,1)}), (bf16[1,128,512]{2,0,1:T(2,128)(2,1)}, ...) | async-done | bytes 524304
  989.8 3.3 fusion.144
  993.2 3.4 convolution_add_fusion
  997.8 2.9 fusion.270
  1000.8 3.4 convolution_add_fusion.1
  1012.1 2.6 fusion.263
  1018.4 40.4 %all-reduce.49 = (f32[]{:T(128)}, f32[512]{0:T(512)S(1)}, f32[512]{0:T(512)S(1)}, f32[512]{0:T(512)S(1)}, f32[512]{0:T(512)S(1)}, /*index=5*/f32[2048]{0:T(1024)S(1)}, f32[512]{0:T(512)S(1)}) all-reduce(f32[]{:T(128)S(6)} %add.675, f32[512]{0:T(512)S(1)} %add.734, f32[512]{0:T(512)S(1)} %add.735, ...), channel_id=1, replica_groups=mesh['dp'=8,'cont'=4] {'dp','cont'}, use_global_device_ids=true, to_apply=%region_34.35 | all-reduce | flops 4609 | bytes 36872 | tf_op jit(solution)/shard_map/psum | solution.py:419
  1066.9 49.3 %reduce-scatter.13.cloned.1.call-done = f32[16,512]{1,0:T(8,128)} async-done(((f32[512,512]{1,0:T(8,128)}), f32[16,512]{1,0:T(8,128)}) %reduce-scatter.13.cloned.1.call-update) | async-done | bytes 32784 | tf_op jit(solution)/shard_map/reduce_scatter | solution.py:418
  1116.2 134.6 %reduce-scatter.11.cloned.1.call-done = f32[16,512]{1,0:T(8,128)} async-done(((f32[512,512]{1,0:T(8,128)}), f32[16,512]{1,0:T(8,128)}) %reduce-scatter.11.cloned.1.call-update) | async-done | bytes 32784 | tf_op jit(solution)/shard_map/reduce_scatter | solution.py:418
  1250.8 134.8 %reduce-scatter.9.cloned.1.call-done = f32[16,512]{1,0:T(8,128)} async-done(((f32[512,512]{1,0:T(8,128)}), f32[16,512]{1,0:T(8,128)}) %reduce-scatter.9.cloned.1.call-update) | async-done | bytes 32784 | tf_op jit(solution)/shard_map/reduce_scatter | solution.py:418
  1385.6 134.8 %reduce-scatter.7.cloned.1.call-done = f32[16,512]{1,0:T(8,128)} async-done(((f32[512,512]{1,0:T(8,128)}), f32[16,512]{1,0:T(8,128)}) %reduce-scatter.7.cloned.1.call-update) | async-done | bytes 32784 | tf_op jit(solution)/shard_map/reduce_scatter | solution.py:418
  1520.4 147.2 %reduce-scatter.17.cloned.1.call-done = f32[64,512]{1,0:T(8,128)} async-done(((f32[2048,512]{1,0:T(8,128)}), f32[64,512]{1,0:T(8,128)}) %reduce-scatter.17.cloned.1.call-update) | async-done | bytes 131088 | tf_op jit(solution)/shard_map/reduce_scatter | solution.py:418
  1667.6 148.9 %reduce-scatter.15.cloned.1.call-done = f32[16,2048]{1,0:T(8,128)} async-done(((f32[512,2048]{1,0:T(8,128)}), f32[16,2048]{1,0:T(8,128)}) %reduce-scatter.15.cloned.1.call-update) | async-done | bytes 131088 | tf_op jit(solution)/shard_map/reduce_scatter | solution.py:418
  (1256 shorter events, 403.4 us)
Async XLA Ops:
  7.2 133.4 %copy-start.312 = (bf16[16,512]{1,0:T(8,128)(2,1)S(1)}, bf16[16,512]{1,0:T(8,128)(2,1)}, u32[]{:S(2)}) copy-start(bf16[16,512]{1,0:T(8,128)(2,1)} %param.29) | copy-start | bytes 49156
  7.2 201.2 %copy-start.313 = (bf16[16,512]{1,0:T(8,128)(2,1)S(1)}, bf16[16,512]{1,0:T(8,128)(2,1)}, u32[]{:S(2)}) copy-start(bf16[16,512]{1,0:T(8,128)(2,1)} %param.30) | copy-start | bytes 49156
  7.2 271.0 %copy-start.203 = (bf16[2,256,512]{2,1,0:T(8,128)(2,1)S(1)}, bf16[2,256,512]{2,1,0:T(8,128)(2,1)}, u32[]{:S(2)}) copy-start(bf16[2,256,512]{2,1,0:T(8,128)(2,1)} %param.19) | copy-start | bytes 1572868
  7.2 692.6 %all-gather.7.cloned.1.call-start = ((), (), s32[]{:S(2)}) async-start(), calls=%async_computation.6 | async-start | bytes 2162688 | tf_op jit(solution)/shard_map/all_gather | solution.py:245
  8.0 699.4 %all-gather.9.cloned.1.call-start = ((), (), s32[]{:S(2)}) async-start(), calls=%async_computation.7 | async-start | bytes 2162688 | tf_op jit(solution)/shard_map/all_gather | solution.py:247
  8.7 969.8 %all-reduce.54.cloned.1.call-start = ((), (), s32[]{:S(2)}) async-start(), calls=%async_computation.14 | async-start | bytes 2097152
  14.7 282.0 %copy-start.260 = (f32[1,3,4,2,16]{4,3,2,0,1:T(2,128)}, f32[1,3,4,2,16]{4,3,2,0,1:T(2,128)S(1)}, u32[]{:S(2)}) copy-start(f32[1,3,4,2,16]{4,3,2,0,1:T(2,128)S(1)} %reshape.2997) | copy-start | bytes 4612
  18.6 259.6 %copy-start.177 = (f32[3,64,2]{2,1,0:T(8,128)}, f32[3,64,2]{2,1,0:T(8,128)S(1)}, u32[]{:S(2)}) copy-start(f32[3,64,2]{2,1,0:T(8,128)S(1)} %mul.1204) | copy-start | bytes 4612
  68.4 214.1 %copy-start.335 = (f32[512]{0:T(512)}, f32[512]{0:T(512)S(1)}, u32[]{:S(2)}) copy-start(f32[512]{0:T(512)S(1)} %convert_element_type.343) | copy-start | bytes 6148
  68.4 214.1 %copy-start.289 = (f32[512]{0:T(512)}, f32[512]{0:T(512)S(1)}, u32[]{:S(2)}) copy-start(f32[512]{0:T(512)S(1)} %convert_element_type.342) | copy-start | bytes 6148
  69.4 209.9 %copy-start.77 = (bf16[128,512]{1,0:T(8,128)(2,1)}, bf16[128,512]{1,0:T(8,128)(2,1)S(1)}, u32[]{:S(2)}) copy-start(bf16[128,512]{1,0:T(8,128)(2,1)S(1)} %get-tuple-element.103) | copy-start | bytes 393220
  69.4 213.1 %copy-start.80 = (bf16[128,512]{1,0:T(8,128)(2,1)}, bf16[128,512]{1,0:T(8,128)(2,1)S(1)}, u32[]{:S(2)}) copy-start(bf16[128,512]{1,0:T(8,128)(2,1)S(1)} %get-tuple-element.104) | copy-start | bytes 393220
  289.2 109.4 %copy-start = (f32[3,8,16,8,64]{4,3,2,1,0:T(8,128)}, f32[3,8,16,8,64]{4,3,2,1,0:T(8,128)S(1)}, u32[]{:S(2)}) copy-start(f32[3,8,16,8,64]{4,3,2,1,0:T(8,128)S(1)} %reshape.2960) | copy-start | bytes 2359300
  292.5 302.2 %copy-start.240 = (f32[3,4,1,16]{3,1,0,2:T(4,128)}, f32[3,4,1,16]{3,1,0,2:T(4,128)S(1)}, u32[]{:S(2)}) copy-start(f32[3,4,1,16]{3,1,0,2:T(4,128)S(1)} %copy.1281) | copy-start | bytes 2308
  310.8 58.3 %copy-start.263 = (f32[3,128]{1,0:T(4,128)}, f32[3,128]{1,0:T(4,128)S(1)}, u32[]{:S(2)}) copy-start(f32[3,128]{1,0:T(4,128)S(1)} %get-tuple-element.131) | copy-start | bytes 4612
  351.4 5.7 copy-start.128
  367.8 204.5 %copy-start.73 = (f32[8,128,48]{1,2,0}, f32[8,128,48]{1,2,0:S(1)}, u32[]{:S(2)}) copy-start(f32[8,128,48]{1,2,0:S(1)} %fusion.279) | copy-start | bytes 589828
  383.1 253.0 %copy-start.242 = (f32[3,4,1,16]{3,1,0,2:T(4,128)}, f32[3,4,1,16]{3,1,0,2:T(4,128)S(1)}, u32[]{:S(2)}) copy-start(f32[3,4,1,16]{3,1,0,2:T(4,128)S(1)} %copy.1280) | copy-start | bytes 2308
  405.2 5.2 copy-start.4
  407.3 7.0 copy-start.130
  410.4 161.2 %copy-start.132 = (f32[3,8,1,8,16]{4,2,3,1,0:T(1,128)}, f32[3,8,1,8,16]{4,2,3,1,0:T(1,128)S(1)}, u32[]{:S(2)}) copy-start(f32[3,8,1,8,16]{4,2,3,1,0:T(1,128)S(1)} %fusion.34) | copy-start | bytes 36868
  410.4 146.7 %copy-start.244 = (bf16[32,512]{1,0:T(8,128)(2,1)S(1)}, bf16[32,512]{1,0:T(8,128)(2,1)}, u32[]{:S(2)}) copy-start(bf16[32,512]{1,0:T(8,128)(2,1)} %fusion.168) | copy-start | bytes 98308
  410.4 160.4 %copy-start.67 = (f32[3,64,8,64]{3,2,1,0:T(8,128)S(1)}, f32[3,64,8,64]{3,2,1,0:T(8,128)}, u32[]{:S(2)}) copy-start(f32[3,64,8,64]{3,2,1,0:T(8,128)} %broadcast_multiply_fusion.2) | copy-start | bytes 1179652
  411.2 160.4 %copy-start.129 = (f32[3,32,8,64]{3,2,1,0:T(8,128)S(1)}, f32[3,32,8,64]{3,2,1,0:T(8,128)}, u32[]{:S(2)}) copy-start(f32[3,32,8,64]{3,2,1,0:T(8,128)} %copy-done.128) | copy-start | bytes 589828
  412.7 159.6 %copy-start.264 = (f32[3,128]{1,0:T(4,128)S(1)}, f32[3,128]{1,0:T(4,128)}, u32[]{:S(2)}) copy-start(f32[3,128]{1,0:T(4,128)} %copy-done.263) | copy-start | bytes 4612
  466.3 106.0 %copy-start.285 = (f32[1,3,1,2,16]{4,3,1,2,0:T(2,128)}, f32[1,3,1,2,16]{4,3,1,2,0:T(2,128)S(1)}, u32[]{:S(2)}) copy-start(f32[1,3,1,2,16]{4,3,1,2,0:T(2,128)S(1)} %reshape.3054) | copy-start | bytes 1156
  581.4 5.1 copy-start.38
  622.2 5.5 copy-start.22
  622.7 5.1 copy-start.40
  649.5 6.4 copy-start.251
  676.3 45.5 %copy-start.267 = (f32[384]{0:T(512)}, f32[384]{0:T(512)S(1)}, u32[]{:S(2)}) copy-start(f32[384]{0:T(512)S(1)} %broadcast_multiply_fusion.12) | copy-start | bytes 4612
  689.0 5.1 copy-start.159
  689.3 5.6 copy-start.308
  689.3 5.5 copy-start.237
  689.9 31.9 %copy-start.277 = (f32[384]{0:T(512)}, f32[384]{0:T(512)S(1)}, u32[]{:S(2)}) copy-start(f32[384]{0:T(512)S(1)} %broadcast_multiply_fusion.10) | copy-start | bytes 4612
  691.9 12.6 copy-start.279
  691.9 7.9 copy-start.301
  713.9 9.9 copy-start.84
  741.9 5.1 copy-start.63
  741.9 5.1 copy-start.65
  741.9 5.1 copy-start.155
  741.9 5.1 copy-start.256
  741.9 5.1 copy-start.258
  741.9 5.1 copy-start.323
  767.1 8.1 copy-start.71
  768.6 8.1 copy-start.149
  768.6 9.1 copy-start.151
  768.6 10.3 copy-start.56
  829.6 7.0 copy-start.69
  829.6 8.6 copy-start.145
  830.1 9.1 copy-start.147
  830.1 10.2 copy-start.55
  928.0 188.2 %reduce-scatter.13.cloned.1.call-start = ((), (), s32[]{:S(2)}) async-start(), calls=%async_computation.11 | async-start | bytes 1081344 | tf_op jit(solution)/shard_map/reduce_scatter | solution.py:418
  930.7 320.2 %reduce-scatter.11.cloned.1.call-start = ((), (), s32[]{:S(2)}) async-start(), calls=%async_computation.10 | async-start | bytes 1081344 | tf_op jit(solution)/shard_map/reduce_scatter | solution.py:418
  933.3 49.1 %copy-start.121 = (f32[1,384,512]{2,1,0:T(8,128)S(1)}, f32[1,384,512]{2,1,0:T(8,128)}, u32[]{:S(2)}) copy-start(f32[1,384,512]{2,1,0:T(8,128)} %copy-done.120) | copy-start | bytes 2359300
  934.2 48.4 %copy-start.119 = (f32[1,384,512]{2,1,0:T(8,128)S(1)}, f32[1,384,512]{2,1,0:T(8,128)}, u32[]{:S(2)}) copy-start(f32[1,384,512]{2,1,0:T(8,128)} %copy-done.118) | copy-start | bytes 2359300
  988.4 397.2 %reduce-scatter.9.cloned.1.call-start = ((), (), s32[]{:S(2)}) async-start(), calls=%async_computation.9 | async-start | bytes 1081344 | tf_op jit(solution)/shard_map/reduce_scatter | solution.py:418
  989.0 531.4 %reduce-scatter.7.cloned.1.call-start = ((), (), s32[]{:S(2)}) async-start(), calls=%async_computation.8 | async-start | bytes 1081344 | tf_op jit(solution)/shard_map/reduce_scatter | solution.py:418
  989.8 677.8 %reduce-scatter.17.cloned.1.call-start = ((), (), s32[]{:S(2)}) async-start(), calls=%async_computation.13 | async-start | bytes 4325376 | tf_op jit(solution)/shard_map/reduce_scatter | solution.py:418
  996.7 819.9 %reduce-scatter.15.cloned.1.call-start = ((), (), s32[]{:S(2)}) async-start(), calls=%async_computation.12 | async-start | bytes 4325376 | tf_op jit(solution)/shard_map/reduce_scatter | solution.py:418
  1004.3 6.1 copy-start.314
  1004.3 6.1 copy-start.315
  1015.9 46.4 %copy-start.295 = (f32[384]{0:T(512)S(1)}, f32[384]{0:T(512)}, u32[]{:S(2)}) copy-start(f32[384]{0:T(512)} %copy-done.292) | copy-start | bytes 4612
  1016.0 46.4 %copy-start.299 = (f32[384]{0:T(512)S(1)}, f32[384]{0:T(512)}, u32[]{:S(2)}) copy-start(f32[384]{0:T(512)} %copy-done.296) | copy-start | bytes 4612
  (290 other events, 716.3 us)
Sparse Core Ops, SparseCore 0:
  11.0 59.3 all-gather.6
  73.3 55.8 all-gather.8
  928.1 50.3 all-reduce.53
  981.3 134.8 reduce-scatter.12
  1118.8 131.9 reduce-scatter.10
  1253.6 131.9 reduce-scatter.8
  1388.4 131.9 reduce-scatter.6
  1523.3 144.1 reduce-scatter.16
  1670.5 145.9 reduce-scatter.14
where the time goes:
time: 1830 us; the launch traced here: 1820 us
  waiting for transfers between devices  797 us (44%)
  blocking collectives  460 us (25%)
  local copies, waits for them, and re-layouts  277 us (15%)
  matrix products  146 us (8%)
  other arithmetic  119 us (7%)
  between operations  24.6 us (1%)
    reduce_scatter x6, waiting for transfers between devices, local(): lax.psum_scatter(accumulated, ('dp', 'cont'), scatter_dimension=0, tiled=...  750 us
    all_gather x1, blocking collectives, local(): lax.all_gather(shards[5], ('dp', 'cont'), axis=0, tiled=True)  75.8 us
    all_gather x1, blocking collectives, local(): lax.all_gather(shards[2], ('dp', 'cont'), axis=0, tiled=True)  71.2 us
    all_gather x1, blocking collectives, local(): lax.all_gather(shards[4], ('dp', 'cont'), axis=0, tiled=True)  69.7 us
    all_gather x1, blocking collectives, local(): lax.all_gather(shards[3], ('dp', 'cont'), axis=0, tiled=True)  67.8 us
    unnamed x10, waiting for transfers between devices  47 us
    unnamed x733, local copies, waits for them, and re-layouts  46.5 us
    unnamed x1, blocking collectives  43.1 us
  transfers between devices with their start and end apart: 9, of which 7 were waited for; matrix products, arithmetic and copies ran while one was open for 17% of the time, Pallas kernels for 0%

commit v1 on v0

v1 whole, which is shorter than its diff:
```python
import functools
import types

import jax
import jax.numpy as jnp
from jax import lax
from jax.experimental import pallas as pl
from jax.experimental.pallas import tpu as pltpu
from jax.sharding import PartitionSpec as P

D = 512
HEADS = 8
HEAD_DIM = 64
FF = 2048
BLOCK = 16
CONT_LEN = 128
COARSE = CONT_LEN // BLOCK
PAIRS = HEADS // 2
EPS = 1e-5
SCORE = HEAD_DIM**-0.5
LOG2E = 1.4426950408889634
AWAY = -1e30
F32 = jnp.float32
BF16 = jnp.bfloat16
MESH = pl.DeviceIdType.MESH
LANES = 128


def nn(a, b):
    return jnp.dot(a, b, preferred_element_type=F32)


def nt(a, b):
    return lax.dot_general(a, b, (((1,), (1,)), ((), ())), preferred_element_type=F32)


def tn(a, b):
    return lax.dot_general(a, b, (((0,), (0,)), ((), ())), preferred_element_type=F32)


def iota(shape, dim):
    return lax.broadcasted_iota(jnp.int32, shape, dim)


def norm_stats(x):
    center = x - jnp.mean(x, -1, keepdims=True)
    rstd = lax.rsqrt(jnp.mean(center * center, -1, keepdims=True) + EPS)
    return center * rstd, rstd


def norm_back(xhat, rstd, gain, dn):
    dxhat = dn * gain
    mean_one = jnp.mean(dxhat, -1, keepdims=True)
    mean_two = jnp.mean(dxhat * xhat, -1, keepdims=True)
    return rstd * (dxhat - mean_one - xhat * mean_two)


def colsum(x):
    return jnp.sum(x, 0, keepdims=True)


class Sizes:
    def __init__(self, groups, prompt, conts, nz, exchange, ndev):
        self.groups = groups
        self.prompt = prompt
        self.conts = conts
        self.nz = nz
        self.exchange = exchange
        self.ndev = ndev
        self.nb = prompt // CONT_LEN
        self.tb = self.nb + conts
        self.rows_g = self.tb * CONT_LEN
        self.rows = groups * self.rows_g
        self.blocks = groups * self.tb
        self.far_own = prompt // COARSE
        self.far = self.far_own * nz
        self.r = D // ndev
        self.rf = FF // ndev


def kernel(s, names, *refs):
    r = types.SimpleNamespace(**dict(zip(names, refs)))
    z = lax.axis_index("cont")
    dp = lax.axis_index("dp")
    zs = [lax.rem(z + d, s.nz) for d in range(1, s.nz)]
    pending = []

    def remote(src, dst, ssem, rsem, dev):
        return pltpu.make_async_remote_copy(
            src_ref=src, dst_ref=dst, send_sem=ssem, recv_sem=rsem, device_id=dev, device_id_type=MESH
        )

    def send(src, dst, ssem, rsem, dev):
        copy = remote(src, dst, ssem, rsem, dev)
        copy.start()
        pending.append(copy)

    def wait_recv(dst, ssem, rsem, dev):
        remote(dst, dst, ssem, rsem, dev).wait_recv()

    local_count = [0]

    def local(src, dst):
        copy = pltpu.make_async_copy(src, dst, r.lsem.at[local_count[0]])
        local_count[0] += 1
        copy.start()
        return copy

    def rows_in(prompt, cont, dst):
        out = []
        for g in range(s.groups):
            base = g * s.rows_g
            out.append(local(prompt.at[g], dst.at[pl.ds(base, s.prompt)]))
            for c in range(s.conts):
                out.append(local(cont.at[g, c], dst.at[pl.ds(base + s.prompt + c * CONT_LEN, CONT_LEN)]))
        return out

    if s.exchange:
        core = lax.rem(dp, 2)
        ix = lax.rem(dp // 2, 2)
        iy = dp // 4
        sib = dp + 1 - 2 * core
        xn = dp + 2 - 4 * ix
        yn = dp + 4 - 8 * iy
        cell = dp // 2
        cell_x = cell + 1 - 2 * ix
        cell_y = cell + 2 - 4 * iy
        cell_d = cell_x + cell_y - cell
        sibcore = 1 - core
        other = dp + sib - dp
        del other
        me = dp * s.nz + z

        def sq(first, count):
            return lambda a, n: r.w4.at[pl.ds(first, count), pl.ds(pl.multiple_of(a * s.r, s.r), n * s.r)]

        slicers = [
            lambda a, n: r.tiles.at[pl.ds(a, n)],
            sq(0, 3),
            sq(3, 1),
            lambda a, n: r.wu.at[pl.ds(pl.multiple_of(a * s.r, s.r), n * s.r)],
            lambda a, n: r.wd.at[pl.ds(pl.multiple_of(a * s.rf, s.rf), n * s.rf)],
        ]

        def zset(cell_id, core_id):
            return (cell_id * 2 + core_id) * s.nz

        half = s.nz // 2

        def ag0(k):
            for zz in zs:
                own = slicers[k](me, 1)
                send(own, own, r.ags.at[k, zz], r.agr.at[k, z], (dp, zz))

        def ag1(k):
            for zz in zs:
                wait_recv(slicers[k](dp * s.nz + zz, 1), r.ags.at[k, zz], r.agr.at[k, zz], (dp, zz))
            own = slicers[k](zset(cell, core), s.nz)
            send(own, own, r.ags.at[k, 4], r.agr.at[k, 4], (xn, z))
            send(own, own, r.ags.at[k, 5], r.agr.at[k, 5], (yn, z))
            send(own, own, r.ags.at[k, 8], r.agr.at[k, 8], (sib, z))

        def ag2(k):
            xset = slicers[k](zset(cell_x, core), s.nz)
            yset = slicers[k](zset(cell_y, core), s.nz)
            wait_recv(xset, r.ags.at[k, 4], r.agr.at[k, 4], (xn, z))
            lo = slicers[k](zset(cell_x, core), half)
            send(lo, lo, r.ags.at[k, 6], r.agr.at[k, 6], (yn, z))
            send(xset, xset, r.ags.at[k, 9], r.agr.at[k, 9], (sib, z))
            wait_recv(yset, r.ags.at[k, 5], r.agr.at[k, 5], (yn, z))
            hi = slicers[k](zset(cell_y, core) + half, half)
            send(hi, hi, r.ags.at[k, 7], r.agr.at[k, 7], (xn, z))
            send(yset, yset, r.ags.at[k, 10], r.agr.at[k, 10], (sib, z))

        def ag3(k):
            lo = slicers[k](zset(cell_d, core), half)
            hi = slicers[k](zset(cell_d, core) + half, half)
            wait_recv(lo, r.ags.at[k, 6], r.agr.at[k, 6], (yn, z))
            wait_recv(hi, r.ags.at[k, 7], r.agr.at[k, 7], (xn, z))
            both = slicers[k](zset(cell_d, core), s.nz)
            send(both, both, r.ags.at[k, 11], r.agr.at[k, 11], (sib, z))

        def ag4(k):
            for i, c in enumerate((cell, cell_x, cell_y, cell_d)):
                wait_recv(slicers[k](zset(c, sibcore), s.nz), r.ags.at[k, 8 + i], r.agr.at[k, 8 + i], (sib, z))

        grads = [(r.gq, r.rcq, r.rdq, r.rxq, r.rzq), (r.go, r.rco, r.rdo, r.rxo, r.rzo),
                 (r.gu, r.rcu, r.rdu, r.rxu, r.rzu), (r.gd, r.rcd, r.rdd, r.rxd, r.rzd)]

        def rs0(k):
            g, rc, _, _, _ = grads[k]
            send(g.at[:, :, sibcore], rc, r.rss.at[k, 0], r.rsr.at[k, 0], (sib, z))

        def add_to(g, j, c, lo, n, term):
            place = (j, c, core, pl.ds(lo, n))
            g[place] = (g[place].astype(F32) + term).astype(BF16)

        def rs1(k):
            g, rc, rd, _, _ = grads[k]
            nj, m = g.shape[0], g.shape[3]
            wait_recv(rc, r.rss.at[k, 0], r.rsr.at[k, 0], (sib, z))
            for j in range(nj):
                add_to(g, j, cell_d, 0, m, rc[j, cell_d].astype(F32))
            mh = m // 2
            send(g.at[:, cell_d, core, pl.ds(0, mh)], rd.at[0], r.rss.at[k, 1], r.rsr.at[k, 1], (yn, z))
            send(g.at[:, cell_d, core, pl.ds(mh, mh)], rd.at[1], r.rss.at[k, 2], r.rsr.at[k, 2], (xn, z))
            for c in (cell_x, cell_y, cell):
                for j in range(nj):
                    add_to(g, j, c, 0, m, rc[j, c].astype(F32))

        def rs2(k):
            g, _, rd, rx, _ = grads[k]
            nj, m = g.shape[0], g.shape[3]
            mh = m // 2
            wait_recv(rd.at[0], r.rss.at[k, 1], r.rsr.at[k, 1], (yn, z))
            for j in range(nj):
                add_to(g, j, cell_x, 0, mh, rd[0, j].astype(F32))
            send(g.at[:, cell_x, core], rx.at[0], r.rss.at[k, 3], r.rsr.at[k, 3], (xn, z))
            wait_recv(rd.at[1], r.rss.at[k, 2], r.rsr.at[k, 2], (xn, z))
            for j in range(nj):
                add_to(g, j, cell_y, mh, mh, rd[1, j].astype(F32))
            send(g.at[:, cell_y, core], rx.at[1], r.rss.at[k, 4], r.rsr.at[k, 4], (yn, z))

        def piece(g, zz):
            n = g.shape[3] // s.nz
            return pl.ds(pl.multiple_of(zz * n, n), n)

        def rs3(k):
            g, _, _, rx, rz = grads[k]
            nj, m = g.shape[0], g.shape[3]
            wait_recv(rx.at[0], r.rss.at[k, 3], r.rsr.at[k, 3], (xn, z))
            wait_recv(rx.at[1], r.rss.at[k, 4], r.rsr.at[k, 4], (yn, z))
            for j in range(nj):
                add_to(g, j, cell, 0, m, rx[0, j].astype(F32) + rx[1, j].astype(F32))
            for zz in zs:
                send(g.at[:, cell, core, piece(g, zz)], rz.at[z], r.rss.at[k, 5 + zz], r.rsr.at[k, 5 + z], (dp, zz))

        def rs4(k, outs):
            g, _, _, _, rz = grads[k]
            for zz in zs:
                wait_recv(rz.at[zz], r.rss.at[k, 5 + zz], r.rsr.at[k, 5 + zz], (dp, zz))
            for j, out in enumerate(outs):
                total = g[j, cell, core, piece(g, z)].astype(F32)
                for zz in zs:
                    total = total + rz[zz, j].astype(F32)
                out[...] = total
    else:

        def nothing(*_):
            return None

        ag0 = ag1 = ag2 = ag3 = ag4 = rs0 = rs1 = rs2 = rs3 = rs4 = nothing

    if s.exchange:
        weights_in = [
            local(r.wq, r.w4.at[0, pl.ds(pl.multiple_of(me * s.r, s.r), s.r)]),
            local(r.wk, r.w4.at[1, pl.ds(pl.multiple_of(me * s.r, s.r), s.r)]),
            local(r.wv, r.w4.at[2, pl.ds(pl.multiple_of(me * s.r, s.r), s.r)]),
            local(r.wo, r.w4.at[3, pl.ds(pl.multiple_of(me * s.r, s.r), s.r)]),
            local(r.wup, slicers[3](me, 1)),
            local(r.wdn, slicers[4](me, 1)),
        ]
    else:
        weights_in = [local(w, r.w4.at[j]) for j, w in enumerate((r.wq, r.wk, r.wv, r.wo))]
        weights_in += [local(r.wup, r.wu), local(r.wdn, r.wd)]
    x_in = rows_in(r.px, r.cx, r.x)
    later_in = rows_in(r.pdy, r.cdy, r.dy) + [
        local(r.te.at[g, c], r.teach.at[g * s.conts + c]) for g in range(s.groups) for c in range(s.conts)
    ]

    barrier = pltpu.get_barrier_semaphore()
    partners = [(dp, zz) for zz in zs]
    if s.exchange:
        partners += [(sib, z), (xn, z), (yn, z)]
    for dev in partners:
        pl.semaphore_signal(barrier, inc=1, device_id=dev, device_id_type=MESH)

    if s.exchange:
        r.build[...] = jnp.zeros_like(r.build)
        for i, v in enumerate((r.v1g, r.v1b, r.v2g, r.v2b, r.vdb)):
            r.build[pl.ds(i, 1), pl.ds(0, s.r)] = v[...].astype(F32)
        r.build[pl.ds(5, 1), pl.ds(0, s.rf)] = r.vub[...].astype(F32)
        own_tokens = 0
        for g in range(s.groups):
            for c in range(s.conts):
                own_tokens = own_tokens + r.lens[g, c]
        tile = r.build[...]
        row = iota((8, LANES), 0)
        placed = jnp.where(
            row < 5,
            pltpu.roll(tile, lax.rem(me, LANES // s.r) * s.r, 1),
            pltpu.roll(tile, lax.rem(me, LANES // s.rf) * s.rf, 1),
        )
        r.tiles[me] = jnp.where(row == 6, own_tokens.astype(F32), placed)

    lane_lo = iota((CONT_LEN, LANES), 1) < HEAD_DIM
    ri = iota((3 * CONT_LEN, CONT_LEN), 0)
    ci = iota((3 * CONT_LEN, CONT_LEN), 1)
    level = ri // CONT_LEN + 1
    rep = jnp.where(((ri % CONT_LEN) >> level) == (ci >> level), 1.0, 0.0)
    scale_l = jnp.where(level == 1, 0.5, jnp.where(level == 2, 0.25, 0.125))
    r.rep[...] = (rep * scale_l).astype(BF16)
    ri = iota((64, CONT_LEN), 0)
    ci = iota((64, CONT_LEN), 1)
    coarse_ci = jnp.where(ri < 32, ci >> 1, jnp.where(ri < 48, ci >> 2, ci >> 3))
    position = jnp.where(ri < 16, ri, jnp.where(ri < 32, ri + 16, jnp.where(ri < 48, ri - 32, ri - 48)))
    r.pool[...] = jnp.where(coarse_ci == position, 1.0, 0.0).astype(BF16)
    ri = iota((CONT_LEN, CONT_LEN), 0)
    ci = iota((CONT_LEN, CONT_LEN), 1)
    bi, bj = ri >> 4, ci >> 4
    near = ((bi == bj) & (ci <= ri)) | (((bi & 1) == 1) & (bj == bi - 1))
    r.bias0[...] = jnp.where(near, 0.0, AWAY)
    ri = iota((CONT_LEN, 64), 0)
    ci = iota((CONT_LEN, 64), 1)
    reader = jnp.where(ci < 32, ri >> 5, ri >> 6)
    wanted = jnp.where(ci < 16, 1, jnp.where(ci < 32, 3, jnp.where(ci < 48, 1, 9)))
    r.bias1[...] = jnp.where(reader == wanted, 0.0, AWAY)
    r.vg[...] = jnp.zeros_like(r.vg)
    r.df[...] = jnp.zeros_like(r.df)

    for copy in weights_in:
        copy.wait()
    pl.semaphore_wait(barrier, len(partners))

    if s.exchange:
        for k in range(5):
            ag0(k)
        ag1(0)
        ag1(1)
        ag2(0)
        ag2(1)
        ag3(0)
        ag3(1)
        ag4(0)
        count = 8
        for k in range(s.ndev // count):
            part = jnp.sum(r.tiles[pl.ds(k * count, count)], 0)
            r.vec[:, pl.ds(k * LANES, LANES)] = part
        for k in range(s.ndev // 2):
            part = r.tiles[2 * k] + r.tiles[2 * k + 1]
            r.upb[:, pl.ds(k * LANES, LANES)] = part[5:6]
        ag1(2)
    else:
        r.vec[...] = r.vecs[...]
        r.upb[...] = r.upbs[...]

    def vec(i):
        return r.vec[pl.ds(i, 1), :]

    token_row = r.vec[pl.ds(6, 1), pl.ds(0, LANES)]
    for k in range(1, D // LANES):
        token_row = token_row + r.vec[pl.ds(6, 1), pl.ds(k * LANES, LANES)]
    token_row = jnp.concatenate([token_row] * (D // LANES), 1)

    def length_of(g, b):
        c = jnp.clip(b - s.nb, 0, s.conts - 1)
        return jnp.where(b >= s.nb, r.lens[g, c], CONT_LEN)

    for copy in x_in:
        copy.wait()

    def norm_one(i, carry):
        rows = pl.ds(pl.multiple_of(i * CONT_LEN, CONT_LEN), CONT_LEN)
        xhat, _ = norm_stats(r.x[rows].astype(F32))
        r.n1[rows] = (xhat * vec(0) + vec(1)).astype(BF16)
        return carry

    lax.fori_loop(0, s.blocks, norm_one, 0)
    ag1(3)
    ag4(1)

    def project(t, carry):
        g, b = t // s.tb, lax.rem(t, s.tb)
        rows = pl.ds(pl.multiple_of(t * CONT_LEN, CONT_LEN), CONT_LEN)
        n1 = r.n1[rows]
        keep = iota((CONT_LEN, D), 0) < length_of(g, b)
        qv = nn(n1, r.w4[0]).astype(BF16)
        kv = jnp.where(keep, nn(n1, r.w4[1]), 0.0).astype(BF16)
        vv = jnp.where(keep, nn(n1, r.w4[2]), 0.0).astype(BF16)
        r.q[rows] = qv
        r.k[rows] = kv
        r.v[rows] = vv
        pr = iota((64, D), 0)
        mean_scale = jnp.where(pr < 32, 0.5, jnp.where(pr < 48, 0.25, 0.125))
        r.kl[t] = (nn(r.pool[...], kv) * mean_scale).astype(BF16)
        r.vl[t] = nn(r.pool[...], vv).astype(BF16)
        return carry

    lax.fori_loop(0, s.blocks, project, 0)
    for g in range(s.groups):
        for b in range(s.nb):
            place = pl.ds(pl.multiple_of(z * s.far_own + b * BLOCK, BLOCK), BLOCK)
            r.fkv[0, g, place] = r.kl[g * s.tb + b, pl.ds(48, BLOCK)]
            r.fkv[1, g, place] = r.vl[g * s.tb + b, pl.ds(48, BLOCK)]

    def far_rows(zz):
        return r.fkv.at[:, :, pl.ds(pl.multiple_of(zz * s.far_own, s.far_own), s.far_own)]

    for zz in zs:
        send(far_rows(z), far_rows(z), r.fs.at[0, zz], r.fr.at[0, z], (dp, zz))
    ag1(4)
    ag2(2)
    ag2(3)

    def reps(t, carry):
        rows = pl.ds(pl.multiple_of(t * CONT_LEN, CONT_LEN), CONT_LEN)
        r.qr[t] = nn(r.rep[...], r.q[rows]).astype(BF16)
        return carry

    lax.fori_loop(0, s.blocks, reps, 0)
    ag3(2)
    for zz in zs:
        wait_recv(far_rows(zz), r.fs.at[0, zz], r.fr.at[0, zz], (dp, zz))

    def two(a):
        zero = jnp.zeros_like(a)
        return jnp.concatenate([jnp.where(lane_lo, a, zero), jnp.where(lane_lo, zero, a)], 0)

    def pick(a):
        return jnp.where(lane_lo, a[:CONT_LEN], a[CONT_LEN:])

    def operands(t, g, p):
        rows = pl.ds(pl.multiple_of(t * CONT_LEN, CONT_LEN), CONT_LEN)
        lanes = pl.ds(p * LANES, LANES)
        q = r.q[rows, lanes]
        q1 = r.qr[t, pl.ds(0, CONT_LEN), lanes]
        q2 = r.qr[t, pl.ds(CONT_LEN, CONT_LEN), lanes]
        q3 = r.qr[t, pl.ds(2 * CONT_LEN, CONT_LEN), lanes]
        q03 = jnp.concatenate([two(q), two(q3)], 1)
        q12 = jnp.concatenate([two(q1), two(q2)], 1)
        k0 = r.k[rows, lanes]
        kf = r.fkv[0, g, :, lanes]
        zero = jnp.zeros_like(k0)
        k03 = jnp.concatenate([jnp.concatenate([k0, zero], 1), jnp.concatenate([zero, kf], 1)], 0)
        kl = r.kl[t, :, lanes]
        kr = iota(kl.shape, 0)
        zl = jnp.zeros_like(kl)
        k12 = jnp.concatenate(
            [jnp.where(kr < 32, kl, zl), jnp.where((kr >= 32) & (kr < 48), kl, zl)], 1
        )
        return q03, q12, k03, k12

    def value_operands(t, g, p, counts0, counts1):
        rows = pl.ds(pl.multiple_of(t * CONT_LEN, CONT_LEN), CONT_LEN)
        lanes = pl.ds(p * LANES, LANES)
        v0 = r.v[rows, lanes]
        vf = r.fkv[1, g, :, lanes]
        eight = jnp.full((s.far, LANES), float(COARSE), BF16)
        vn03 = jnp.concatenate(
            [jnp.concatenate([v0, counts0], 1), jnp.concatenate([vf, eight], 1)], 0
        )
        vn12 = jnp.concatenate([r.vl[t, :, lanes], counts1], 1)
        return vn03, vn12

    def counts(length):
        i0 = iota((CONT_LEN, LANES), 0)
        counts0 = jnp.where(i0 < length, 1.0, 0.0).astype(BF16)
        i1 = iota((64, LANES), 0)
        first = jnp.where(i1 < 16, 2 * i1, jnp.where(i1 < 32, 2 * (i1 + 16), 4 * (i1 - 32)))
        width = jnp.where(i1 < 32, 2, 4)
        counts1 = jnp.where(i1 < 48, jnp.clip(length - first, 0, width), 0).astype(F32).astype(BF16)
        return counts0, counts1

    def attend(t, carry):
        g, b = t // s.tb, lax.rem(t, s.tb)
        rows = pl.ds(pl.multiple_of(t * CONT_LEN, CONT_LEN), CONT_LEN)
        counts0, counts1 = counts(length_of(g, b))
        limit = jnp.where(b >= s.nb, s.far, BLOCK * (z * s.nb + b))
        bias_far = jnp.where(iota((CONT_LEN, s.far), 1) < limit, 0.0, AWAY)
        bias = jnp.concatenate([r.bias0[...], bias_far], 1)
        bias = jnp.concatenate([bias, bias], 0)
        bias1 = jnp.concatenate([r.bias1[...], r.bias1[...]], 0)
        for p in range(PAIRS):
            q03, q12, k03, k12 = operands(t, g, p)
            vn03, vn12 = value_operands(t, g, p, counts0, counts1)
            e03 = jnp.exp2(nt(q03, k03) * (SCORE * LOG2E) + bias).astype(BF16)
            e12 = jnp.exp2(nt(q12, k12) * (SCORE * LOG2E) + bias1).astype(BF16)
            r.e03[t * PAIRS + p] = e03
            r.e12[t * PAIRS + p] = e12
            total = nn(e03, vn03) + nn(e12, vn12)
            numerator = pick(total[:, :LANES])
            denominator = pick(total[:, LANES:])
            lanes = pl.ds(p * LANES, LANES)
            r.att[rows, lanes] = (numerator / denominator).astype(BF16)
            r.den[rows, lanes] = denominator
        return carry

    lax.fori_loop(0, s.tb, attend, 0)
    ag2(4)
    ag3(3)
    lax.fori_loop(s.tb, s.blocks, attend, 0)
    ag3(4)
    ag4(2)

    for copy in later_in:
        copy.wait()
    for g in range(s.groups):
        rows = pl.ds(g * s.rows_g, s.rows_g)
        mixed = r.x[rows].astype(F32) + nn(r.att[rows], r.w4[3])
        r.mix[rows] = mixed
        xhat, _ = norm_stats(mixed)
        r.n2[rows] = (xhat * vec(2) + vec(3)).astype(BF16)
    ag4(3)
    for g in range(s.groups):
        rows = pl.ds(g * s.rows_g, s.rows_g)
        for n in range(FF // D):
            cols = pl.ds(n * D, D)
            pre = nn(r.n2[rows], r.wu[:, cols]) + r.upb[:, cols]
            r.h[rows, cols] = jnp.maximum(pre, 0.0).astype(BF16)
    ag4(4)
    outs = []

    def rows_out(src, prompt, cont, g):
        base = g * s.rows_g
        outs.append(local(src.at[pl.ds(base, s.prompt)], prompt.at[g]))
        for c in range(s.conts):
            outs.append(local(src.at[pl.ds(base + s.prompt + c * CONT_LEN, CONT_LEN)], cont.at[g, c]))

    extra = 2.0 * r.ls[0, 0] / (token_row * float(D))
    for g in range(s.groups):
        base = g * s.rows_g
        rows = pl.ds(base, s.rows_g)
        y = r.mix[rows] + nn(r.h[rows], r.wd[...]) + vec(4)
        r.y[rows] = y.astype(BF16)
        rows_out(r.y, r.py, r.cy, g)
        gy = r.dy[rows].astype(F32)
        parts = [gy[: s.prompt]]
        for c in range(s.conts):
            lo = s.prompt + c * CONT_LEN
            keep = iota((CONT_LEN, D), 0) < r.lens[g, c]
            diff = jnp.where(keep, y[lo : lo + CONT_LEN] - r.teach[g * s.conts + c].astype(F32), 0.0)
            r.vg[pl.ds(5, 1), :] += colsum(diff * diff)
            parts.append(gy[lo : lo + CONT_LEN] + extra * diff)
        gy = jnp.concatenate(parts, 0)
        r.gy[rows] = gy
        r.gyb[rows] = gy.astype(BF16)
        r.vg[pl.ds(4, 1), :] += colsum(gy)

    for n in range(FF // D):
        cols = pl.ds(n * D, D)
        r.gd[0, n] = tn(r.h[:, cols], r.gyb[...]).astype(BF16).reshape(2, FF // 8, D)
    rs0(3)
    for n in range(FF // D):
        cols = pl.ds(n * D, D)
        for g in range(s.groups):
            rows = pl.ds(g * s.rows_g, s.rows_g)
            dh = nt(r.gyb[rows], r.wd[cols])
            dpre = jnp.where(r.h[rows, cols] > 0, dh, 0.0).astype(BF16)
            r.h[rows, cols] = dpre
            r.vg[pl.ds(8 + n, 1), :] += colsum(dpre.astype(F32))
        r.gu[0, :, :, :, cols] = tn(r.n2[...], r.h[:, cols]).astype(BF16).reshape(4, 2, D // 8, D)
    rs0(2)
    rs1(3)
    for g in range(s.groups):
        rows = pl.ds(g * s.rows_g, s.rows_g)
        dn2 = nt(r.h[rows], r.wu[...])
        xhat, rstd = norm_stats(r.mix[rows])
        r.vg[pl.ds(2, 1), :] += colsum(dn2 * xhat)
        r.vg[pl.ds(3, 1), :] += colsum(dn2)
        dmixed = r.gy[rows] + norm_back(xhat, rstd, vec(2), dn2)
        r.gy[rows] = dmixed
        r.gyb[rows] = dmixed.astype(BF16)
    rs1(2)
    rs2(3)
    r.go[0] = tn(r.att[...], r.gyb[...]).astype(BF16).reshape(4, 2, D // 8, D)
    rs0(1)
    for g in range(s.groups):
        rows = pl.ds(g * s.rows_g, s.rows_g)
        dnum = nt(r.gyb[rows], r.w4[3]) / r.den[rows]
        r.dnum[rows] = dnum.astype(BF16)
        r.xo[rows] = (-dnum * r.att[rows].astype(F32)).astype(BF16)
    rs2(2)
    rs1(1)
    rs3(3)

    def attend_back(t, carry):
        g, b = t // s.tb, lax.rem(t, s.tb)
        rows = pl.ds(pl.multiple_of(t * CONT_LEN, CONT_LEN), CONT_LEN)
        length = length_of(g, b)
        counts0, counts1 = counts(length)
        keep = iota((CONT_LEN, LANES), 0) < length
        for p in range(PAIRS):
            lanes = pl.ds(p * LANES, LANES)
            q03, q12, k03, k12 = operands(t, g, p)
            vn03, vn12 = value_operands(t, g, p, counts0, counts1)
            dnum = two(r.dnum[rows, lanes])
            x = jnp.concatenate([dnum, two(r.xo[rows, lanes])], 1)
            e03 = r.e03[t * PAIRS + p]
            e12 = r.e12[t * PAIRS + p]
            ds03 = (nt(x, vn03) * e03.astype(F32)).astype(BF16)
            ds12 = (nt(x, vn12) * e12.astype(F32)).astype(BF16)
            dq03 = nn(ds03, k03)
            dq12 = nn(ds12, k12)
            coarse = jnp.concatenate(
                [pick(dq12[:, :LANES]), pick(dq12[:, LANES:]), pick(dq03[:, LANES:])], 0
            ).astype(BF16)
            dq = pick(dq03[:, :LANES]) + tn(r.rep[...], coarse)
            r.dqkv[0, rows, lanes] = (dq * SCORE).astype(BF16)
            dk03 = tn(ds03, q03)
            dk12 = tn(ds12, q12)
            dv03 = tn(e03, dnum)
            dv12 = tn(e12, dnum)
            kr = iota((64, LANES), 0)
            dkl = jnp.where(
                kr < 32, 0.5 * dk12[:, :LANES], jnp.where(kr < 48, 0.25 * dk12[:, LANES:], 0.0)
            ).astype(BF16)
            dk = dk03[:CONT_LEN, :LANES] + tn(r.pool[...], dkl)
            dv = dv03[:CONT_LEN] + tn(r.pool[...], dv12.astype(BF16))
            r.dkv[0, rows, lanes] = jnp.where(keep, dk * SCORE, 0.0)
            r.dkv[1, rows, lanes] = jnp.where(keep, dv, 0.0)
            r.df[0, g, :, lanes] += dk03[CONT_LEN:, LANES:] * SCORE
            r.df[1, g, :, lanes] += dv03[CONT_LEN:]
        return carry

    def far_part(ref, g, zz):
        return ref.at[g, :, pl.ds(pl.multiple_of(zz * s.far_own, s.far_own), s.far_own)]

    def far_back(g):
        for i in range(2):
            r.dfs[g, i] = r.df[i, g].astype(BF16)
        for zz in zs:
            send(far_part(r.dfs, g, zz), r.rf.at[g, z], r.fs.at[1 + g, zz], r.fr.at[1 + g, z], (dp, zz))

    for g in range(s.groups):
        lax.fori_loop(g * s.tb, (g + 1) * s.tb, attend_back, 0)
        far_back(g)
        if g == 0:
            rs3(2)
            rs2(1)
            rs4(3, [r.ogd] if s.exchange else None)
    r.gq[0] = tn(r.n1[...], r.dqkv[0]).astype(BF16).reshape(4, 2, D // 8, D)
    rs3(1)
    rs4(2, [r.ogu] if s.exchange else None)
    spread = jnp.where(
        iota((s.prompt, s.far_own), 0) // COARSE == iota((s.prompt, s.far_own), 1), 1.0, 0.0
    ).astype(BF16)
    for g in range(s.groups):
        base = g * s.rows_g
        for zz in zs:
            wait_recv(r.rf.at[g, zz], r.fs.at[1 + g, zz], r.fr.at[1 + g, zz], (dp, zz))
        own = pl.ds(pl.multiple_of(z * s.far_own, s.far_own), s.far_own)
        for i, scale in enumerate((1.0 / COARSE, 1.0)):
            total = r.df[i, g, own]
            for zz in zs:
                total = total + r.rf[g, zz, i].astype(F32)
            wide = nn(spread, total.astype(BF16)) * scale
            rows = pl.ds(base, s.prompt)
            r.dqkv[1 + i, rows] = (r.dkv[i, rows] + wide).astype(BF16)
            rows = pl.ds(base + s.prompt, s.rows_g - s.prompt)
            r.dqkv[1 + i, rows] = r.dkv[i, rows].astype(BF16)

    for j in (1, 2):
        r.gq[j] = tn(r.n1[...], r.dqkv[j]).astype(BF16).reshape(4, 2, D // 8, D)
    rs0(0)
    for g in range(s.groups):
        rows = pl.ds(g * s.rows_g, s.rows_g)
        dn1 = nt(r.dqkv[0, rows], r.w4[0]) + nt(r.dqkv[1, rows], r.w4[1]) + nt(r.dqkv[2, rows], r.w4[2])
        xhat, rstd = norm_stats(r.x[rows].astype(F32))
        r.vg[pl.ds(0, 1), :] += colsum(dn1 * xhat)
        r.vg[pl.ds(1, 1), :] += colsum(dn1)
        r.gy[rows] = r.gy[rows] + norm_back(xhat, rstd, vec(0), dn1)
        rows_out(r.gy, r.pdx, r.cdx, g)

    if s.exchange:
        def vsend(src, i, ssem, dev, ri):
            send(src, r.rv.at[i], r.vs.at[ssem], r.vr.at[ri], dev)

        vsend(r.vg, 0, 0, (sib, z), 0)
        rs1(0)
        rs4(1, [r.ogo])
        wait_recv(r.rv.at[0], r.vs.at[0], r.vr.at[0], (sib, z))
        r.vt[0] = r.vg[...] + r.rv[0]
        vsend(r.vt.at[0], 1, 1, (xn, z), 1)
        rs2(0)
        wait_recv(r.rv.at[1], r.vs.at[1], r.vr.at[1], (xn, z))
        r.vt[1] = r.vt[0] + r.rv[1]
        vsend(r.vt.at[1], 2, 2, (yn, z), 2)
        rs3(0)
        wait_recv(r.rv.at[2], r.vs.at[2], r.vr.at[2], (yn, z))
        r.vt[2] = r.vt[1] + r.rv[2]
        for zz in zs:
            send(r.vt.at[2], r.rv.at[3 + z], r.vs.at[3 + zz], r.vr.at[3 + z], (dp, zz))
        for zz in zs:
            wait_recv(r.rv.at[3 + zz], r.vs.at[3 + zz], r.vr.at[3 + zz], (dp, zz))
        r.rv[3 + z] = r.vt[2]
        total = r.rv[3]
        for i in range(1, s.nz):
            total = total + r.rv[3 + i]
        loss = jnp.sum(total[5:6], 1, keepdims=True) / (token_row[:, :1] * float(D))
        mine = jnp.zeros((8, LANES), F32)
        per = LANES // s.r
        for k in range(D // LANES):
            mine = jnp.where(me // per == k, total[:8, k * LANES : (k + 1) * LANES], mine)
        mine = pltpu.roll(mine, lax.rem(LANES - lax.rem(me, per) * s.r, LANES), 1)
        per = LANES // s.rf
        up = jnp.zeros((1, LANES), F32)
        for k in range(FF // LANES):
            i, j = divmod(k, D // LANES)
            up = jnp.where(me // per == k, total[8 + i : 9 + i, j * LANES : (j + 1) * LANES], up)
        up = jnp.broadcast_to(up, (8, LANES))
        up = pltpu.roll(up, lax.rem(LANES - lax.rem(me, per) * s.rf, LANES), 1)
        row = iota((8, LANES), 0)
        r.ov[...] = jnp.where(row < 5, mine, jnp.where(row == 5, loss, up))
        rs4(0, [r.ogq, r.ogk, r.ogv])
    else:
        r.ov[...] = r.vg[...]
        for src, dst in ((r.gq, r.fgq), (r.go, r.fgo), (r.gu, r.fgu), (r.gd, r.fgd)):
            outs.append(local(src, dst))
    for copy in outs:
        copy.wait()
    for copy in pending:
        copy.wait_send()


def layer(
    mesh,
    prompt_x,
    cont_x,
    prompt_dy,
    cont_dy,
    teacher,
    cont_lengths,
    loss_scale,
    norm1_gain,
    norm1_bias,
    w_query,
    w_key,
    w_value,
    w_out,
    norm2_gain,
    norm2_bias,
    w_up,
    up_bias,
    w_down,
    down_bias,
):
    nz, ndp = mesh.shape["cont"], mesh.shape["dp"]
    ndev = nz * ndp
    exchange = ndp == 8 and nz == 4
    groups, prompt = prompt_x.shape[:2]
    conts = cont_x.shape[1]
    s = Sizes(groups, prompt, conts, nz, exchange, ndev)
    both = ("dp", "cont")
    any_spec = pl.BlockSpec(memory_space=pl.ANY)
    vmem = pl.BlockSpec(memory_space=pltpu.VMEM)
    smem = pl.BlockSpec(memory_space=pltpu.SMEM)

    inputs = {
        "px": (prompt_x, any_spec),
        "cx": (cont_x, any_spec),
        "pdy": (prompt_dy, any_spec),
        "cdy": (cont_dy, any_spec),
        "te": (teacher, any_spec),
        "lens": (cont_lengths, smem),
        "ls": (loss_scale.reshape(1, 1), smem),
    }
    weights = {"wq": w_query, "wk": w_key, "wv": w_value, "wo": w_out, "wup": w_up, "wdn": w_down}
    vectors = {"v1g": norm1_gain, "v1b": norm1_bias, "v2g": norm2_gain, "v2b": norm2_bias, "vdb": down_bias}
    if exchange:
        for name, w in weights.items():
            inputs[name] = (w, any_spec)
        for name, v in vectors.items():
            inputs[name] = (v.reshape(1, -1), vmem)
        inputs["vub"] = (up_bias.reshape(1, -1), vmem)
    else:
        for name, w in weights.items():
            inputs[name] = (lax.all_gather(w, both, axis=0, tiled=True), any_spec)
        tokens = lax.psum(jnp.sum(cont_lengths).astype(F32), both)
        full = [lax.all_gather(v, both, axis=0, tiled=True).astype(F32) for v in vectors.values()]
        zero = jnp.zeros((D,), F32)
        inputs["vecs"] = (jnp.stack(full + [zero, jnp.full((D,), tokens / (D // LANES)), zero]), vmem)
        up_full = lax.all_gather(up_bias, both, axis=0, tiled=True).astype(F32)
        inputs["upbs"] = (up_full.reshape(1, FF), vmem)

    m, mf = D // 8, FF // 8
    outputs = {
        "py": (prompt_x.shape, BF16, any_spec),
        "cy": (cont_x.shape, BF16, any_spec),
        "pdx": (prompt_x.shape, F32, any_spec),
        "cdx": (cont_x.shape, F32, any_spec),
    }
    if exchange:
        for name in ("ogq", "ogk", "ogv", "ogo"):
            outputs[name] = ((s.r, D), F32, vmem)
        outputs["ogu"] = ((s.r, FF), F32, vmem)
        outputs["ogd"] = ((s.rf, D), F32, vmem)
        outputs["ov"] = ((8, LANES), F32, vmem)
    else:
        outputs["fgq"] = ((3, 4, 2, m, D), BF16, any_spec)
        outputs["fgo"] = ((1, 4, 2, m, D), BF16, any_spec)
        outputs["fgu"] = ((1, 4, 2, m, FF), BF16, any_spec)
        outputs["fgd"] = ((1, 4, 2, mf, D), BF16, any_spec)
        outputs["ov"] = ((16, D), F32, vmem)

    rows, blocks = s.rows, s.blocks
    dma = pltpu.SemaphoreType.DMA
    scratch = {
        "w4": ((4, D, D), BF16),
        "wu": ((D, FF), BF16),
        "wd": ((FF, D), BF16),
        "vec": ((8, D), F32),
        "upb": ((1, FF), F32),
        "x": ((rows, D), BF16),
        "dy": ((rows, D), BF16),
        "teach": ((groups * conts, CONT_LEN, D), BF16),
        "y": ((rows, D), BF16),
        "n1": ((rows, D), BF16),
        "q": ((rows, D), BF16),
        "k": ((rows, D), BF16),
        "v": ((rows, D), BF16),
        "qr": ((blocks, 3 * CONT_LEN, D), BF16),
        "kl": ((blocks, 64, D), BF16),
        "vl": ((blocks, 64, D), BF16),
        "fkv": ((2, groups, s.far, D), BF16),
        "rep": ((3 * CONT_LEN, CONT_LEN), BF16),
        "pool": ((64, CONT_LEN), BF16),
        "bias0": ((CONT_LEN, CONT_LEN), F32),
        "bias1": ((CONT_LEN, 64), F32),
        "e03": ((blocks * PAIRS, 2 * CONT_LEN, CONT_LEN + s.far), BF16),
        "e12": ((blocks * PAIRS, 2 * CONT_LEN, 64), BF16),
        "att": ((rows, D), BF16),
        "den": ((rows, D), F32),
        "mix": ((rows, D), F32),
        "n2": ((rows, D), BF16),
        "h": ((rows, FF), BF16),
        "gy": ((rows, D), F32),
        "gyb": ((rows, D), BF16),
        "dnum": ((rows, D), BF16),
        "xo": ((rows, D), BF16),
        "dqkv": ((3, rows, D), BF16),
        "dkv": ((2, rows, D), F32),
        "df": ((2, groups, s.far, D), F32),
        "dfs": ((groups, 2, s.far, D), BF16),
        "rf": ((groups, nz, 2, s.far_own, D), BF16),
        "vg": ((16, D), F32),
        "gq": ((3, 4, 2, m, D), BF16),
        "go": ((1, 4, 2, m, D), BF16),
        "gu": ((1, 4, 2, m, FF), BF16),
        "gd": ((1, 4, 2, mf, D), BF16),
        "lsem": dma((64,)),
        "fs": dma((1 + groups, nz)),
        "fr": dma((1 + groups, nz)),
    }
    if exchange:
        scratch["tiles"] = ((ndev, 8, LANES), F32)
        scratch["build"] = ((8, LANES), F32)
        for name, (nj, rr, cc) in {"q": (3, m, D), "o": (1, m, D), "u": (1, m, FF), "d": (1, mf, D)}.items():
            scratch["rc" + name] = ((nj, 4, rr, cc), BF16)
            scratch["rd" + name] = ((2, nj, rr // 2, cc), BF16)
            scratch["rx" + name] = ((2, nj, rr, cc), BF16)
            scratch["rz" + name] = ((nz, nj, rr // nz, cc), BF16)
        scratch["rv"] = ((3 + nz, 16, D), F32)
        scratch["vt"] = ((3, 16, D), F32)
        scratch["ags"] = dma((5, 12))
        scratch["agr"] = dma((5, 12))
        scratch["rss"] = dma((4, 5 + nz))
        scratch["rsr"] = dma((4, 5 + nz))
        scratch["vs"] = dma((3 + nz,))
        scratch["vr"] = dma((3 + nz,))

    names = list(inputs) + list(outputs) + list(scratch)
    results = pl.pallas_call(
        functools.partial(kernel, s, names),
        out_shape=[jax.ShapeDtypeStruct(shape, dtype) for shape, dtype, _ in outputs.values()],
        in_specs=[spec for _, spec in inputs.values()],
        out_specs=[spec for _, _, spec in outputs.values()],
        scratch_shapes=[pltpu.VMEM(*v) if isinstance(v, tuple) else v for v in scratch.values()],
        compiler_params=pltpu.CompilerParams(
            collective_id=0, has_side_effects=True, vmem_limit_bytes=64 * 1024 * 1024 - 65536
        ),
        name="layer",
    )(*[a for a, _ in inputs.values()])
    o = types.SimpleNamespace(**dict(zip(outputs, results)))
    if exchange:
        vec = [o.ov[i, : s.r] for i in range(5)]
        loss = o.ov[5, 0]
        up_vec = o.ov[6, : s.rf]
        mats = [o.ogq, o.ogk, o.ogv, o.ogo, o.ogu, o.ogd]
    else:
        whole = [o.fgq[0], o.fgq[1], o.fgq[2], o.fgo[0], o.fgu[0], o.fgd[0]]
        whole = [w.reshape(-1, w.shape[-1]).astype(F32) for w in whole]
        parts = [o.ov[i] for i in range(5)] + [o.ov[8:12].reshape(FF)]
        *mats, v0, v1, v2, v3, v4, up_vec = [
            lax.psum_scatter(w, both, scatter_dimension=0, tiled=True) for w in whole + parts
        ]
        vec = [v0, v1, v2, v3, v4]
        loss = lax.psum(jnp.sum(o.ov[5]), both) / (tokens * D)
    return (
        o.py,
        o.cy,
        loss,
        o.pdx,
        o.cdx,
        vec[0],
        vec[1],
        mats[0],
        mats[1],
        mats[2],
        mats[3],
        vec[2],
        vec[3],
        mats[4],
        up_vec,
        mats[5],
        vec[4],
    )


def solution(mesh):
    rows = P("dp", "cont", None)
    conts = P("dp", "cont", None, None)
    vector = P(("dp", "cont"))
    matrix = P(("dp", "cont"), None)
    return jax.shard_map(
        functools.partial(layer, mesh),
        mesh=mesh,
        in_specs=(rows, conts, rows, conts, conts, P("dp", "cont"), P())
        + (vector, vector, matrix, matrix, matrix, matrix, vector, vector, matrix, vector, matrix, vector),
        out_specs=(rows, conts, P(), rows, conts)
        + (vector, vector, matrix, matrix, matrix, matrix, vector, vector, matrix, vector, matrix, vector),
        check_vma=False,
    )
```

time: 1830 us -> 138 us (0.08)
  waiting for transfers between devices: 797 us -> 0 us
  blocking collectives: 460 us -> 0 us
  local copies, waits for them, and re-layouts: 277 us -> 15.1 us
  matrix products: 146 us -> 0 us
  Pallas kernels: 0 us -> 121 us
  other arithmetic: 119 us -> 0 us
  between operations: 24.6 us -> 1.34 us
    reduce_scatter x6 -> x0, waiting for transfers between devices: 750 us -> none  [local(): lax.psum_scatter(accumulated, ('dp', 'cont'), scatter_dimension=0, tiled=...]
    all_gather x8 -> x0, blocking collectives: 339 us -> none  [the longest x1 75.8 us: local(): lax.all_gather(shards[5], ('dp', 'cont'), axis=0, tiled=True)]
    dot_general x90 -> x0, matrix products: 144 us -> none  [the longest x6 25.8 us: diagonal_terms(): jnp.einsum('hqkab,abkhd->abqhd', expo_scores, value_block, precision=larg...]
    pallas_call x0 -> x1, Pallas kernels: none -> 121 us  [layer(): pl.pallas_call(functools.partial(kernel, s, names), out_shape=[jax.ShapeD...]
    psum x2 -> x0, blocking collectives: 78.1 us -> none  [the longest x1 40.4 us: local(): loss_value = lax.psum(square_sum, ('dp', 'cont')) / scale_all]
    reshape x56 -> x0, local copies, waits for them, and re-layouts: 67.3 us -> none  [the longest x6 12.3 us: one_group(): value_rows.reshape(shaped)]
    reduce_sum x46 -> x0, other arithmetic: 50.1 us -> none  [the longest x16 23.8 us: pair_sum(): row_data.reshape((old_shape[0], old_shape[1] // 2, 2) + old_shape[2:])]
    unnamed x10 -> x0, waiting for transfers between devices: 47 us -> none
  transfers between devices with their start and end apart: 9 -> 0, of which waited for: 7 -> 0; matrix products, arithmetic and copies ran while one was open for 17% -> 0% of each run, Pallas kernels for 0% -> 0%
where the time goes in v1:
time: 138 us; the launch traced here: 137 us
  Pallas kernels  121 us (88%)
  local copies, waits for them, and re-layouts  15.1 us (11%)
    pallas_call x1, Pallas kernels, layer(): pl.pallas_call(functools.partial(kernel, s, names), out_shape=[jax.ShapeD...  121 us
    unnamed x29, local copies, waits for them, and re-layouts  11.3 us

profile of v1, /device:TPU:0, one launch (start us, length us, event | category | flops | bytes accessed | tf_op | source)
XLA Modules:
  0.0 137.3 jit_solution(9947560297613040759)
XLA Ops:
  1.3 0.0 copy-start.8
  1.3 0.6 copy-done.8
  2.0 0.6 copy.36.refs_5_
  2.6 120.9 %layer.1 = (bf16[2,256,512]{2,1,0:T(8,128)(2,1)}, bf16[2,1,128,512]{3,2,1,0:T(8,128)(2,1)}, f32[2,256,512]{2,1,0:T(8,128)}, f32[2,1,128,512]{3,2,1,0:T(8,128)}, ...) custom-call(bf16[2,256,512]{2,1,0:T(8,128)(2,1)} %refs_0_.1, ...), custom_call_target="tpu_custom_call" | custom-call | tf_op jit(solution)/shard_map/layer/pallas_call | solution.py:862
  123.5 0.0 copy-start
  123.5 1.3 slice.21
  124.8 1.2 slice_bitcast_fusion.1
  126.0 1.4 %slice_bitcast_fusion = (f32[16]{0:T(128)}, f32[16]{0:T(128)}, f32[16]{0:T(128)}, f32[16]{0:T(128)}, f32[16]{0:T(128)}) fusion(f32[8,128]{1,0:T(8,128)} %get-tuple-element.30), kind=kLoop, calls=%fused_computation | loop fusion | bytes 640 | tf_op jit(solution)/shard_map/squeeze | solution.py:875
  127.3 1.9 %copy.48 = bf16[2,256,512]{2,1,0:T(8,128)(2,1)} copy(bf16[2,256,512]{2,1,0:T(8,128)(2,1)} %get-tuple-element.61) | data formatting | bytes 1048576
  129.2 1.7 %copy.49 = bf16[2,1,128,512]{3,2,1,0:T(8,128)(2,1)} copy(bf16[2,1,128,512]{3,2,1,0:T(8,128)(2,1)} %get-tuple-element.62) | data formatting | bytes 524288
  130.9 0.0 copy-done
  130.9 0.0 copy-start.1
  130.9 1.0 copy.50
  131.9 0.4 copy-done.1
  132.3 0.0 copy-start.7
  132.3 0.0 copy-start.6
  132.3 0.0 copy-start.5
  132.3 0.8 copy.51
  133.1 0.0 copy-done.7
  133.1 0.0 copy-start.3
  133.1 0.6 copy.52
  133.7 0.0 copy-done.6
  133.7 0.6 copy.53
  134.3 0.0 copy-done.5
  134.3 0.0 copy-start.4
  134.3 0.6 copy.54
  134.9 0.2 copy-done.4
  135.1 0.6 copy.55
  135.7 0.0 copy-done.3
  135.7 0.0 copy-start.2
  135.7 0.7 copy.56
  136.4 0.3 copy-done.2
  136.7 0.7 copy.57
Async XLA Ops:
  1.3 0.7 copy-start.8
  123.5 7.4 %copy-start = (f32[2,256,512]{2,1,0:T(8,128)S(1)}, f32[2,256,512]{2,1,0:T(8,128)}, u32[]{:S(2)}) copy-start(f32[2,256,512]{2,1,0:T(8,128)} %get-tuple-element.64) | copy-start | bytes 3145732
  130.9 1.4 %copy-start.1 = (f32[2,1,128,512]{3,2,1,0:T(8,128)S(1)}, f32[2,1,128,512]{3,2,1,0:T(8,128)}, u32[]{:S(2)}) copy-start(f32[2,1,128,512]{3,2,1,0:T(8,128)} %get-tuple-element.65) | copy-start | bytes 1572868
  132.3 0.8 copy-start.7
  132.3 1.4 %copy-start.6 = (f32[16,512]{1,0:T(8,128)S(1)}, f32[16,512]{1,0:T(8,128)}, u32[]{:S(2)}) copy-start(f32[16,512]{1,0:T(8,128)} %get-tuple-element.69) | copy-start | bytes 98308
  132.3 2.0 %copy-start.5 = (f32[16,512]{1,0:T(8,128)S(1)}, f32[16,512]{1,0:T(8,128)}, u32[]{:S(2)}) copy-start(f32[16,512]{1,0:T(8,128)} %get-tuple-element.70) | copy-start | bytes 98308
  133.1 2.6 %copy-start.3 = (f32[16,2048]{1,0:T(8,128)S(1)}, f32[16,2048]{1,0:T(8,128)}, u32[]{:S(2)}) copy-start(f32[16,2048]{1,0:T(8,128)} %get-tuple-element.74) | copy-start | bytes 393220
  134.3 0.8 copy-start.4
  135.7 1.0 copy-start.2

commit v2 on v1

v2 whole, which is shorter than its diff:
```python
import functools
import types

import jax
import jax.numpy as jnp
from jax import lax
from jax.experimental import pallas as pl
from jax.experimental.pallas import tpu as pltpu
from jax.sharding import PartitionSpec as P

D = 512
HEADS = 8
HEAD_DIM = 64
FF = 2048
BLOCK = 16
CONT_LEN = 128
COARSE = CONT_LEN // BLOCK
PAIRS = HEADS // 2
EPS = 1e-5
SCORE = HEAD_DIM**-0.5
LOG2E = 1.4426950408889634
AWAY = -1e30
F32 = jnp.float32
BF16 = jnp.bfloat16
MESH = pl.DeviceIdType.MESH
LANES = 128
SENDS = 24


def nn(a, b):
    return jnp.dot(a, b, preferred_element_type=F32)


def nt(a, b):
    return lax.dot_general(a, b, (((1,), (1,)), ((), ())), preferred_element_type=F32)


def tn(a, b):
    return lax.dot_general(a, b, (((0,), (0,)), ((), ())), preferred_element_type=F32)


def iota(shape, dim):
    return lax.broadcasted_iota(jnp.int32, shape, dim)


def norm_stats(x):
    center = x - jnp.mean(x, -1, keepdims=True)
    rstd = lax.rsqrt(jnp.mean(center * center, -1, keepdims=True) + EPS)
    return center * rstd, rstd


def norm_back(xhat, rstd, gain, dn):
    dxhat = dn * gain
    mean_one = jnp.mean(dxhat, -1, keepdims=True)
    mean_two = jnp.mean(dxhat * xhat, -1, keepdims=True)
    return rstd * (dxhat - mean_one - xhat * mean_two)


def colsum(x):
    return jnp.sum(x, 0, keepdims=True)


class Sizes:
    def __init__(self, groups, prompt, conts, nz, exchange, ndev):
        self.groups = groups
        self.prompt = prompt
        self.conts = conts
        self.nz = nz
        self.exchange = exchange
        self.ndev = ndev
        self.nb = prompt // CONT_LEN
        self.tb = self.nb + conts
        self.rows_g = self.tb * CONT_LEN
        self.rows = groups * self.rows_g
        self.blocks = groups * self.tb
        self.far_own = prompt // COARSE
        self.far = self.far_own * nz
        self.r = D // ndev
        self.rf = FF // ndev


def kernel(s, names, *refs):
    r = types.SimpleNamespace(**dict(zip(names, refs)))
    z = lax.axis_index("cont")
    dp = lax.axis_index("dp")
    zs = [lax.rem(z + d, s.nz) for d in range(1, s.nz)]
    pending = {}
    sent = [0]

    def remote(src, dst, ssem, rsem, dev):
        return pltpu.make_async_remote_copy(
            src_ref=src, dst_ref=dst, send_sem=ssem, recv_sem=rsem, device_id=dev, device_id_type=MESH
        )

    def send(src, dst, rsem, dev):
        slot = sent[0] % SENDS
        sent[0] += 1
        if slot in pending:
            pending[slot].wait_send()
        copy = remote(src, dst, r.ss.at[slot], rsem, dev)
        copy.start()
        pending[slot] = copy

    def wait_recv(ref, rsem):
        pltpu.make_async_copy(ref, ref, rsem).wait()

    local_count = [0]
    outs = []

    def local(pairs, whole=None):
        sem = r.lsem.at[local_count[0]]
        local_count[0] += 1
        copies = [pltpu.make_async_copy(src, dst, sem) for src, dst in pairs]
        for copy in copies:
            copy.start()
        return copies[0] if whole is None else pltpu.make_async_copy(whole, whole, sem)

    def row_pairs(prompt, cont, rows):
        out = []
        for g in range(s.groups):
            base = g * s.rows_g
            out.append((prompt.at[g], rows.at[pl.ds(base, s.prompt)]))
            for c in range(s.conts):
                out.append((cont.at[g, c], rows.at[pl.ds(base + s.prompt + c * CONT_LEN, CONT_LEN)]))
        return out

    if s.exchange:
        core = lax.rem(dp, 2)
        ix = lax.rem(dp // 2, 2)
        iy = dp // 4
        sib = dp + 1 - 2 * core
        xn = dp + 2 - 4 * ix
        yn = dp + 4 - 8 * iy
        cell = dp // 2
        cell_x = cell + 1 - 2 * ix
        cell_y = cell + 2 - 4 * iy
        cell_d = cell_x + cell_y - cell
        sibcore = 1 - core
        me = dp * s.nz + z

        def view(k, a, n, part=None):
            if k == 0:
                return r.tiles.at[pl.ds(a, n)]
            ref, rows = [(r.w4, s.r), (r.w4, s.r), (r.wu, s.r), (r.wd, s.rf)][k - 1]
            place = pl.ds(pl.multiple_of(a * rows, rows), n * rows)
            width = ref.shape[-1]
            cols = pl.ds(0, width) if part is None else pl.ds(part * (width // 2), width // 2)
            if k == 1:
                return ref.at[pl.ds(0, 3), place, cols]
            if k == 2:
                return ref.at[3, place, cols]
            return ref.at[place, cols]

        def shard(c, co, zz):
            return (c * 2 + co) * s.nz + zz

        def ag_move(k, kind, a, n, dev, part=None):
            v = view(k, a, n, part)
            send(v, v, r.agr.at[k, kind], dev)

        def ag_got(k, kind, n, part=None):
            wait_recv(view(k, 0, n, part), r.agr.at[k, kind])

        def ag_z(k):
            for zz in zs:
                ag_move(k, 0, me, 1, (dp, zz))

        def ag_out(k, wave, starts, n):
            if wave == 1 or n > 1:
                ag_got(k, 0, s.nz - 1)
            for zz in starts:
                a = shard(cell, core, zz)
                ag_move(k, 1 + wave, a, n, (xn, z))
                ag_move(k, 3 + wave, a, n, (yn, z))
            for zz in starts:
                ag_move(k, 9, shard(cell, core, zz), n, (sib, z))

        def ag_pass(k, wave, starts, n):
            total = len(starts) * n
            ag_got(k, 1 + wave, total)
            for zz in starts:
                ag_move(k, 5 + wave, shard(cell_x, core, zz), n, (yn, z), 0)
            ag_got(k, 3 + wave, total)
            if k > 0:
                for zz in starts:
                    ag_move(k, 7 + wave, shard(cell_y, core, zz), n, (xn, z), 1)
            for zz in starts:
                ag_move(k, 9, shard(cell_x, core, zz), n, (sib, z))
                ag_move(k, 9, shard(cell_y, core, zz), n, (sib, z))

        def ag_last(k, wave, starts, n):
            total = len(starts) * n
            ag_got(k, 5 + wave, total, 0)
            if k > 0:
                ag_got(k, 7 + wave, total, 1)
            for zz in starts:
                ag_move(k, 9, shard(cell_d, core, zz), n, (sib, z))

        def ag1(k):
            ag_out(k, 0, [0], s.nz)

        def ag2(k):
            ag_pass(k, 0, [0], s.nz)

        def ag3(k):
            ag_last(k, 0, [0], s.nz)

        def ag4(k):
            ag_got(k, 9, 4 * s.nz)

        grads = [(r.gd.at[...], r.rcd, r.rdd, r.rxd, r.rzd), (r.gu.at[...], r.rcu, r.rdu, r.rxu, r.rzu),
                 (r.go.at[...], r.rco, r.rdo, r.rxo, r.rzo)]
        for p in range(PAIRS):
            grads.append((r.gq.at[p], r.rcq.at[p], r.rdq.at[p], r.rxq.at[p], r.rzq.at[p]))

        def rs0(k):
            g, rc, _, _, _ = grads[k]
            send(g.at[:, sibcore], rc, r.rsr.at[k, 0], (sib, z))

        def add_to(g, c, lo, n, term):
            place = (c, core, pl.ds(lo, n))
            g[place] = (g[place].astype(F32) + term).astype(BF16)

        def rs1(k):
            g, rc, rd, _, _ = grads[k]
            m = g.shape[2]
            wait_recv(rc, r.rsr.at[k, 0])
            add_to(g, cell_d, 0, m, rc[cell_d].astype(F32))
            mh = m // 2
            send(g.at[cell_d, core, pl.ds(0, mh)], rd.at[0], r.rsr.at[k, 1], (yn, z))
            send(g.at[cell_d, core, pl.ds(mh, mh)], rd.at[1], r.rsr.at[k, 2], (xn, z))
            for c in (cell_x, cell_y, cell):
                add_to(g, c, 0, m, rc[c].astype(F32))

        def rs2(k):
            g, _, rd, rx, _ = grads[k]
            mh = g.shape[2] // 2
            wait_recv(rd.at[0], r.rsr.at[k, 1])
            add_to(g, cell_x, 0, mh, rd[0].astype(F32))
            send(g.at[cell_x, core], rx.at[0], r.rsr.at[k, 3], (xn, z))
            wait_recv(rd.at[1], r.rsr.at[k, 2])
            add_to(g, cell_y, mh, mh, rd[1].astype(F32))
            send(g.at[cell_y, core], rx.at[1], r.rsr.at[k, 3], (yn, z))

        def piece(g, zz):
            n = g.shape[2] // s.nz
            return pl.ds(pl.multiple_of(zz * n, n), n)

        def rs3(k):
            g, _, _, rx, rz = grads[k]
            wait_recv(rx, r.rsr.at[k, 3])
            add_to(g, cell, 0, g.shape[2], rx[0].astype(F32) + rx[1].astype(F32))
            for d, zz in enumerate(zs):
                send(g.at[cell, core, piece(g, zz)], rz.at[d], r.rsr.at[k, 4], (dp, zz))

        def rs4(k):
            g, _, _, _, rz = grads[k]
            wait_recv(rz, r.rsr.at[k, 4])
            total = g[cell, core, piece(g, z)].astype(F32)
            for d in range(s.nz - 1):
                total = total + rz[d].astype(F32)
            if k < 3:
                held, out = ((r.hgd, r.ogd), (r.hgu, r.ogu), (r.hgo, r.ogo))[k]
                held[...] = total
                outs.append(local([(held, out)]))
            else:
                lanes = pl.ds((k - 3) * LANES, LANES)
                for j, (held, out) in enumerate(((r.hgq, r.ogq), (r.hgk, r.ogk), (r.hgv, r.ogv))):
                    held[:, lanes] = total[:, j * LANES : (j + 1) * LANES]
                    if k == 2 + PAIRS:
                        outs.append(local([(held, out)]))
    else:

        def nothing(*_):
            return None

        ag1 = ag2 = ag3 = ag4 = ag_z = ag_out = ag_pass = ag_last = nothing
        rs0 = rs1 = rs2 = rs3 = rs4 = nothing

    scalars_in = [local([(r.lens_in, r.lens)]), local([(r.ls_in, r.ls)])]
    if s.exchange:
        vectors_in = (r.v1g, r.v1b, r.v2g, r.v2b, r.vdb)
        scalars_in.append(local([(v, r.small.at[i]) for i, v in enumerate(vectors_in)], r.small))
        scalars_in.append(local([(r.vub, r.smallup)]))
        own_rows = pl.ds(pl.multiple_of(me * s.r, s.r), s.r)
        weights_in = [
            local([(w, r.w4.at[j, own_rows]) for j, w in enumerate((r.wq, r.wk, r.wv, r.wo))], r.w4.at[:, own_rows]),
            local([(r.wup, view(3, me, 1))]),
            local([(r.wdn, view(4, me, 1))]),
        ]
    else:
        weights_in = [local([(w, r.w4.at[j]) for j, w in enumerate((r.wq, r.wk, r.wv, r.wo))], r.w4)]
        weights_in += [local([(r.wup, r.wu)]), local([(r.wdn, r.wd)])]
    barrier = pltpu.get_barrier_semaphore()
    partners = [(dp, zz) for zz in zs]
    if s.exchange:
        partners += [(sib, z), (xn, z), (yn, z)]
    for dev in partners:
        pl.semaphore_signal(barrier, inc=1, device_id=dev, device_id_type=MESH)
    x_in = [local(row_pairs(r.px, r.cx, r.x), r.x)]
    teach_pairs = [(r.te.at[g, c], r.teach.at[g * s.conts + c]) for g in range(s.groups) for c in range(s.conts)]
    later_in = [local(row_pairs(r.pdy, r.cdy, r.dy), r.dy), local(teach_pairs, r.teach)]

    for copy in scalars_in:
        copy.wait()
    if s.exchange:
        r.build[...] = jnp.zeros_like(r.build)
        for i in range(5):
            r.build[pl.ds(i, 1), pl.ds(0, s.r)] = r.small[i].astype(F32)
        r.build[pl.ds(5, 1), pl.ds(0, s.rf)] = r.smallup[...].astype(F32)
        own_tokens = 0
        for g in range(s.groups):
            for c in range(s.conts):
                own_tokens = own_tokens + r.lens[c, g]
        tile = r.build[...]
        row = iota((8, LANES), 0)
        placed = jnp.where(
            row < 5,
            pltpu.roll(tile, lax.rem(me, LANES // s.r) * s.r, 1),
            pltpu.roll(tile, lax.rem(me, LANES // s.rf) * s.rf, 1),
        )
        r.tiles[me] = jnp.where(row == 6, own_tokens.astype(F32), placed)

    for copy in weights_in:
        copy.wait()
    pl.semaphore_wait(barrier, len(partners))
    first, rest = [z], zs
    ag_z(0)
    ag_z(1)
    ag_out(1, 0, first, 1)

    lane_lo = iota((CONT_LEN, LANES), 1) < HEAD_DIM
    lane_lo48 = iota((48, LANES), 1) < HEAD_DIM
    ri = iota((64, CONT_LEN), 0)
    ci = iota((64, CONT_LEN), 1)
    coarse_ci = jnp.where(ri < 32, ci >> 1, jnp.where(ri < 48, ci >> 2, ci >> 3))
    position = jnp.where(ri < 16, ri, jnp.where(ri < 32, ri + 16, jnp.where(ri < 48, ri - 32, ri - 48)))
    r.poolk[...] = jnp.where(coarse_ci == position, 1.0, 0.0).astype(BF16)
    position = jnp.where(ri < 48, position + 16, position)
    r.poolq[...] = jnp.where(coarse_ci == position, 1.0, 0.0).astype(BF16)
    ri = iota((CONT_LEN, 96), 0)
    ci = lax.rem(iota((CONT_LEN, 96), 1), 48)
    coarse_ri = jnp.where(ci < 32, ri >> 1, ri >> 2)
    position = jnp.where(ci < 16, ci + 16, jnp.where(ci < 32, ci + 32, ci - 16))
    r.widen[...] = jnp.where(coarse_ri == position, 1.0, 0.0).astype(BF16)
    ri = iota((CONT_LEN, CONT_LEN), 0)
    ci = iota((CONT_LEN, CONT_LEN), 1)
    bi, bj = ri >> 4, ci >> 4
    near = ((bi == bj) & (ci <= ri)) | (((bi & 1) == 1) & (bj == bi - 1))
    near = jnp.where(near, 0.0, AWAY)
    r.bias0[pl.ds(0, CONT_LEN)] = near
    r.bias0[pl.ds(CONT_LEN, CONT_LEN)] = near
    ri = lax.rem(iota((96, 48), 0), 48)
    r.bias1[...] = jnp.where((ri >> 4) == (iota((96, 48), 1) >> 4), 0.0, AWAY)
    nq = s.tb * BLOCK
    blk = lax.rem(iota((2 * nq, s.far), 0), nq) >> 4
    limit = jnp.where(blk >= s.nb, s.far, BLOCK * (z * s.nb + blk))
    r.biasf[...] = jnp.where(iota((2 * nq, s.far), 1) < limit, 0.0, AWAY)
    scale_rows = iota((64, D), 0)
    mean_scale = jnp.where(scale_rows < 32, 0.5, jnp.where(scale_rows < 48, 0.25, 0.125))
    r.vg[...] = jnp.zeros_like(r.vg)

    ag_pass(1, 0, first, 1)
    ag1(0)
    ag_out(1, 1, rest, 1)
    ag_z(2)
    ag_z(3)
    ag_last(1, 0, first, 1)
    ag2(0)
    ag_pass(1, 1, rest, 1)
    ag1(2)
    ag3(0)
    ag4(0)
    if s.exchange:
        count = 8
        for k in range(s.ndev // count):
            part = jnp.sum(r.tiles[pl.ds(k * count, count)], 0)
            r.vec[:, pl.ds(k * LANES, LANES)] = part
        for k in range(s.ndev // 2):
            part = r.tiles[2 * k] + r.tiles[2 * k + 1]
            r.upb[:, pl.ds(k * LANES, LANES)] = part[5:6]
    else:
        r.vec[...] = r.vecs[...]
        r.upb[...] = r.upbs[...]

    def vec(i):
        return r.vec[pl.ds(i, 1), :]

    token_row = r.vec[pl.ds(6, 1), pl.ds(0, LANES)]
    for k in range(1, D // LANES):
        token_row = token_row + r.vec[pl.ds(6, 1), pl.ds(k * LANES, LANES)]
    token_row = jnp.concatenate([token_row] * (D // LANES), 1)

    def length_of(g, b):
        if isinstance(b, int):
            return CONT_LEN if b < s.nb else r.lens[b - s.nb, g]
        c = jnp.clip(b - s.nb, 0, s.conts - 1)
        return jnp.where(b >= s.nb, r.lens[c, g], CONT_LEN)

    def block_rows(t):
        if isinstance(t, int):
            return pl.ds(t * CONT_LEN, CONT_LEN)
        return pl.ds(pl.multiple_of(t * CONT_LEN, CONT_LEN), CONT_LEN)

    for copy in x_in:
        copy.wait()

    def norm_one(i, carry):
        rows = block_rows(i)
        xhat, _ = norm_stats(r.x[rows].astype(F32))
        r.n1[rows] = (xhat * vec(0) + vec(1)).astype(BF16)
        return carry

    lax.fori_loop(0, s.blocks, norm_one, 0)
    ag_z(4)
    ag1(3)
    ag_last(1, 1, rest, 1)
    ag4(1)

    def project(t, carry):
        g, b = t // s.tb, lax.rem(t, s.tb)
        rows = block_rows(t)
        n1 = r.n1[rows]
        keep = iota((CONT_LEN, D), 0) < length_of(g, b)
        qv = nn(n1, r.w4[0]).astype(BF16)
        kv = jnp.where(keep, nn(n1, r.w4[1]), 0.0).astype(BF16)
        vv = jnp.where(keep, nn(n1, r.w4[2]), 0.0).astype(BF16)
        r.q[rows] = qv
        r.k[rows] = kv
        r.v[rows] = vv
        r.ql[t] = (nn(r.poolq[...], qv) * mean_scale).astype(BF16)
        r.kl[t] = (nn(r.poolk[...], kv) * mean_scale).astype(BF16)
        r.vl[t] = nn(r.poolk[...], vv).astype(BF16)
        return carry

    lax.fori_loop(0, s.blocks, project, 0)
    for g in range(s.groups):
        for b in range(s.nb):
            place = pl.ds(pl.multiple_of(z * s.far_own + b * BLOCK, BLOCK), BLOCK)
            r.fkv[0, g, place] = r.kl[g * s.tb + b, pl.ds(48, BLOCK)]
            r.fkv[1, g, place] = r.vl[g * s.tb + b, pl.ds(48, BLOCK)]

    def far_rows(zz):
        return r.fkv.at[:, :, pl.ds(pl.multiple_of(zz * s.far_own, s.far_own), s.far_own)]

    for zz in zs:
        send(far_rows(z), far_rows(z), r.fr.at[0], (dp, zz))
    ag2(2)
    ag2(3)
    ag1(4)

    def two(a):
        low = lane_lo if a.shape[0] == CONT_LEN else lane_lo48
        zero = jnp.zeros_like(a)
        return jnp.concatenate([jnp.where(low, a, zero), jnp.where(low, zero, a)], 0)

    def pick(a):
        n = a.shape[0] // 2
        return jnp.where(lane_lo if n == CONT_LEN else lane_lo48, a[:n], a[n:])

    def counts(length):
        i0 = iota((CONT_LEN, LANES), 0)
        counts0 = jnp.where(i0 < length, 1.0, 0.0).astype(BF16)
        i1 = iota((48, LANES), 0)
        first = jnp.where(i1 < 16, 2 * i1, jnp.where(i1 < 32, 2 * (i1 + 16), 4 * (i1 - 32)))
        width = jnp.where(i1 < 32, 2, 4)
        counts1 = jnp.clip(length - first, 0, width).astype(F32).astype(BF16)
        return counts0, counts1

    def pair_lanes(p):
        return pl.ds(p * LANES, LANES)

    low48 = pl.ds(0, 48)
    far16 = pl.ds(48, BLOCK)

    def near(t, carry):
        g, b = t // s.tb, lax.rem(t, s.tb)
        rows = block_rows(t)
        counts0, counts1 = counts(length_of(g, b))
        for p in range(PAIRS):
            lanes = pair_lanes(p)
            e0 = jnp.exp2(nt(two(r.q[rows, lanes]), r.k[rows, lanes]) * (SCORE * LOG2E) + r.bias0[...])
            e0 = e0.astype(BF16)
            e1 = jnp.exp2(
                nt(two(r.ql[t, low48, lanes]), r.kl[t, low48, lanes]) * (SCORE * LOG2E) + r.bias1[...]
            ).astype(BF16)
            r.e0[t * PAIRS + p] = e0
            r.e1[t * PAIRS + p] = e1
            t0 = nn(e0, jnp.concatenate([r.v[rows, lanes], counts0], 1))
            t1 = nn(e1, jnp.concatenate([r.vl[t, low48, lanes], counts1], 1))
            t1 = jnp.concatenate([pick(t1[:, :LANES]), pick(t1[:, LANES:])], 1)
            high = t1.astype(BF16)
            t1 = nn(r.widen[...], jnp.concatenate([high, (t1 - high.astype(F32)).astype(BF16)], 0))
            r.num[rows, lanes] = pick(t0[:, :LANES]) + t1[:, :LANES]
            r.den[rows, lanes] = pick(t0[:, LANES:]) + t1[:, LANES:]
        return carry

    eight = jnp.full((s.far, LANES), float(COARSE), BF16)

    def gathered(ref, g, lanes):
        return jnp.concatenate([ref[g * s.tb + b, far16, lanes] for b in range(s.tb)], 0)

    def repeat_rows(a):
        n = a.shape[0]
        return jnp.broadcast_to(a[:, None, :], (n, COARSE, LANES)).reshape(n * COARSE, LANES)

    def far_forward(g):
        rows = pl.ds(g * s.rows_g, s.rows_g)
        for p in range(PAIRS):
            lanes = pair_lanes(p)
            ef = nt(two(gathered(r.ql, g, lanes)), r.fkv[0, g, :, lanes]) * (SCORE * LOG2E) + r.biasf[...]
            ef = jnp.exp2(ef).astype(BF16)
            r.ef[g, p] = ef
            total = nn(ef, jnp.concatenate([r.fkv[1, g, :, lanes], eight], 1))
            denominator = r.den[rows, lanes] + repeat_rows(pick(total[:, LANES:]))
            numerator = r.num[rows, lanes] + repeat_rows(pick(total[:, :LANES]))
            r.den[rows, lanes] = denominator
            r.att[rows, lanes] = (numerator / denominator).astype(BF16)

    lax.fori_loop(0, s.tb, near, 0)
    ag3(2)
    ag3(3)
    ag2(4)
    lax.fori_loop(s.tb, s.blocks, near, 0)
    wait_recv(r.fkv.at[:, :, pl.ds(0, s.far - s.far_own)], r.fr.at[0])
    for g in range(s.groups):
        far_forward(g)
    ag4(2)
    ag3(4)

    for copy in later_in:
        copy.wait()
    for g in range(s.groups):
        rows = pl.ds(g * s.rows_g, s.rows_g)
        mixed = r.x[rows].astype(F32) + nn(r.att[rows], r.w4[3])
        r.mix[rows] = mixed
        xhat, _ = norm_stats(mixed)
        r.n2[rows] = (xhat * vec(2) + vec(3)).astype(BF16)
    ag4(3)
    for g in range(s.groups):
        rows = pl.ds(g * s.rows_g, s.rows_g)
        for n in range(FF // D):
            cols = pl.ds(n * D, D)
            pre = nn(r.n2[rows], r.wu[:, cols]) + r.upb[:, cols]
            r.h[rows, cols] = jnp.maximum(pre, 0.0).astype(BF16)
    ag4(4)
    extra = 2.0 * r.ls[0, 0] / (token_row * float(D))
    for g in range(s.groups):
        base = g * s.rows_g
        rows = pl.ds(base, s.rows_g)
        y = r.mix[rows] + nn(r.h[rows], r.wd[...]) + vec(4)
        r.y[rows] = y.astype(BF16)
        gy = r.dy[rows].astype(F32)
        parts = [gy[: s.prompt]]
        for c in range(s.conts):
            lo = s.prompt + c * CONT_LEN
            keep = iota((CONT_LEN, D), 0) < r.lens[c, g]
            diff = jnp.where(keep, y[lo : lo + CONT_LEN] - r.teach[g * s.conts + c].astype(F32), 0.0)
            r.vg[pl.ds(5, 1), :] += colsum(diff * diff)
            parts.append(gy[lo : lo + CONT_LEN] + extra * diff)
        gy = jnp.concatenate(parts, 0)
        r.gy[rows] = gy
        r.gyb[rows] = gy.astype(BF16)
        r.vg[pl.ds(4, 1), :] += colsum(gy)

    outs.append(local([(b, a) for a, b in row_pairs(r.py, r.cy, r.y)], r.y))

    for n in range(FF // D):
        cols = pl.ds(n * D, D)
        r.gd[n] = tn(r.h[:, cols], r.gyb[...]).astype(BF16).reshape(2, FF // 8, D)
    rs0(0)
    for n in range(FF // D):
        cols = pl.ds(n * D, D)
        for g in range(s.groups):
            rows = pl.ds(g * s.rows_g, s.rows_g)
            dh = nt(r.gyb[rows], r.wd[cols])
            dpre = jnp.where(r.h[rows, cols] > 0, dh, 0.0).astype(BF16)
            r.h[rows, cols] = dpre
            r.vg[pl.ds(8 + n, 1), :] += colsum(dpre.astype(F32))
        if n == 1:
            rs1(0)
    for g in range(s.groups):
        rows = pl.ds(g * s.rows_g, s.rows_g)
        dn2 = nt(r.h[rows], r.wu[...])
        xhat, rstd = norm_stats(r.mix[rows])
        r.vg[pl.ds(2, 1), :] += colsum(dn2 * xhat)
        r.vg[pl.ds(3, 1), :] += colsum(dn2)
        dmixed = r.gy[rows] + norm_back(xhat, rstd, vec(2), dn2)
        r.gy[rows] = dmixed
        r.gyb[rows] = dmixed.astype(BF16)
    rs2(0)
    for g in range(s.groups):
        rows = pl.ds(g * s.rows_g, s.rows_g)
        dnum = nt(r.gyb[rows], r.w4[3]) / r.den[rows]
        r.dnum[rows] = dnum.astype(BF16)
        r.xo[rows] = (-dnum * r.att[rows].astype(F32)).astype(BF16)
        for b in range(s.tb):
            t = g * s.tb + b
            for ref, fine in ((r.dnl, r.dnum), (r.xol, r.xo)):
                pooled = nn(r.poolq[...], fine[block_rows(t)])
                high = pooled.astype(BF16)
                ref[0, t] = high
                ref[1, t] = (pooled - high.astype(F32)).astype(BF16)

    for g in range(s.groups):
        for p in range(PAIRS):
            lanes = pair_lanes(p)
            d3, x3, d3_low, x3_low = [two(gathered(ref.at[i], g, lanes)) for i in range(2) for ref in (r.dnl, r.xol)]
            x = jnp.concatenate([d3, x3, d3_low, x3_low], 1)
            vn = jnp.concatenate([r.fkv[1, g, :, lanes], eight], 1)
            ef = r.ef[g, p]
            kf = r.fkv[0, g, :, lanes]
            ds = nt(x, jnp.concatenate([vn, vn], 1)) * ef.astype(F32)
            ds = ds.astype(BF16)
            dq3 = (pick(nn(ds, kf)) * 0.125).astype(BF16)
            for b in range(s.tb):
                r.dql[g * s.tb + b, :, lanes] = dq3[b * BLOCK : (b + 1) * BLOCK]
            dkf = tn(ds, two(gathered(r.ql, g, lanes)))
            dvf = tn(ef, d3)
            r.df[g, 0, :, lanes] = dkf
            r.df[g, 1, :, lanes] = dvf
            r.dfs[g, 0, :, lanes] = dkf.astype(BF16)
            r.dfs[g, 1, :, lanes] = dvf.astype(BF16)

    def far_part(zz):
        return r.dfs.at[:, :, pl.ds(pl.multiple_of(zz * s.far_own, s.far_own), s.far_own)]

    for d, zz in enumerate(zs):
        send(far_part(zz), r.rf.at[d], r.fr.at[1], (dp, zz))
    for n in range(FF // D):
        cols = pl.ds(n * D, D)
        r.gu[:, :, :, cols] = tn(r.n2[...], r.h[:, cols]).astype(BF16).reshape(4, 2, D // 8, D)
    rs0(1)
    rs3(0)
    r.go[...] = tn(r.att[...], r.gyb[...]).astype(BF16).reshape(4, 2, D // 8, D)
    rs0(2)
    rs1(1)

    def near_back(t, g, b, p):
        lanes = pair_lanes(p)
        rows = block_rows(t)
        length = length_of(g, b)
        counts0, counts1 = counts(length)
        q2 = two(r.q[rows, lanes])
        ql2 = two(r.ql[t, low48, lanes])
        k0 = r.k[rows, lanes]
        kl = r.kl[t, low48, lanes]
        e0 = r.e0[t * PAIRS + p]
        e1 = r.e1[t * PAIRS + p]
        dn2 = two(r.dnum[rows, lanes])
        dnl2 = two(r.dnl[0, t, low48, lanes])
        x0 = jnp.concatenate([dn2, two(r.xo[rows, lanes])], 1)
        x1 = [dnl2, two(r.xol[0, t, low48, lanes]), two(r.dnl[1, t, low48, lanes]), two(r.xol[1, t, low48, lanes])]
        x1 = jnp.concatenate(x1, 1)
        vn1 = jnp.concatenate([r.vl[t, low48, lanes], counts1], 1)
        ds0 = nt(x0, jnp.concatenate([r.v[rows, lanes], counts0], 1)) * e0.astype(F32)
        ds1 = nt(x1, jnp.concatenate([vn1, vn1], 1)) * e1.astype(F32)
        ds0 = ds0.astype(BF16)
        ds1 = ds1.astype(BF16)
        lr = iota((48, LANES), 0)
        level_scale = jnp.where(lr < 32, 0.5, 0.25)
        dql = (pick(nn(ds1, kl)) * level_scale).astype(BF16)
        dql = jnp.concatenate([dql, r.dql[t, :, lanes]], 0)
        dq = pick(nn(ds0, k0)) + tn(r.poolq[...], dql)
        dk0 = tn(ds0, q2)
        dv0 = tn(e0, dn2)
        dkl = (tn(ds1, ql2) * level_scale).astype(BF16)
        dvl = tn(e1, dnl2).astype(BF16)
        coarse = jnp.concatenate([dkl, dvl], 1)
        if b < s.nb:
            own = pl.ds(b * BLOCK, BLOCK)
            coarse = jnp.concatenate(
                [coarse, jnp.concatenate([r.ft[g, 0, own, lanes], r.ft[g, 1, own, lanes]], 1)], 0
            )
            fine = tn(r.poolk[...], coarse)
        else:
            fine = tn(r.poolk[low48], coarse)
        dk = dk0 + fine[:, :LANES]
        dv = dv0 + fine[:, LANES:]
        if b >= s.nb:
            keep = iota((CONT_LEN, LANES), 0) < length
            dk = jnp.where(keep, dk, 0.0)
            dv = jnp.where(keep, dv, 0.0)
        r.dqkv[p, rows, pl.ds(0, LANES)] = (dq * SCORE).astype(BF16)
        r.dqkv[p, rows, pl.ds(LANES, LANES)] = (dk * SCORE).astype(BF16)
        r.dqkv[p, rows, pl.ds(2 * LANES, LANES)] = dv.astype(BF16)

    def conts_back(g, carry):
        for b in range(s.nb, s.tb):
            for p in range(PAIRS):
                near_back(g * s.tb + b, g, b, p)
        return carry

    lax.fori_loop(0, s.groups, conts_back, 0)
    rs2(1)
    rs1(2)
    wait_recv(r.rf, r.fr.at[1])
    own = pl.ds(pl.multiple_of(z * s.far_own, s.far_own), s.far_own)
    for g in range(s.groups):
        for i, scale in enumerate((1.0 / COARSE, 1.0)):
            total = r.df[g, i, own]
            for d in range(s.nz - 1):
                total = total + r.rf[d, g, i].astype(F32)
            r.ft[g, i] = (total * scale).astype(BF16)
    rs4(0)
    rs2(2)

    def prompts_back(p):
        def body(g, carry):
            for b in range(s.nb):
                near_back(g * s.tb + b, g, b, p)
            return carry

        lax.fori_loop(0, s.groups, body, 0)
        r.gq[p] = tn(r.n1[...], r.dqkv[p]).astype(BF16).reshape(4, 2, D // 8, 3 * LANES)

    prompts_back(0)
    rs0(3)
    rs3(1)
    rs3(2)
    prompts_back(1)
    rs0(4)
    rs1(3)
    prompts_back(2)
    rs0(5)
    rs2(3)
    rs1(4)
    rs4(1)
    prompts_back(3)
    rs0(6)
    rs3(3)
    rs2(4)
    rs1(5)

    for g in range(s.groups):
        rows = pl.ds(g * s.rows_g, s.rows_g)
        dn1 = 0.0
        for j in range(3):
            d = jnp.concatenate([r.dqkv[p, rows, pl.ds(j * LANES, LANES)] for p in range(PAIRS)], 1)
            dn1 = dn1 + nt(d, r.w4[j])
        xhat, rstd = norm_stats(r.x[rows].astype(F32))
        r.vg[pl.ds(0, 1), :] += colsum(dn1 * xhat)
        r.vg[pl.ds(1, 1), :] += colsum(dn1)
        r.gy[rows] = r.gy[rows] + norm_back(xhat, rstd, vec(0), dn1)
        if g == 0:
            rs1(6)
            rs2(5)
            rs3(4)

    outs.append(local([(b, a) for a, b in row_pairs(r.pdx, r.cdx, r.gy)], r.gy))
    if s.exchange:

        def vsend(src, i, dev):
            send(src, r.rv.at[i], r.vr.at[i], dev)

        vsend(r.vg, 0, (sib, z))
        rs2(6)
        rs3(5)
        wait_recv(r.rv.at[0], r.vr.at[0])
        r.vt[0] = r.vg[...] + r.rv[0]
        vsend(r.vt.at[0], 1, (xn, z))
        rs4(2)
        rs4(3)
        rs3(6)
        wait_recv(r.rv.at[1], r.vr.at[1])
        r.vt[1] = r.vt[0] + r.rv[1]
        vsend(r.vt.at[1], 2, (yn, z))
        rs4(4)
        wait_recv(r.rv.at[2], r.vr.at[2])
        r.vt[2] = r.vt[1] + r.rv[2]
        for zz in zs:
            send(r.vt.at[2], r.rv.at[3 + z], r.vr.at[3], (dp, zz))
        rs4(5)
        rs4(6)
        wait_recv(r.rv.at[pl.ds(3, s.nz - 1)], r.vr.at[3])
        r.rv[3 + z] = r.vt[2]
        total = r.rv[3]
        for i in range(1, s.nz):
            total = total + r.rv[3 + i]
        loss = jnp.sum(total[5:6], 1, keepdims=True) / (token_row[:, :1] * float(D))
        mine = jnp.zeros((8, LANES), F32)
        per = LANES // s.r
        for k in range(D // LANES):
            mine = jnp.where(me // per == k, total[:8, k * LANES : (k + 1) * LANES], mine)
        mine = pltpu.roll(mine, lax.rem(LANES - lax.rem(me, per) * s.r, LANES), 1)
        per = LANES // s.rf
        up = jnp.zeros((1, LANES), F32)
        for k in range(FF // LANES):
            i, j = divmod(k, D // LANES)
            up = jnp.where(me // per == k, total[8 + i : 9 + i, j * LANES : (j + 1) * LANES], up)
        up = jnp.broadcast_to(up, (8, LANES))
        up = pltpu.roll(up, lax.rem(LANES - lax.rem(me, per) * s.rf, LANES), 1)
        row = iota((8, LANES), 0)
        r.hv[...] = jnp.where(row < 5, mine, jnp.where(row == 5, loss, up))
        outs.append(local([(r.hv, r.ov)]))
    else:
        r.ov[...] = r.vg[...]
        for src, dst in ((r.gq, r.fgq), (r.go, r.fgo), (r.gu, r.fgu), (r.gd, r.fgd)):
            outs.append(local([(src, dst)]))
    for copy in outs:
        copy.wait()
    for copy in pending.values():
        copy.wait_send()


def finish(n_mats, *refs):
    ov = refs[0]
    srcs = refs[1 : 1 + n_mats]
    dsts = refs[1 + n_mats : 1 + 2 * n_mats]
    vectors = refs[1 + 2 * n_mats : -1 - n_mats]
    held = refs[-1 - n_mats : -1]
    sems = refs[-1]
    reads = [pltpu.make_async_copy(a, b, sems.at[0, i]) for i, (a, b) in enumerate(zip(srcs, held))]
    writes = [pltpu.make_async_copy(a, b, sems.at[1, i]) for i, (a, b) in enumerate(zip(held, dsts))]
    for copy in reads:
        copy.start()
    for i, out in enumerate(vectors):
        out[...] = ov[pl.ds(i, 1), pl.ds(0, out.shape[1])]
    for read, write in zip(reads, writes):
        read.wait()
        write.start()
    for copy in writes:
        copy.wait()


def layer(
    mesh,
    prompt_x,
    cont_x,
    prompt_dy,
    cont_dy,
    teacher,
    cont_lengths,
    loss_scale,
    norm1_gain,
    norm1_bias,
    w_query,
    w_key,
    w_value,
    w_out,
    norm2_gain,
    norm2_bias,
    w_up,
    up_bias,
    w_down,
    down_bias,
):
    nz, ndp = mesh.shape["cont"], mesh.shape["dp"]
    ndev = nz * ndp
    exchange = ndp == 8 and nz == 4
    groups, prompt = prompt_x.shape[:2]
    conts = cont_x.shape[1]
    s = Sizes(groups, prompt, conts, nz, exchange, ndev)
    both = ("dp", "cont")
    any_spec = pl.BlockSpec(memory_space=pl.ANY)
    vmem = pl.BlockSpec(memory_space=pltpu.VMEM)

    inputs = {
        "px": (prompt_x, any_spec),
        "cx": (cont_x, any_spec),
        "pdy": (prompt_dy, any_spec),
        "cdy": (cont_dy, any_spec),
        "te": (teacher, any_spec),
        "lens_in": (cont_lengths.T, any_spec),
        "ls_in": (loss_scale.reshape(1, 1), any_spec),
    }
    weights = {"wq": w_query, "wk": w_key, "wv": w_value, "wo": w_out, "wup": w_up, "wdn": w_down}
    vectors = {"v1g": norm1_gain, "v1b": norm1_bias, "v2g": norm2_gain, "v2b": norm2_bias, "vdb": down_bias}
    if exchange:
        for name, w in weights.items():
            inputs[name] = (w, any_spec)
        for name, v in vectors.items():
            inputs[name] = (v.reshape(1, -1), any_spec)
        inputs["vub"] = (up_bias.reshape(1, -1), any_spec)
    else:
        for name, w in weights.items():
            inputs[name] = (lax.all_gather(w, both, axis=0, tiled=True), any_spec)
        tokens = lax.psum(jnp.sum(cont_lengths).astype(F32), both)
        full = [lax.all_gather(v, both, axis=0, tiled=True).astype(F32) for v in vectors.values()]
        zero = jnp.zeros((D,), F32)
        inputs["vecs"] = (jnp.stack(full + [zero, jnp.full((D,), tokens / (D // LANES)), zero]), vmem)
        up_full = lax.all_gather(up_bias, both, axis=0, tiled=True).astype(F32)
        inputs["upbs"] = (up_full.reshape(1, FF), vmem)

    m, mf = D // 8, FF // 8
    outputs = {
        "py": (prompt_x.shape, BF16, any_spec),
        "cy": (cont_x.shape, BF16, any_spec),
        "pdx": (prompt_x.shape, F32, any_spec),
        "cdx": (cont_x.shape, F32, any_spec),
    }
    if exchange:
        for name in ("ogq", "ogk", "ogv", "ogo"):
            outputs[name] = ((s.r, D), F32, any_spec)
        outputs["ogu"] = ((s.r, FF), F32, any_spec)
        outputs["ogd"] = ((s.rf, D), F32, any_spec)
        outputs["ov"] = ((8, LANES), F32, any_spec)
    else:
        outputs["fgq"] = ((PAIRS, 4, 2, m, 3 * LANES), BF16, any_spec)
        outputs["fgo"] = ((4, 2, m, D), BF16, any_spec)
        outputs["fgu"] = ((4, 2, m, FF), BF16, any_spec)
        outputs["fgd"] = ((4, 2, mf, D), BF16, any_spec)
        outputs["ov"] = ((16, D), F32, vmem)

    rows, blocks = s.rows, s.blocks
    dma = pltpu.SemaphoreType.DMA
    scratch = {
        "w4": ((4, D, D), BF16),
        "wu": ((D, FF), BF16),
        "wd": ((FF, D), BF16),
        "vec": ((8, D), F32),
        "upb": ((1, FF), F32),
        "x": ((rows, D), BF16),
        "dy": ((rows, D), BF16),
        "teach": ((groups * conts, CONT_LEN, D), BF16),
        "y": ((rows, D), BF16),
        "n1": ((rows, D), BF16),
        "q": ((rows, D), BF16),
        "k": ((rows, D), BF16),
        "v": ((rows, D), BF16),
        "ql": ((blocks, 64, D), BF16),
        "kl": ((blocks, 64, D), BF16),
        "vl": ((blocks, 64, D), BF16),
        "fkv": ((2, groups, s.far, D), BF16),
        "poolk": ((64, CONT_LEN), BF16),
        "poolq": ((64, CONT_LEN), BF16),
        "widen": ((CONT_LEN, 96), BF16),
        "bias0": ((2 * CONT_LEN, CONT_LEN), F32),
        "bias1": ((96, 48), F32),
        "biasf": ((2 * s.tb * BLOCK, s.far), F32),
        "e0": ((blocks * PAIRS, 2 * CONT_LEN, CONT_LEN), BF16),
        "e1": ((blocks * PAIRS, 96, 48), BF16),
        "ef": ((groups, PAIRS, 2 * s.tb * BLOCK, s.far), BF16),
        "num": ((rows, D), F32),
        "att": ((rows, D), BF16),
        "den": ((rows, D), F32),
        "mix": ((rows, D), F32),
        "n2": ((rows, D), BF16),
        "h": ((rows, FF), BF16),
        "gy": ((rows, D), F32),
        "gyb": ((rows, D), BF16),
        "dnum": ((rows, D), BF16),
        "xo": ((rows, D), BF16),
        "dnl": ((2, blocks, 64, D), BF16),
        "xol": ((2, blocks, 64, D), BF16),
        "dql": ((blocks, BLOCK, D), BF16),
        "dqkv": ((PAIRS, rows, 3 * LANES), BF16),
        "df": ((groups, 2, s.far, D), F32),
        "dfs": ((groups, 2, s.far, D), BF16),
        "rf": ((nz - 1, groups, 2, s.far_own, D), BF16),
        "ft": ((groups, 2, s.far_own, D), BF16),
        "vg": ((16, D), F32),
        "gq": ((PAIRS, 4, 2, m, 3 * LANES), BF16),
        "go": ((4, 2, m, D), BF16),
        "gu": ((4, 2, m, FF), BF16),
        "gd": ((4, 2, mf, D), BF16),
        "lens": pltpu.SMEM((conts, groups), jnp.int32),
        "ls": pltpu.SMEM((1, 1), F32),
        "lsem": dma((20,)),
        "ss": dma((SENDS,)),
        "fr": dma((2,)),
    }
    if exchange:
        scratch["tiles"] = ((ndev, 8, LANES), F32)
        scratch["build"] = ((8, LANES), F32)
        scratch["small"] = ((5, 1, s.r), BF16)
        scratch["smallup"] = ((1, s.rf), BF16)
        for name in ("q", "k", "v", "o"):
            scratch["hg" + name] = ((s.r, D), F32)
        scratch["hgu"] = ((s.r, FF), F32)
        scratch["hgd"] = ((s.rf, D), F32)
        scratch["hv"] = ((8, LANES), F32)
        for name, lead, rr, cc in (("q", (PAIRS,), m, 3 * LANES), ("o", (), m, D), ("u", (), m, FF), ("d", (), mf, D)):
            scratch["rc" + name] = (lead + (4, rr, cc), BF16)
            scratch["rd" + name] = (lead + (2, rr // 2, cc), BF16)
            scratch["rx" + name] = (lead + (2, rr, cc), BF16)
            scratch["rz" + name] = (lead + (nz - 1, rr // nz, cc), BF16)
        scratch["rv"] = ((3 + nz, 16, D), F32)
        scratch["vt"] = ((3, 16, D), F32)
        scratch["agr"] = dma((5, 10))
        scratch["rsr"] = dma((3 + PAIRS, 5))
        scratch["vr"] = dma((4,))

    names = list(inputs) + list(outputs) + list(scratch)
    results = pl.pallas_call(
        functools.partial(kernel, s, names),
        out_shape=[jax.ShapeDtypeStruct(shape, dtype) for shape, dtype, _ in outputs.values()],
        in_specs=[spec for _, spec in inputs.values()],
        out_specs=[spec for _, _, spec in outputs.values()],
        scratch_shapes=[pltpu.VMEM(*v) if isinstance(v, tuple) else v for v in scratch.values()],
        compiler_params=pltpu.CompilerParams(
            collective_id=0, has_side_effects=True, vmem_limit_bytes=64 * 1024 * 1024 - 65536
        ),
        name="layer",
    )(*[a for a, _ in inputs.values()])
    o = types.SimpleNamespace(**dict(zip(outputs, results)))
    if exchange:
        bulk = ["py", "cy", "pdx", "cdx", "ogq", "ogk", "ogv", "ogo", "ogu", "ogd"]
        shapes = [jax.ShapeDtypeStruct(outputs[k][0], outputs[k][1]) for k in bulk]
        vectors = [jax.ShapeDtypeStruct((1, n), F32) for n in [s.r] * 5 + [1, s.rf]]
        done = pl.pallas_call(
            functools.partial(finish, len(bulk)),
            out_shape=shapes + vectors,
            in_specs=[vmem] + [any_spec] * len(bulk),
            out_specs=[any_spec] * len(bulk) + [vmem] * len(vectors),
            scratch_shapes=[pltpu.VMEM(v.shape, v.dtype) for v in shapes] + [dma((2, len(bulk)))],
            name="finish",
        )(o.ov, *[getattr(o, k) for k in bulk])
        for k, v in zip(bulk, done):
            setattr(o, k, v)
        *vec, loss, up_vec = [v.reshape(-1) for v in done[len(bulk) :]]
        loss = loss.reshape(())
        mats = [o.ogq, o.ogk, o.ogv, o.ogo, o.ogu, o.ogd]
    else:
        three = o.fgq.reshape(PAIRS, D, 3, LANES).transpose(2, 1, 0, 3).reshape(3, D, D)
        whole = [three[0], three[1], three[2], o.fgo, o.fgu, o.fgd]
        whole = [w.reshape(-1, w.shape[-1]).astype(F32) for w in whole]
        parts = [o.ov[i] for i in range(5)] + [o.ov[8:12].reshape(FF)]
        *mats, v0, v1, v2, v3, v4, up_vec = [
            lax.psum_scatter(w, both, scatter_dimension=0, tiled=True) for w in whole + parts
        ]
        vec = [v0, v1, v2, v3, v4]
        loss = lax.psum(jnp.sum(o.ov[5]), both) / (tokens * D)
    return (
        o.py,
        o.cy,
        loss,
        o.pdx,
        o.cdx,
        vec[0],
        vec[1],
        mats[0],
        mats[1],
        mats[2],
        mats[3],
        vec[2],
        vec[3],
        mats[4],
        up_vec,
        mats[5],
        vec[4],
    )


def solution(mesh):
    rows = P("dp", "cont", None)
    conts = P("dp", "cont", None, None)
    vector = P(("dp", "cont"))
    matrix = P(("dp", "cont"), None)
    return jax.shard_map(
        functools.partial(layer, mesh),
        mesh=mesh,
        in_specs=(rows, conts, rows, conts, conts, P("dp", "cont"), P())
        + (vector, vector, matrix, matrix, matrix, matrix, vector, vector, matrix, vector, matrix, vector),
        out_specs=(rows, conts, P(), rows, conts)
        + (vector, vector, matrix, matrix, matrix, matrix, vector, vector, matrix, vector, matrix, vector),
        check_vma=False,
    )
```

time: 138 us -> 117 us (0.85)
  local copies, waits for them, and re-layouts: 15.1 us -> 0 us
  Pallas kernels: 121 us -> 115 us
    unnamed x29 -> x0, local copies, waits for them, and re-layouts: 11.3 us -> none
    pallas_call x1, Pallas kernels: 121 us -> 111 us  [layer(): pl.pallas_call(functools.partial(kernel, s, names), out_shape=[jax.ShapeD...]
    pallas_call x0 -> x1, Pallas kernels: none -> 4.14 us  [layer(): pl.pallas_call(functools.partial(finish, len(bulk)), out_shape=shapes + v...]
    squeeze x2 -> x0, local copies, waits for them, and re-layouts: 2.57 us -> none  [the longest x1 1.39 us: layer(): vec = [o.ov[i, :s.r] for i in range(5)]]
where the time goes in v2:
time: 117 us; the launch traced here: 116 us
  Pallas kernels  115 us (98%)
  between operations  1.52 us (1%)
    pallas_call x1, Pallas kernels, layer(): pl.pallas_call(functools.partial(kernel, s, names), out_shape=[jax.ShapeD...  111 us
    pallas_call x1, Pallas kernels, layer(): pl.pallas_call(functools.partial(finish, len(bulk)), out_shape=shapes + v...  4.14 us

profile of v2, /device:TPU:0, one launch (start us, length us, event | category | flops | bytes accessed | tf_op | source)
XLA Modules:
  0.0 116.3 jit_solution(17480691799377836432)
XLA Ops:
  1.3 110.6 %layer.1 = (bf16[2,256,512]{2,1,0:T(8,128)(2,1)}, bf16[2,1,128,512]{3,2,1,0:T(8,128)(2,1)}, f32[2,256,512]{2,1,0:T(8,128)}, f32[2,1,128,512]{3,2,1,0:T(8,128)}, ...) custom-call(bf16[2,256,512]{2,1,0:T(8,128)(2,1)} %refs_0_.1, ...), custom_call_target="tpu_custom_call" | custom-call | tf_op jit(solution)/shard_map/layer/pallas_call | solution.py:985
  112.0 4.1 %finish.1 = (bf16[2,256,512]{2,1,0:T(8,128)(2,1)}, bf16[2,1,128,512]{3,2,1,0:T(8,128)(2,1)}, f32[2,256,512]{2,1,0:T(8,128)}, f32[2,1,128,512]{3,2,1,0:T(8,128)},...) custom-call(f32[8,128]{1,0:T(8,128)} %get-tuple-element.45.refs_0_, ...), custom_call_target="tpu_custom_call" | custom-call | tf_op jit(solution)/shard_map/finish/pallas_call | solution.py:1001

commit v3 on v2

--- a/solution.py
+++ b/solution.py
@@ -72,6 +72,7 @@
         self.tb = self.nb + conts
         self.rows_g = self.tb * CONT_LEN
         self.rows = groups * self.rows_g
+        self.nl = 48 * self.tb
         self.blocks = groups * self.tb
         self.far_own = prompt // COARSE
         self.far = self.far_own * nz
@@ -92,14 +93,39 @@
             src_ref=src, dst_ref=dst, send_sem=ssem, recv_sem=rsem, device_id=dev, device_id_type=MESH
         )
 
-    def send(src, dst, rsem, dev):
+    def send(src, dst, rsem, dev, cond=None):
         slot = sent[0] % SENDS
         sent[0] += 1
         if slot in pending:
-            pending[slot].wait_send()
+            left(slot)
         copy = remote(src, dst, r.ss.at[slot], rsem, dev)
-        copy.start()
-        pending[slot] = copy
+        on(cond, copy.start)
+        pending[slot] = (cond, copy)
+
+    def on(cond, act):
+        if cond is None:
+            act()
+        else:
+            pl.when(cond)(act)
+
+    def left(slot):
+        cond, copy = pending[slot]
+        on(cond, copy.wait_send)
+
+    def line_send(src, dst, rsem):
+        for d, zz in enumerate(zs):
+            cond = None
+            if s.exchange and d != 1:
+                cond = z != (s.nz - 1 if d == 0 else 0)
+            send(src, dst, rsem, (dp, zz), cond)
+
+    middle = (z == 1) | (z == 2)
+    far_end = jnp.clip(3 * (z - 1), 0, s.nz - 1)
+
+    def line_relay(piece, rsem):
+        if s.exchange:
+            ref = piece(3 - far_end)
+            send(ref, ref, rsem, (dp, far_end), middle)
 
     def wait_recv(ref, rsem):
         pltpu.make_async_copy(ref, ref, rsem).wait()
@@ -141,60 +167,62 @@
         def view(k, a, n, part=None):
             if k == 0:
                 return r.tiles.at[pl.ds(a, n)]
-            ref, rows = [(r.w4, s.r), (r.w4, s.r), (r.wu, s.r), (r.wd, s.rf)][k - 1]
+            ref, rows = (r.w4, s.r) if k < 5 else (r.wu, s.r) if k == 5 else (r.wd, s.rf)
             place = pl.ds(pl.multiple_of(a * rows, rows), n * rows)
             width = ref.shape[-1]
             cols = pl.ds(0, width) if part is None else pl.ds(part * (width // 2), width // 2)
-            if k == 1:
-                return ref.at[pl.ds(0, 3), place, cols]
-            if k == 2:
-                return ref.at[3, place, cols]
+            if k < 5:
+                return ref.at[(1, 2, 0, 3)[k - 1], place, cols]
             return ref.at[place, cols]
 
         def shard(c, co, zz):
             return (c * 2 + co) * s.nz + zz
 
-        def ag_move(k, kind, a, n, dev, part=None):
+        def ag_sem(k, kind, wave):
+            return r.agw.at[kind - 1] if wave and 0 < kind < 5 else r.agr.at[k, kind]
+
+        def ag_move(k, kind, a, n, dev, part=None, wave=0):
             v = view(k, a, n, part)
-            send(v, v, r.agr.at[k, kind], dev)
-
-        def ag_got(k, kind, n, part=None):
-            wait_recv(view(k, 0, n, part), r.agr.at[k, kind])
+            send(v, v, ag_sem(k, kind, wave), dev)
+
+        def ag_got(k, kind, n, part=None, wave=0):
+            wait_recv(view(k, 0, n, part), ag_sem(k, kind, wave))
 
         def ag_z(k):
-            for zz in zs:
-                ag_move(k, 0, me, 1, (dp, zz))
+            own = view(k, me, 1)
+            line_send(own, own, ag_sem(k, 0, 0))
 
         def ag_out(k, wave, starts, n):
             if wave == 1 or n > 1:
                 ag_got(k, 0, s.nz - 1)
+                line_relay(lambda zz: view(k, dp * s.nz + zz, 1), ag_sem(k, 0, 0))
             for zz in starts:
                 a = shard(cell, core, zz)
-                ag_move(k, 1 + wave, a, n, (xn, z))
-                ag_move(k, 3 + wave, a, n, (yn, z))
+                ag_move(k, 1, a, n, (xn, z), None, wave)
+                ag_move(k, 2, a, n, (yn, z), None, wave)
             for zz in starts:
-                ag_move(k, 9, shard(cell, core, zz), n, (sib, z))
+                ag_move(k, 5, shard(cell, core, zz), n, (sib, z))
 
         def ag_pass(k, wave, starts, n):
             total = len(starts) * n
-            ag_got(k, 1 + wave, total)
+            ag_got(k, 1, total, None, wave)
             for zz in starts:
-                ag_move(k, 5 + wave, shard(cell_x, core, zz), n, (yn, z), 0)
-            ag_got(k, 3 + wave, total)
+                ag_move(k, 3, shard(cell_x, core, zz), n, (yn, z), 0, wave)
+            ag_got(k, 2, total, None, wave)
             if k > 0:
                 for zz in starts:
-                    ag_move(k, 7 + wave, shard(cell_y, core, zz), n, (xn, z), 1)
+                    ag_move(k, 4, shard(cell_y, core, zz), n, (xn, z), 1, wave)
             for zz in starts:
-                ag_move(k, 9, shard(cell_x, core, zz), n, (sib, z))
-                ag_move(k, 9, shard(cell_y, core, zz), n, (sib, z))
+                ag_move(k, 5, shard(cell_x, core, zz), n, (sib, z))
+                ag_move(k, 5, shard(cell_y, core, zz), n, (sib, z))
 
         def ag_last(k, wave, starts, n):
             total = len(starts) * n
-            ag_got(k, 5 + wave, total, 0)
+            ag_got(k, 3, total, 0, wave)
             if k > 0:
-                ag_got(k, 7 + wave, total, 1)
+                ag_got(k, 4, total, 1, wave)
             for zz in starts:
-                ag_move(k, 9, shard(cell_d, core, zz), n, (sib, z))
+                ag_move(k, 5, shard(cell_d, core, zz), n, (sib, z))
 
         def ag1(k):
             ag_out(k, 0, [0], s.nz)
@@ -206,7 +234,7 @@
             ag_last(k, 0, [0], s.nz)
 
         def ag4(k):
-            ag_got(k, 9, 4 * s.nz)
+            ag_got(k, 5, 4 * s.nz)
 
         grads = [(r.gd.at[...], r.rcd, r.rdd, r.rxd, r.rzd), (r.gu.at[...], r.rcu, r.rdu, r.rxu, r.rzu),
                  (r.go.at[...], r.rco, r.rdo, r.rxo, r.rzo)]
@@ -219,27 +247,27 @@
 
         def add_to(g, c, lo, n, term):
             place = (c, core, pl.ds(lo, n))
-            g[place] = (g[place].astype(F32) + term).astype(BF16)
+            g[place] = (g[place].astype(F32) + term.astype(F32)).astype(BF16) if term.dtype == F32 else g[place] + term
 
         def rs1(k):
             g, rc, rd, _, _ = grads[k]
             m = g.shape[2]
             wait_recv(rc, r.rsr.at[k, 0])
-            add_to(g, cell_d, 0, m, rc[cell_d].astype(F32))
+            add_to(g, cell_d, 0, m, rc[cell_d])
             mh = m // 2
             send(g.at[cell_d, core, pl.ds(0, mh)], rd.at[0], r.rsr.at[k, 1], (yn, z))
             send(g.at[cell_d, core, pl.ds(mh, mh)], rd.at[1], r.rsr.at[k, 2], (xn, z))
             for c in (cell_x, cell_y, cell):
-                add_to(g, c, 0, m, rc[c].astype(F32))
+                add_to(g, c, 0, m, rc[c])
 
         def rs2(k):
             g, _, rd, rx, _ = grads[k]
             mh = g.shape[2] // 2
             wait_recv(rd.at[0], r.rsr.at[k, 1])
-            add_to(g, cell_x, 0, mh, rd[0].astype(F32))
+            add_to(g, cell_x, 0, mh, rd[0])
             send(g.at[cell_x, core], rx.at[0], r.rsr.at[k, 3], (xn, z))
             wait_recv(rd.at[1], r.rsr.at[k, 2])
-            add_to(g, cell_y, mh, mh, rd[1].astype(F32))
+            add_to(g, cell_y, mh, mh, rd[1])
             send(g.at[cell_y, core], rx.at[1], r.rsr.at[k, 3], (yn, z))
 
         def piece(g, zz):
@@ -285,8 +313,8 @@
         own_rows = pl.ds(pl.multiple_of(me * s.r, s.r), s.r)
         weights_in = [
             local([(w, r.w4.at[j, own_rows]) for j, w in enumerate((r.wq, r.wk, r.wv, r.wo))], r.w4.at[:, own_rows]),
-            local([(r.wup, view(3, me, 1))]),
-            local([(r.wdn, view(4, me, 1))]),
+            local([(r.wup, view(5, me, 1))]),
+            local([(r.wdn, view(6, me, 1))]),
         ]
     else:
         weights_in = [local([(w, r.w4.at[j]) for j, w in enumerate((r.wq, r.wk, r.wv, r.wo))], r.w4)]
@@ -328,9 +356,8 @@
     ag_z(0)
     ag_z(1)
     ag_out(1, 0, first, 1)
-
-    lane_lo = iota((CONT_LEN, LANES), 1) < HEAD_DIM
-    lane_lo48 = iota((48, LANES), 1) < HEAD_DIM
+    ag_z(2)
+
     ri = iota((64, CONT_LEN), 0)
     ci = iota((64, CONT_LEN), 1)
     coarse_ci = jnp.where(ri < 32, ci >> 1, jnp.where(ri < 48, ci >> 2, ci >> 3))
@@ -338,11 +365,14 @@
     r.poolk[...] = jnp.where(coarse_ci == position, 1.0, 0.0).astype(BF16)
     position = jnp.where(ri < 48, position + 16, position)
     r.poolq[...] = jnp.where(coarse_ci == position, 1.0, 0.0).astype(BF16)
-    ri = iota((CONT_LEN, 96), 0)
-    ci = lax.rem(iota((CONT_LEN, 96), 1), 48)
-    coarse_ri = jnp.where(ci < 32, ri >> 1, ri >> 2)
-    position = jnp.where(ci < 16, ci + 16, jnp.where(ci < 32, ci + 32, ci - 16))
-    r.widen[...] = jnp.where(coarse_ri == position, 1.0, 0.0).astype(BF16)
+    r.pq3[...] = jnp.zeros_like(r.pq3)
+    r.pk3[...] = jnp.zeros_like(r.pk3)
+    for b in range(s.tb):
+        cols = pl.ds(b * CONT_LEN, CONT_LEN)
+        for first_row in (0, s.nl):
+            r.pq3[pl.ds(first_row + b * 48, 48), cols] = r.poolq[pl.ds(0, 48)]
+        r.pq3[pl.ds(2 * s.nl + b * BLOCK, BLOCK), cols] = r.poolq[pl.ds(48, BLOCK)]
+        r.pk3[pl.ds(b * 48, 48), cols] = r.poolk[pl.ds(0, 48)]
     ri = iota((CONT_LEN, CONT_LEN), 0)
     ci = iota((CONT_LEN, CONT_LEN), 1)
     bi, bj = ri >> 4, ci >> 4
@@ -350,8 +380,9 @@
     near = jnp.where(near, 0.0, AWAY)
     r.bias0[pl.ds(0, CONT_LEN)] = near
     r.bias0[pl.ds(CONT_LEN, CONT_LEN)] = near
-    ri = lax.rem(iota((96, 48), 0), 48)
-    r.bias1[...] = jnp.where((ri >> 4) == (iota((96, 48), 1) >> 4), 0.0, AWAY)
+    ri = iota((2 * s.nl, s.nl), 0)
+    ri = jnp.where(ri >= s.nl, ri - s.nl, ri)
+    r.bias1[...] = jnp.where((ri >> 4) == (iota((2 * s.nl, s.nl), 1) >> 4), 0.0, AWAY)
     nq = s.tb * BLOCK
     blk = lax.rem(iota((2 * nq, s.far), 0), nq) >> 4
     limit = jnp.where(blk >= s.nb, s.far, BLOCK * (z * s.nb + blk))
@@ -363,13 +394,18 @@
     ag_pass(1, 0, first, 1)
     ag1(0)
     ag_out(1, 1, rest, 1)
-    ag_z(2)
     ag_z(3)
     ag_last(1, 0, first, 1)
+    ag1(2)
+    ag_z(4)
+    ag_z(5)
     ag2(0)
     ag_pass(1, 1, rest, 1)
-    ag1(2)
+    ag1(3)
     ag3(0)
+    ag_z(6)
+    ag_last(1, 1, rest, 1)
+    ag2(2)
     ag4(0)
     if s.exchange:
         count = 8
@@ -412,28 +448,32 @@
         return carry
 
     lax.fori_loop(0, s.blocks, norm_one, 0)
-    ag_z(4)
-    ag1(3)
-    ag_last(1, 1, rest, 1)
+    ag2(3)
     ag4(1)
 
-    def project(t, carry):
-        g, b = t // s.tb, lax.rem(t, s.tb)
-        rows = block_rows(t)
-        n1 = r.n1[rows]
-        keep = iota((CONT_LEN, D), 0) < length_of(g, b)
-        qv = nn(n1, r.w4[0]).astype(BF16)
-        kv = jnp.where(keep, nn(n1, r.w4[1]), 0.0).astype(BF16)
-        vv = jnp.where(keep, nn(n1, r.w4[2]), 0.0).astype(BF16)
-        r.q[rows] = qv
-        r.k[rows] = kv
-        r.v[rows] = vv
-        r.ql[t] = (nn(r.poolq[...], qv) * mean_scale).astype(BF16)
-        r.kl[t] = (nn(r.poolk[...], kv) * mean_scale).astype(BF16)
-        r.vl[t] = nn(r.poolk[...], vv).astype(BF16)
-        return carry
-
-    lax.fori_loop(0, s.blocks, project, 0)
+    def project(j, out, pools):
+        for g in range(s.groups):
+            rows = pl.ds(g * s.rows_g, s.rows_g)
+            value = nn(r.n1[rows], r.w4[j])
+            parts = [value[: s.prompt]]
+            for c in range(s.conts):
+                lo = s.prompt + c * CONT_LEN
+                part = value[lo : lo + CONT_LEN]
+                if j > 0:
+                    part = jnp.where(iota((CONT_LEN, D), 0) < r.lens[c, g], part, 0.0)
+                parts.append(part)
+            value = jnp.concatenate(parts, 0).astype(BF16)
+            out[rows] = value
+            pool, pooled, scale = pools
+            for b in range(s.tb):
+                pooled[g * s.tb + b] = (nn(pool[...], value[b * CONT_LEN : (b + 1) * CONT_LEN]) * scale).astype(BF16)
+
+    project(1, r.k, (r.poolk, r.kl, mean_scale))
+    ag3(2)
+    ag1(4)
+    ag1(5)
+    ag4(2)
+    project(2, r.v, (r.poolk, r.vl, 1.0))
     for g in range(s.groups):
         for b in range(s.nb):
             place = pl.ds(pl.multiple_of(z * s.far_own + b * BLOCK, BLOCK), BLOCK)
@@ -443,20 +483,26 @@
     def far_rows(zz):
         return r.fkv.at[:, :, pl.ds(pl.multiple_of(zz * s.far_own, s.far_own), s.far_own)]
 
-    for zz in zs:
-        send(far_rows(z), far_rows(z), r.fr.at[0], (dp, zz))
-    ag2(2)
-    ag2(3)
-    ag1(4)
+    line_send(far_rows(z), far_rows(z), r.fr.at[0])
+
+    def far_got():
+        wait_recv(r.fkv.at[:, :, pl.ds(0, s.far - s.far_own)], r.fr.at[0])
+
+    ag3(3)
+    ag2(4)
+    ag4(3)
+    project(0, r.q, (r.poolq, r.ql, mean_scale))
+    ag2(5)
+    ag1(6)
 
     def two(a):
-        low = lane_lo if a.shape[0] == CONT_LEN else lane_lo48
+        low = iota(a.shape, 1) < HEAD_DIM
         zero = jnp.zeros_like(a)
         return jnp.concatenate([jnp.where(low, a, zero), jnp.where(low, zero, a)], 0)
 
     def pick(a):
         n = a.shape[0] // 2
-        return jnp.where(lane_lo if n == CONT_LEN else lane_lo48, a[:n], a[n:])
+        return jnp.where(iota((n, LANES), 1) < HEAD_DIM, a[:n], a[n:])
 
     def counts(length):
         i0 = iota((CONT_LEN, LANES), 0)
@@ -476,29 +522,46 @@
     def near(t, carry):
         g, b = t // s.tb, lax.rem(t, s.tb)
         rows = block_rows(t)
-        counts0, counts1 = counts(length_of(g, b))
+        counts0, _ = counts(length_of(g, b))
         for p in range(PAIRS):
             lanes = pair_lanes(p)
             e0 = jnp.exp2(nt(two(r.q[rows, lanes]), r.k[rows, lanes]) * (SCORE * LOG2E) + r.bias0[...])
             e0 = e0.astype(BF16)
-            e1 = jnp.exp2(
-                nt(two(r.ql[t, low48, lanes]), r.kl[t, low48, lanes]) * (SCORE * LOG2E) + r.bias1[...]
-            ).astype(BF16)
             r.e0[t * PAIRS + p] = e0
-            r.e1[t * PAIRS + p] = e1
             t0 = nn(e0, jnp.concatenate([r.v[rows, lanes], counts0], 1))
-            t1 = nn(e1, jnp.concatenate([r.vl[t, low48, lanes], counts1], 1))
+            r.num[rows, lanes] = pick(t0[:, :LANES])
+            r.den[rows, lanes] = pick(t0[:, LANES:])
+        return carry
+
+    eight = jnp.full((s.far, LANES), float(COARSE), BF16)
+
+    def gathered(ref, g, lanes, part=None):
+        part = far16 if part is None else part
+        return jnp.concatenate([ref[g * s.tb + b, part, lanes] for b in range(s.tb)], 0)
+
+    def coarse_values(g, lanes):
+        widths = jnp.concatenate([counts(length_of(g, b))[1] for b in range(s.tb)], 0)
+        return jnp.concatenate([gathered(r.vl, g, lanes, low48), widths], 1)
+
+    def group_rows(g):
+        if isinstance(g, int):
+            return pl.ds(g * s.rows_g, s.rows_g)
+        return pl.ds(pl.multiple_of(g * s.rows_g, CONT_LEN), s.rows_g)
+
+    def coarse_forward(g):
+        rows = group_rows(g)
+        for p in range(PAIRS):
+            lanes = pair_lanes(p)
+            e1 = nt(two(gathered(r.ql, g, lanes, low48)), gathered(r.kl, g, lanes, low48))
+            e1 = jnp.exp2(e1 * (SCORE * LOG2E) + r.bias1[...]).astype(BF16)
+            r.e1[g, p] = e1
+            t1 = nn(e1, coarse_values(g, lanes))
             t1 = jnp.concatenate([pick(t1[:, :LANES]), pick(t1[:, LANES:])], 1)
             high = t1.astype(BF16)
-            t1 = nn(r.widen[...], jnp.concatenate([high, (t1 - high.astype(F32)).astype(BF16)], 0))
-            r.num[rows, lanes] = pick(t0[:, :LANES]) + t1[:, :LANES]
-            r.den[rows, lanes] = pick(t0[:, LANES:]) + t1[:, LANES:]
-        return carry
-
-    eight = jnp.full((s.far, LANES), float(COARSE), BF16)
-
-    def gathered(ref, g, lanes):
-        return jnp.concatenate([ref[g * s.tb + b, far16, lanes] for b in range(s.tb)], 0)
+            both = jnp.concatenate([high, (t1 - high.astype(F32)).astype(BF16)], 0)
+            t1 = tn(r.pq3[pl.ds(0, 2 * s.nl)], both)
+            r.num[rows, lanes] += t1[:, :LANES]
+            r.den[rows, lanes] += t1[:, LANES:]
 
     def repeat_rows(a):
         n = a.shape[0]
@@ -518,15 +581,21 @@
             r.att[rows, lanes] = (numerator / denominator).astype(BF16)
 
     lax.fori_loop(0, s.tb, near, 0)
-    ag3(2)
-    ag3(3)
-    ag2(4)
+    ag3(4)
+    ag3(5)
+    ag2(6)
+    if s.exchange:
+        on(middle, far_got)
+    line_relay(far_rows, r.fr.at[0])
+    coarse_forward(0)
     lax.fori_loop(s.tb, s.blocks, near, 0)
-    wait_recv(r.fkv.at[:, :, pl.ds(0, s.far - s.far_own)], r.fr.at[0])
+    for g in range(1, s.groups):
+        coarse_forward(g)
+    on(jnp.logical_not(middle) if s.exchange else None, far_got)
     for g in range(s.groups):
         far_forward(g)
-    ag4(2)
-    ag3(4)
+    ag4(4)
+    ag3(6)
 
     for copy in later_in:
         copy.wait()
@@ -536,14 +605,14 @@
         r.mix[rows] = mixed
         xhat, _ = norm_stats(mixed)
         r.n2[rows] = (xhat * vec(2) + vec(3)).astype(BF16)
-    ag4(3)
+    ag4(5)
     for g in range(s.groups):
         rows = pl.ds(g * s.rows_g, s.rows_g)
         for n in range(FF // D):
             cols = pl.ds(n * D, D)
             pre = nn(r.n2[rows], r.wu[:, cols]) + r.upb[:, cols]
             r.h[rows, cols] = jnp.maximum(pre, 0.0).astype(BF16)
-    ag4(4)
+    ag4(6)
     extra = 2.0 * r.ls[0, 0] / (token_row * float(D))
     for g in range(s.groups):
         base = g * s.rows_g
@@ -577,8 +646,7 @@
             dpre = jnp.where(r.h[rows, cols] > 0, dh, 0.0).astype(BF16)
             r.h[rows, cols] = dpre
             r.vg[pl.ds(8 + n, 1), :] += colsum(dpre.astype(F32))
-        if n == 1:
-            rs1(0)
+    rs1(0)
     for g in range(s.groups):
         rows = pl.ds(g * s.rows_g, s.rows_g)
         dn2 = nt(r.h[rows], r.wu[...])
@@ -588,7 +656,6 @@
         dmixed = r.gy[rows] + norm_back(xhat, rstd, vec(2), dn2)
         r.gy[rows] = dmixed
         r.gyb[rows] = dmixed.astype(BF16)
-    rs2(0)
     for g in range(s.groups):
         rows = pl.ds(g * s.rows_g, s.rows_g)
         dnum = nt(r.gyb[rows], r.w4[3]) / r.den[rows]
@@ -602,6 +669,7 @@
                 ref[0, t] = high
                 ref[1, t] = (pooled - high.astype(F32)).astype(BF16)
 
+    rs2(0)
     for g in range(s.groups):
         for p in range(PAIRS):
             lanes = pair_lanes(p)
@@ -631,120 +699,140 @@
         cols = pl.ds(n * D, D)
         r.gu[:, :, :, cols] = tn(r.n2[...], r.h[:, cols]).astype(BF16).reshape(4, 2, D // 8, D)
     rs0(1)
-    rs3(0)
     r.go[...] = tn(r.att[...], r.gyb[...]).astype(BF16).reshape(4, 2, D // 8, D)
     rs0(2)
+
+    def pair_back(p, g):
+        lanes = pair_lanes(p)
+        e1 = r.e1[g, p]
+        q1 = two(gathered(r.ql, g, lanes, low48))
+        k1 = gathered(r.kl, g, lanes, low48)
+        d1, x1, d1_low, x1_low = [
+            two(gathered(ref.at[i], g, lanes, low48)) for i in range(2) for ref in (r.dnl, r.xol)
+        ]
+        vn1 = coarse_values(g, lanes)
+        ds1 = nt(jnp.concatenate([d1, x1, d1_low, x1_low], 1), jnp.concatenate([vn1, vn1], 1))
+        ds1 = (ds1 * e1.astype(F32)).astype(BF16)
+        lr = lax.rem(iota((s.nl, LANES), 0), 48)
+        level_scale = jnp.where(lr < 32, 0.5, 0.25)
+        dql = (pick(nn(ds1, k1)) * level_scale).astype(BF16)
+        dql = jnp.concatenate([dql] + [r.dql[g * s.tb + b, :, lanes] for b in range(s.tb)], 0)
+        fine_q = tn(r.pq3[pl.ds(s.nl, s.nl + s.tb * BLOCK)], dql)
+        dkl = (tn(ds1, q1) * level_scale).astype(BF16)
+        dvl = tn(e1, d1).astype(BF16)
+        fine = tn(r.pk3[...], jnp.concatenate([dkl, dvl], 1))
+        for b in range(s.tb):
+            t = g * s.tb + b
+            rows = block_rows(t)
+            length = length_of(g, b)
+            counts0, _ = counts(length)
+            q2 = two(r.q[rows, lanes])
+            e0 = r.e0[t * PAIRS + p]
+            dn2 = two(r.dnum[rows, lanes])
+            x0 = jnp.concatenate([dn2, two(r.xo[rows, lanes])], 1)
+            ds0 = nt(x0, jnp.concatenate([r.v[rows, lanes], counts0], 1)) * e0.astype(F32)
+            ds0 = ds0.astype(BF16)
+            part = slice(b * CONT_LEN, (b + 1) * CONT_LEN)
+            dq = pick(nn(ds0, r.k[rows, lanes])) + fine_q[part]
+            dkv = tn(jnp.concatenate([ds0, e0], 1), jnp.concatenate([q2, dn2], 1))
+            dk = (dkv[:CONT_LEN, :LANES] + fine[part, :LANES]) * SCORE
+            dv = dkv[CONT_LEN:, LANES:] + fine[part, LANES:]
+            r.dqkv[p, rows, pl.ds(0, LANES)] = (dq * SCORE).astype(BF16)
+            if b >= s.nb:
+                keep = iota((CONT_LEN, LANES), 0) < length
+                dk = jnp.where(keep, dk, 0.0)
+                dv = jnp.where(keep, dv, 0.0)
+            elif p == 0:
+                r.num[rows, pl.ds(0, LANES)] = dk
+                r.num[rows, pl.ds(LANES, LANES)] = dv
+                continue
+            else:
+                far_k, far_v = far_terms(p, g, b)
+                dk = dk + far_k
+                dv = dv + far_v
+            r.dqkv[p, rows, pl.ds(LANES, LANES)] = dk.astype(BF16)
+            r.dqkv[p, rows, pl.ds(2 * LANES, LANES)] = dv.astype(BF16)
+
+    def far_terms(p, g, b):
+        own = pl.ds(b * BLOCK, BLOCK)
+        lanes = pair_lanes(p)
+        return repeat_rows(r.ft[g, 0, own, lanes]), repeat_rows(r.ft[g, 1, own, lanes])
+
+    def each_group(p):
+        def body(g, carry):
+            pair_back(p, g)
+            return carry
+
+        lax.fori_loop(0, s.groups, body, 0)
+
+    each_group(0)
     rs1(1)
-
-    def near_back(t, g, b, p):
-        lanes = pair_lanes(p)
-        rows = block_rows(t)
-        length = length_of(g, b)
-        counts0, counts1 = counts(length)
-        q2 = two(r.q[rows, lanes])
-        ql2 = two(r.ql[t, low48, lanes])
-        k0 = r.k[rows, lanes]
-        kl = r.kl[t, low48, lanes]
-        e0 = r.e0[t * PAIRS + p]
-        e1 = r.e1[t * PAIRS + p]
-        dn2 = two(r.dnum[rows, lanes])
-        dnl2 = two(r.dnl[0, t, low48, lanes])
-        x0 = jnp.concatenate([dn2, two(r.xo[rows, lanes])], 1)
-        x1 = [dnl2, two(r.xol[0, t, low48, lanes]), two(r.dnl[1, t, low48, lanes]), two(r.xol[1, t, low48, lanes])]
-        x1 = jnp.concatenate(x1, 1)
-        vn1 = jnp.concatenate([r.vl[t, low48, lanes], counts1], 1)
-        ds0 = nt(x0, jnp.concatenate([r.v[rows, lanes], counts0], 1)) * e0.astype(F32)
-        ds1 = nt(x1, jnp.concatenate([vn1, vn1], 1)) * e1.astype(F32)
-        ds0 = ds0.astype(BF16)
-        ds1 = ds1.astype(BF16)
-        lr = iota((48, LANES), 0)
-        level_scale = jnp.where(lr < 32, 0.5, 0.25)
-        dql = (pick(nn(ds1, kl)) * level_scale).astype(BF16)
-        dql = jnp.concatenate([dql, r.dql[t, :, lanes]], 0)
-        dq = pick(nn(ds0, k0)) + tn(r.poolq[...], dql)
-        dk0 = tn(ds0, q2)
-        dv0 = tn(e0, dn2)
-        dkl = (tn(ds1, ql2) * level_scale).astype(BF16)
-        dvl = tn(e1, dnl2).astype(BF16)
-        coarse = jnp.concatenate([dkl, dvl], 1)
-        if b < s.nb:
-            own = pl.ds(b * BLOCK, BLOCK)
-            coarse = jnp.concatenate(
-                [coarse, jnp.concatenate([r.ft[g, 0, own, lanes], r.ft[g, 1, own, lanes]], 1)], 0
-            )
-            fine = tn(r.poolk[...], coarse)
-        else:
-            fine = tn(r.poolk[low48], coarse)
-        dk = dk0 + fine[:, :LANES]
-        dv = dv0 + fine[:, LANES:]
-        if b >= s.nb:
-            keep = iota((CONT_LEN, LANES), 0) < length
-            dk = jnp.where(keep, dk, 0.0)
-            dv = jnp.where(keep, dv, 0.0)
-        r.dqkv[p, rows, pl.ds(0, LANES)] = (dq * SCORE).astype(BF16)
-        r.dqkv[p, rows, pl.ds(LANES, LANES)] = (dk * SCORE).astype(BF16)
-        r.dqkv[p, rows, pl.ds(2 * LANES, LANES)] = dv.astype(BF16)
-
-    def conts_back(g, carry):
-        for b in range(s.nb, s.tb):
-            for p in range(PAIRS):
-                near_back(g * s.tb + b, g, b, p)
-        return carry
-
-    lax.fori_loop(0, s.groups, conts_back, 0)
-    rs2(1)
     rs1(2)
+    rs3(0)
     wait_recv(r.rf, r.fr.at[1])
     own = pl.ds(pl.multiple_of(z * s.far_own, s.far_own), s.far_own)
     for g in range(s.groups):
-        for i, scale in enumerate((1.0 / COARSE, 1.0)):
+        for i, scale in enumerate((SCORE / COARSE, 1.0)):
             total = r.df[g, i, own]
             for d in range(s.nz - 1):
                 total = total + r.rf[d, g, i].astype(F32)
-            r.ft[g, i] = (total * scale).astype(BF16)
-    rs4(0)
-    rs2(2)
+            r.ft[g, i] = total.astype(BF16).astype(F32) * scale
+    for g in range(s.groups):
+        for b in range(s.nb):
+            rows = block_rows(g * s.tb + b)
+            far_k, far_v = far_terms(0, g, b)
+            r.dqkv[0, rows, pl.ds(LANES, LANES)] = (r.num[rows, pl.ds(0, LANES)] + far_k).astype(BF16)
+            r.dqkv[0, rows, pl.ds(2 * LANES, LANES)] = (r.num[rows, pl.ds(LANES, LANES)] + far_v).astype(BF16)
 
     def prompts_back(p):
-        def body(g, carry):
-            for b in range(s.nb):
-                near_back(g * s.tb + b, g, b, p)
-            return carry
-
-        lax.fori_loop(0, s.groups, body, 0)
+        if p > 0:
+            each_group(p)
         r.gq[p] = tn(r.n1[...], r.dqkv[p]).astype(BF16).reshape(4, 2, D // 8, 3 * LANES)
+
+    def dn1_part(p, g):
+        rows = pl.ds(g * s.rows_g, s.rows_g)
+        w = jnp.concatenate([r.w4[j, :, pair_lanes(p)] for j in range(3)], 1)
+        return nt(r.dqkv[p, rows], w)
+
+    def dn1_add(p):
+        for g in range(s.groups):
+            rows = pl.ds(g * s.rows_g, s.rows_g)
+            part = dn1_part(p, g)
+            r.num[rows] = part if p == 0 else r.num[rows] + part
 
     prompts_back(0)
     rs0(3)
+    rs2(1)
+    rs2(2)
+    dn1_add(0)
+    rs1(3)
+    prompts_back(1)
+    rs0(4)
+    rs4(0)
+    dn1_add(1)
+    rs1(4)
+    rs2(3)
+    prompts_back(2)
+    rs0(5)
     rs3(1)
     rs3(2)
-    prompts_back(1)
-    rs0(4)
-    rs1(3)
-    prompts_back(2)
-    rs0(5)
-    rs2(3)
-    rs1(4)
-    rs4(1)
+    dn1_add(2)
+    rs2(4)
+    rs1(5)
+    rs3(3)
     prompts_back(3)
     rs0(6)
-    rs3(3)
-    rs2(4)
-    rs1(5)
+    rs2(5)
 
     for g in range(s.groups):
         rows = pl.ds(g * s.rows_g, s.rows_g)
-        dn1 = 0.0
-        for j in range(3):
-            d = jnp.concatenate([r.dqkv[p, rows, pl.ds(j * LANES, LANES)] for p in range(PAIRS)], 1)
-            dn1 = dn1 + nt(d, r.w4[j])
+        dn1 = r.num[rows] + dn1_part(PAIRS - 1, g)
         xhat, rstd = norm_stats(r.x[rows].astype(F32))
         r.vg[pl.ds(0, 1), :] += colsum(dn1 * xhat)
         r.vg[pl.ds(1, 1), :] += colsum(dn1)
         r.gy[rows] = r.gy[rows] + norm_back(xhat, rstd, vec(0), dn1)
         if g == 0:
             rs1(6)
-            rs2(5)
             rs3(4)
 
     outs.append(local([(b, a) for a, b in row_pairs(r.pdx, r.cdx, r.gy)], r.gy))
@@ -755,21 +843,22 @@
 
         vsend(r.vg, 0, (sib, z))
         rs2(6)
-        rs3(5)
         wait_recv(r.rv.at[0], r.vr.at[0])
         r.vt[0] = r.vg[...] + r.rv[0]
         vsend(r.vt.at[0], 1, (xn, z))
-        rs4(2)
-        rs4(3)
-        rs3(6)
+        rs3(5)
+        rs4(1)
         wait_recv(r.rv.at[1], r.vr.at[1])
         r.vt[1] = r.vt[0] + r.rv[1]
         vsend(r.vt.at[1], 2, (yn, z))
-        rs4(4)
+        rs4(2)
+        rs3(6)
         wait_recv(r.rv.at[2], r.vr.at[2])
         r.vt[2] = r.vt[1] + r.rv[2]
         for zz in zs:
             send(r.vt.at[2], r.rv.at[3 + z], r.vr.at[3], (dp, zz))
+        rs4(3)
+        rs4(4)
         rs4(5)
         rs4(6)
         wait_recv(r.rv.at[pl.ds(3, s.nz - 1)], r.vr.at[3])
@@ -799,8 +888,8 @@
             outs.append(local([(src, dst)]))
     for copy in outs:
         copy.wait()
-    for copy in pending.values():
-        copy.wait_send()
+    for slot in pending:
+        left(slot)
 
 
 def finish(n_mats, *refs):
@@ -924,12 +1013,13 @@
         "fkv": ((2, groups, s.far, D), BF16),
         "poolk": ((64, CONT_LEN), BF16),
         "poolq": ((64, CONT_LEN), BF16),
-        "widen": ((CONT_LEN, 96), BF16),
+        "pq3": ((2 * s.nl + s.tb * BLOCK, s.rows_g), BF16),
+        "pk3": ((s.nl, s.rows_g), BF16),
         "bias0": ((2 * CONT_LEN, CONT_LEN), F32),
-        "bias1": ((96, 48), F32),
+        "bias1": ((2 * s.nl, s.nl), F32),
         "biasf": ((2 * s.tb * BLOCK, s.far), F32),
         "e0": ((blocks * PAIRS, 2 * CONT_LEN, CONT_LEN), BF16),
-        "e1": ((blocks * PAIRS, 96, 48), BF16),
+        "e1": ((groups, PAIRS, 2 * s.nl, s.nl), BF16),
         "ef": ((groups, PAIRS, 2 * s.tb * BLOCK, s.far), BF16),
         "num": ((rows, D), F32),
         "att": ((rows, D), BF16),
@@ -948,7 +1038,7 @@
         "df": ((groups, 2, s.far, D), F32),
         "dfs": ((groups, 2, s.far, D), BF16),
         "rf": ((nz - 1, groups, 2, s.far_own, D), BF16),
-        "ft": ((groups, 2, s.far_own, D), BF16),
+        "ft": ((groups, 2, s.far_own, D), F32),
         "vg": ((16, D), F32),
         "gq": ((PAIRS, 4, 2, m, 3 * LANES), BF16),
         "go": ((4, 2, m, D), BF16),
@@ -977,7 +1067,8 @@
             scratch["rz" + name] = (lead + (nz - 1, rr // nz, cc), BF16)
         scratch["rv"] = ((3 + nz, 16, D), F32)
         scratch["vt"] = ((3, 16, D), F32)
-        scratch["agr"] = dma((5, 10))
+        scratch["agr"] = dma((7, 6))
+        scratch["agw"] = dma((4,))
         scratch["rsr"] = dma((3 + PAIRS, 5))
         scratch["vr"] = dma((4,))
 

time: 117 us -> 114 us (0.974)
  Pallas kernels: 115 us -> 112 us
    pallas_call x1, Pallas kernels: 111 us -> 108 us  [layer(): pl.pallas_call(functools.partial(kernel, s, names), out_shape=[jax.ShapeD...]
where the time goes in v3:
time: 114 us; the launch traced here: 113 us
  Pallas kernels  112 us (98%)
  between operations  1.52 us (1%)
    pallas_call x1, Pallas kernels, layer(): pl.pallas_call(functools.partial(kernel, s, names), out_shape=[jax.ShapeD...  108 us
    pallas_call x1, Pallas kernels, layer(): pl.pallas_call(functools.partial(finish, len(bulk)), out_shape=shapes + v...  4.14 us

profile of v3, /device:TPU:0, one launch (start us, length us, event | category | flops | bytes accessed | tf_op | source)
XLA Modules:
  0.0 113.5 jit_solution(13577579531234240823)
XLA Ops:
  1.3 107.8 %layer.1 = (bf16[2,256,512]{2,1,0:T(8,128)(2,1)}, bf16[2,1,128,512]{3,2,1,0:T(8,128)(2,1)}, f32[2,256,512]{2,1,0:T(8,128)}, f32[2,1,128,512]{3,2,1,0:T(8,128)}, ...) custom-call(bf16[2,256,512]{2,1,0:T(8,128)(2,1)} %refs_0_.1, ...), custom_call_target="tpu_custom_call" | custom-call | tf_op jit(solution)/shard_map/layer/pallas_call | solution.py:1076
  109.1 4.1 %finish.1 = (bf16[2,256,512]{2,1,0:T(8,128)(2,1)}, bf16[2,1,128,512]{3,2,1,0:T(8,128)(2,1)}, f32[2,256,512]{2,1,0:T(8,128)}, f32[2,1,128,512]{3,2,1,0:T(8,128)},...) custom-call(f32[8,128]{1,0:T(8,128)} %get-tuple-element.45.refs_0_, ...), custom_call_target="tpu_custom_call" | custom-call | tf_op jit(solution)/shard_map/finish/pallas_call | solution.py:1092

commit v4 on v3

--- a/solution.py
+++ b/solution.py
@@ -25,6 +25,7 @@
 MESH = pl.DeviceIdType.MESH
 LANES = 128
 SENDS = 24
+EARLY = 2
 
 
 def nn(a, b):
@@ -490,10 +491,9 @@
 
     ag3(3)
     ag2(4)
+    ag1(6)
     ag4(3)
     project(0, r.q, (r.poolq, r.ql, mean_scale))
-    ag2(5)
-    ag1(6)
 
     def two(a):
         low = iota(a.shape, 1) < HEAD_DIM
@@ -581,8 +581,8 @@
             r.att[rows, lanes] = (numerator / denominator).astype(BF16)
 
     lax.fori_loop(0, s.tb, near, 0)
+    ag2(5)
     ag3(4)
-    ag3(5)
     ag2(6)
     if s.exchange:
         on(middle, far_got)
@@ -591,6 +591,7 @@
     lax.fori_loop(s.tb, s.blocks, near, 0)
     for g in range(1, s.groups):
         coarse_forward(g)
+    ag3(5)
     on(jnp.logical_not(middle) if s.exchange else None, far_got)
     for g in range(s.groups):
         far_forward(g)
@@ -669,7 +670,6 @@
                 ref[0, t] = high
                 ref[1, t] = (pooled - high.astype(F32)).astype(BF16)
 
-    rs2(0)
     for g in range(s.groups):
         for p in range(PAIRS):
             lanes = pair_lanes(p)
@@ -695,6 +695,7 @@
 
     for d, zz in enumerate(zs):
         send(far_part(zz), r.rf.at[d], r.fr.at[1], (dp, zz))
+    rs2(0)
     for n in range(FF // D):
         cols = pl.ds(n * D, D)
         r.gu[:, :, :, cols] = tn(r.n2[...], r.h[:, cols]).astype(BF16).reshape(4, 2, D // 8, D)
@@ -742,9 +743,9 @@
                 keep = iota((CONT_LEN, LANES), 0) < length
                 dk = jnp.where(keep, dk, 0.0)
                 dv = jnp.where(keep, dv, 0.0)
-            elif p == 0:
-                r.num[rows, pl.ds(0, LANES)] = dk
-                r.num[rows, pl.ds(LANES, LANES)] = dv
+            elif p < EARLY:
+                r.num[rows, pl.ds(2 * p * LANES, LANES)] = dk
+                r.num[rows, pl.ds((2 * p + 1) * LANES, LANES)] = dv
                 continue
             else:
                 far_k, far_v = far_terms(p, g, b)
@@ -765,9 +766,10 @@
 
         lax.fori_loop(0, s.groups, body, 0)
 
+    rs1(1)
     each_group(0)
-    rs1(1)
     rs1(2)
+    each_group(1)
     rs3(0)
     wait_recv(r.rf, r.fr.at[1])
     own = pl.ds(pl.multiple_of(z * s.far_own, s.far_own), s.far_own)
@@ -777,15 +779,20 @@
             for d in range(s.nz - 1):
                 total = total + r.rf[d, g, i].astype(F32)
             r.ft[g, i] = total.astype(BF16).astype(F32) * scale
-    for g in range(s.groups):
-        for b in range(s.nb):
-            rows = block_rows(g * s.tb + b)
-            far_k, far_v = far_terms(0, g, b)
-            r.dqkv[0, rows, pl.ds(LANES, LANES)] = (r.num[rows, pl.ds(0, LANES)] + far_k).astype(BF16)
-            r.dqkv[0, rows, pl.ds(2 * LANES, LANES)] = (r.num[rows, pl.ds(LANES, LANES)] + far_v).astype(BF16)
+    def add_far(p):
+        for g in range(s.groups):
+            for b in range(s.nb):
+                rows = block_rows(g * s.tb + b)
+                far_k, far_v = far_terms(p, g, b)
+                dk = r.num[rows, pl.ds(2 * p * LANES, LANES)] + far_k
+                dv = r.num[rows, pl.ds((2 * p + 1) * LANES, LANES)] + far_v
+                r.dqkv[p, rows, pl.ds(LANES, LANES)] = dk.astype(BF16)
+                r.dqkv[p, rows, pl.ds(2 * LANES, LANES)] = dv.astype(BF16)
 
     def prompts_back(p):
-        if p > 0:
+        if p < EARLY:
+            add_far(p)
+        else:
             each_group(p)
         r.gq[p] = tn(r.n1[...], r.dqkv[p]).astype(BF16).reshape(4, 2, D // 8, 3 * LANES)
 
@@ -803,26 +810,24 @@
     prompts_back(0)
     rs0(3)
     rs2(1)
-    rs2(2)
-    dn1_add(0)
-    rs1(3)
     prompts_back(1)
     rs0(4)
-    rs4(0)
+    rs2(2)
+    rs1(3)
+    dn1_add(0)
     dn1_add(1)
     rs1(4)
-    rs2(3)
     prompts_back(2)
     rs0(5)
-    rs3(1)
-    rs3(2)
+    rs4(0)
     dn1_add(2)
-    rs2(4)
     rs1(5)
-    rs3(3)
     prompts_back(3)
     rs0(6)
-    rs2(5)
+    rs3(1)
+    rs2(3)
+    rs3(2)
+    rs2(4)
 
     for g in range(s.groups):
         rows = pl.ds(g * s.rows_g, s.rows_g)
@@ -833,7 +838,8 @@
         r.gy[rows] = r.gy[rows] + norm_back(xhat, rstd, vec(0), dn1)
         if g == 0:
             rs1(6)
-            rs3(4)
+            rs2(5)
+            rs3(3)
 
     outs.append(local([(b, a) for a, b in row_pairs(r.pdx, r.cdx, r.gy)], r.gy))
     if s.exchange:
@@ -842,21 +848,22 @@
             send(src, r.rv.at[i], r.vr.at[i], dev)
 
         vsend(r.vg, 0, (sib, z))
+        rs3(4)
         rs2(6)
         wait_recv(r.rv.at[0], r.vr.at[0])
         r.vt[0] = r.vg[...] + r.rv[0]
         vsend(r.vt.at[0], 1, (xn, z))
         rs3(5)
-        rs4(1)
         wait_recv(r.rv.at[1], r.vr.at[1])
         r.vt[1] = r.vt[0] + r.rv[1]
         vsend(r.vt.at[1], 2, (yn, z))
-        rs4(2)
         rs3(6)
+        rs4(1)
         wait_recv(r.rv.at[2], r.vr.at[2])
         r.vt[2] = r.vt[1] + r.rv[2]
         for zz in zs:
             send(r.vt.at[2], r.rv.at[3 + z], r.vr.at[3], (dp, zz))
+        rs4(2)
         rs4(3)
         rs4(4)
         rs4(5)

time: 114 us -> 105 us (0.921)
  Pallas kernels: 112 us -> 103 us
    pallas_call x1, Pallas kernels: 108 us -> 99 us  [layer(): pl.pallas_call(functools.partial(kernel, s, names), out_shape=[jax.ShapeD...]
where the time goes in v4:
time: 105 us
  Pallas kernels  103 us (98%)
  between operations  1.52 us (1%)
    pallas_call x1, Pallas kernels, layer(): pl.pallas_call(functools.partial(kernel, s, names), out_shape=[jax.ShapeD...  99 us
    pallas_call x1, Pallas kernels, layer(): pl.pallas_call(functools.partial(finish, len(bulk)), out_shape=shapes + v...  4.14 us

profile of v4, /device:TPU:0, one launch (start us, length us, event | category | flops | bytes accessed | tf_op | source)
XLA Modules:
  0.0 104.7 jit_solution(3961426055498019184)
XLA Ops:
  1.3 99.0 %layer.1 = (bf16[2,256,512]{2,1,0:T(8,128)(2,1)}, bf16[2,1,128,512]{3,2,1,0:T(8,128)(2,1)}, f32[2,256,512]{2,1,0:T(8,128)}, f32[2,1,128,512]{3,2,1,0:T(8,128)}, ...) custom-call(bf16[2,256,512]{2,1,0:T(8,128)(2,1)} %refs_0_.1, ...), custom_call_target="tpu_custom_call" | custom-call | tf_op jit(solution)/shard_map/layer/pallas_call | solution.py:1083
  100.3 4.1 %finish.1 = (bf16[2,256,512]{2,1,0:T(8,128)(2,1)}, bf16[2,1,128,512]{3,2,1,0:T(8,128)(2,1)}, f32[2,256,512]{2,1,0:T(8,128)}, f32[2,1,128,512]{3,2,1,0:T(8,128)},...) custom-call(f32[8,128]{1,0:T(8,128)} %get-tuple-element.45.refs_0_, ...), custom_call_target="tpu_custom_call" | custom-call | tf_op jit(solution)/shard_map/finish/pallas_call | solution.py:1099

commit v5 on v4

--- a/solution.py
+++ b/solution.py
@@ -899,19 +899,23 @@
         left(slot)
 
 
-def finish(n_mats, *refs):
+def finish(n_mats, n_vecs, *refs):
     ov = refs[0]
     srcs = refs[1 : 1 + n_mats]
-    dsts = refs[1 + n_mats : 1 + 2 * n_mats]
-    vectors = refs[1 + 2 * n_mats : -1 - n_mats]
-    held = refs[-1 - n_mats : -1]
-    sems = refs[-1]
+    dsts = refs[1 + n_mats : 1 + 2 * n_mats + n_vecs]
+    held = refs[1 + 2 * n_mats + n_vecs : -2]
+    hov, sems = refs[-2:]
+    first = pltpu.make_async_copy(ov, hov, sems.at[0, n_mats])
+    first.start()
     reads = [pltpu.make_async_copy(a, b, sems.at[0, i]) for i, (a, b) in enumerate(zip(srcs, held))]
     writes = [pltpu.make_async_copy(a, b, sems.at[1, i]) for i, (a, b) in enumerate(zip(held, dsts))]
     for copy in reads:
         copy.start()
-    for i, out in enumerate(vectors):
-        out[...] = ov[pl.ds(i, 1), pl.ds(0, out.shape[1])]
+    first.wait()
+    for i in range(n_vecs):
+        out = held[n_mats + i]
+        out[...] = hov[pl.ds(i, 1), pl.ds(0, out.shape[1])]
+        writes[n_mats + i].start()
     for read, write in zip(reads, writes):
         read.wait()
         write.start()
@@ -1097,11 +1101,12 @@
         shapes = [jax.ShapeDtypeStruct(outputs[k][0], outputs[k][1]) for k in bulk]
         vectors = [jax.ShapeDtypeStruct((1, n), F32) for n in [s.r] * 5 + [1, s.rf]]
         done = pl.pallas_call(
-            functools.partial(finish, len(bulk)),
+            functools.partial(finish, len(bulk), len(vectors)),
             out_shape=shapes + vectors,
-            in_specs=[vmem] + [any_spec] * len(bulk),
-            out_specs=[any_spec] * len(bulk) + [vmem] * len(vectors),
-            scratch_shapes=[pltpu.VMEM(v.shape, v.dtype) for v in shapes] + [dma((2, len(bulk)))],
+            in_specs=[any_spec] * (1 + len(bulk)),
+            out_specs=[any_spec] * (len(bulk) + len(vectors)),
+            scratch_shapes=[pltpu.VMEM(v.shape, v.dtype) for v in shapes + vectors]
+            + [pltpu.VMEM((8, LANES), F32), dma((2, len(bulk) + len(vectors)))],
             name="finish",
         )(o.ov, *[getattr(o, k) for k in bulk])
         for k, v in zip(bulk, done):

time: 105 us -> 104 us (level)
    pallas_call x1, Pallas kernels: 4.14 us -> 3.06 us  [layer(): pl.pallas_call(functools.partial(finish, len(bulk), len(vectors)), out_sh...]
where the time goes in v5:
time: 104 us
  Pallas kernels  102 us (98%)
  between operations  1.52 us (1%)
    pallas_call x1, Pallas kernels, layer(): pl.pallas_call(functools.partial(kernel, s, names), out_shape=[jax.ShapeD...  99 us
    pallas_call x1, Pallas kernels, layer(): pl.pallas_call(functools.partial(finish, len(bulk), len(vectors)), out_sh...  3.06 us

profile of v5, /device:TPU:0, one launch (start us, length us, event | category | flops | bytes accessed | tf_op | source)
XLA Modules:
  0.0 103.6 jit_solution(5937833629154173818)
XLA Ops:
  1.3 99.0 %layer.1 = (bf16[2,256,512]{2,1,0:T(8,128)(2,1)}, bf16[2,1,128,512]{3,2,1,0:T(8,128)(2,1)}, f32[2,256,512]{2,1,0:T(8,128)}, f32[2,1,128,512]{3,2,1,0:T(8,128)}, ...) custom-call(bf16[2,256,512]{2,1,0:T(8,128)(2,1)} %refs_0_.1, ...), custom_call_target="tpu_custom_call" | custom-call | tf_op jit(solution)/shard_map/layer/pallas_call | solution.py:1087
  100.3 3.1 %finish.1 = (bf16[2,256,512]{2,1,0:T(8,128)(2,1)}, bf16[2,1,128,512]{3,2,1,0:T(8,128)(2,1)}, f32[2,256,512]{2,1,0:T(8,128)}, f32[2,1,128,512]{3,2,1,0:T(8,128)},...) custom-call(f32[8,128]{1,0:T(8,128)} %get-tuple-element.45.refs_0_, ...), custom_call_target="tpu_custom_call" | custom-call | tf_op jit(solution)/shard_map/finish/pallas_call | solution.py:1103
